TPU v7x, 32 devices: a whole 2x2x4 slice. The times are simulated.
32 devices in a mesh: rows: 8 (over y, x, core), rep: 4 (over z).
Axes of the slice: x: 2, y: 2, z: 4, core: 2. Of those that a mesh axis runs over, the one named last changes fastest.
Arguments:
- features: bfloat16 [4096, 256], P(('rows', 'rep')), may hold values from -6 to 6
- weight: bfloat16 [256, 256], replicated, may hold values from -0.375 to 0.375
- tiles: bfloat16 [8, 4, 4, 8, 128, 128], P('rows', 'rep'), as said below
- send_src: int32 [8, 4, 8, 24], P('rows', 'rep'), may hold values from 0 to 4095, as said below
- send_dst: int32 [8, 4, 8, 24], P('rows', 'rep'), may hold values from 0 to 128, as said below
- cotangent: bfloat16 [4096, 256], P(('rows', 'rep')), may hold values from -6 to 6
Outputs:
- output: bfloat16 [4096, 256], P(('rows', 'rep'))
- grad_w: float32 [256, 256], replicated
- grad_x: bfloat16 [4096, 256], P(('rows', 'rep'))
Inputs may be any that keep to these rules, and one draw needn't show every extreme that they name: Device (g, c)'s tiles are nonnegative; a tile row is nonzero only if some live slot of that device names it. `send_src`: A flattened tile row (b * 8 + k) * 128 + i of the sending device. Each tile row is named by at most one live slot, and all live slots naming rows of one tile belong to one peer p. An empty slot holds 0. `send_dst`: 128 marks an empty slot. For each rep index c there is a peer p to which every device (g, c) sends all 24 slots live, and some device has an empty slot. Destination rows may repeat.
All inputs are finite; a program needn't handle non-finite values.
Results may differ from a plain program's by a relative error of at most 0.02.
Values may be sent and summed in bfloat16 or wider, within the bound.
No kernel may reach another device: no remote copies, remote signals or barrier semaphores. Data moves between devices by JAX's collectives and lax.ppermute only.
A program may use at most 64 MiB of HBM per device.

v0:
```python
import math

import jax
import jax.numpy as jnp
from jax import lax
from jax.sharding import PartitionSpec as P


def local(features, weight, tiles, send_src, send_dst, cotangent):
    blocks = tiles[0, 0]
    source = send_src[0, 0]
    target = send_dst[0, 0]
    rows_dev = features.shape[0]
    feature_width = features.shape[1]
    col_blocks = blocks.shape[0]
    per_col = blocks.shape[1]
    block_size = blocks.shape[2]
    tile_rows = col_blocks * per_col * block_size
    whole_group = lax.all_gather(features, "rep", axis=0, tiled=True)
    partial_value = jnp.einsum(
        "bkij,bjf->bkif",
        blocks,
        whole_group.reshape(col_blocks, block_size, feature_width),
        preferred_element_type=jnp.float32,
    )
    flattened = partial_value.reshape(tile_rows, feature_width)
    outgoing = flattened[source]
    incoming, landing = (
        lax.all_to_all(outgoing, "rows", split_axis=0, concat_axis=0, tiled=True),
        lax.all_to_all(target, "rows", split_axis=0, concat_axis=0, tiled=True),
    )
    summed = (
        features.astype(jnp.float32)
        .at[landing.reshape(-1)]
        .add(incoming.reshape(-1, feature_width), mode="drop")
    )
    aggregated = summed.astype(jnp.bfloat16)
    preact = jnp.dot(aggregated, weight, preferred_element_type=jnp.float32)
    sigmoid = jax.nn.sigmoid(preact)
    output = (preact * sigmoid).astype(jnp.bfloat16)
    pre_grad = (cotangent.astype(jnp.float32) * sigmoid * (1.0 + preact * (1.0 - sigmoid))).astype(
        jnp.bfloat16
    )
    local_w = jnp.einsum("nf,ng->fg", aggregated, pre_grad, preferred_element_type=jnp.float32)
    node_count = rows_dev * lax.axis_size("rows") * lax.axis_size("rep")
    grad_w = lax.psum(local_w, ("rows", "rep")) * (1.0 / math.sqrt(node_count))
    back_in = jnp.einsum("ng,fg->nf", pre_grad, weight, preferred_element_type=jnp.float32).astype(
        jnp.bfloat16
    )
    requested = back_in[jnp.minimum(landing, rows_dev - 1)]
    returned = lax.all_to_all(requested, "rows", split_axis=0, concat_axis=0, tiled=True)
    placed = jnp.where(target < rows_dev, source, tile_rows)
    spread = (
        jnp.zeros((tile_rows, feature_width), jnp.bfloat16)
        .at[placed.reshape(-1)]
        .set(returned.reshape(-1, feature_width), mode="drop")
    )
    spread = spread.reshape(col_blocks, per_col, block_size, feature_width)
    group_rows = col_blocks * block_size
    group_terms = jnp.einsum(
        "bkij,bkif->bjf", blocks, spread, preferred_element_type=jnp.float32
    ).reshape(group_rows, feature_width)
    group_total = lax.psum(group_terms.astype(jnp.bfloat16), "rep").astype(jnp.float32)
    transposed = lax.dynamic_slice_in_dim(
        group_total, lax.axis_index("rep") * rows_dev, rows_dev, 0
    )
    grad_x = (back_in.astype(jnp.float32) + transposed).astype(jnp.bfloat16)
    return (output, grad_w, grad_x)


def solution(mesh):
    placed = (
        P(("rows", "rep"), None),
        P(),
        P("rows", "rep", None, None, None, None),
        P("rows", "rep", None, None),
        P("rows", "rep", None, None),
        P(("rows", "rep"), None),
    )
    return jax.shard_map(
        local,
        mesh=mesh,
        in_specs=placed,
        out_specs=(P(("rows", "rep"), None), P(), P(("rows", "rep"), None)),
        check_vma=False,
    )
```

profile of v0, /device:TPU:0, one launch (start us, length us, event | category | flops | bytes accessed | tf_op | source)
XLA Modules:
  0.0 232.0 jit_solution(4209044904271957521)
XLA Ops:
  7.2 5.3 %all-to-all-start = ((s32[8,1,24]{2,1,0:T(1,128)}), s32[8,1,24]{2,1,0:T(1,128)S(1)}, u32[]{:S(2)}, u32[]{:S(2)}) async-start(s32[8,1,24]{2,1,0:T(1,128)} %bitcast.46), calls=%async_computation | async-start | bytes 8192 | tf_op jit(solution)/shard_map/all_to_all | solution.py:30
  12.5 0.7 compare_select_fusion.1
  13.2 0.7 compare_select_fusion.4
  13.9 14.5 %all_gather.3 = bf16[512,256]{1,0:T(8,128)(2,1)S(1)} all-gather(bf16[128,256]{1,0:T(8,128)(2,1)} %param.6), channel_id=1, replica_groups=mesh['rows'=8,'rep'=4] {'rep'}, dimensions={0}, use_global_device_ids=true | all-gather | bytes 327680 | tf_op jit(solution)/shard_map/all_gather | solution.py:19
  28.5 2.6 %fusion.2 = f32[4,8,128,256]{3,2,1,0:T(8,128)} fusion(bf16[4,128,256,1]{2,1,3,0:T(8,128)(2,1)S(1)} %bitcast.43, bf16[1,1,4,8,128,128]{5,4,3,2,1,0:T(8,128)(2,1)S(1)} %copy-done), kind=kOutput, calls=%fused_computation.8 | convolution fusion | flops 268435456 | bytes 5505024 | tf_op jit(solution)/shard_map/bkij,bjf->bkif/dot_general | solution.py:20
  31.2 3.7 %gather_fusion = f32[192,256]{1,0:T(8,128)} fusion(f32[4096,256]{1,0:T(8,128)} %bitcast.41, s32[1024]{0:T(1024)S(1)} %pad_clamp_fusion.1), kind=kCustom, calls=%fused_computation | custom fusion | bytes 393984 | tf_op jit(solution)/shard_map/gather | solution.py:27
  34.9 4.1 %all-to-all-start.1 = ((f32[8,24,256]{2,1,0:T(8,128)}), f32[8,24,256]{2,1,0:T(8,128)S(1)}, u32[]{:S(2)}, u32[]{:S(2)}) async-start(f32[8,24,256]{2,1,0:T(8,128)} %bitcast.8), calls=%async_computation.1 | async-start | bytes 393216 | tf_op jit(solution)/shard_map/all_to_all | solution.py:29
  39.0 0.5 broadcast.121
  39.5 0.7 broadcast_minimum_fusion
  40.3 0.1 reshape.159
  40.4 4.9 %all-to-all-done.1 = f32[8,24,256]{2,1,0:T(8,128)S(1)} async-done(((f32[8,24,256]{2,1,0:T(8,128)}), f32[8,24,256]{2,1,0:T(8,128)S(1)}, u32[]{:S(2)}, u32[]{:S(2)}) %all-to-all-start.1) | async-done | bytes 196640 | tf_op jit(solution)/shard_map/all_to_all | solution.py:29
  45.3 1.7 scatter_fusion
  47.0 0.8 multiply_convert_fusion.1
  47.8 0.2 convolution_convert_fusion
  48.0 1.7 gather_fusion.1
  49.6 3.4 %all-to-all-start.2 = ((bf16[8,24,256]{2,1,0:T(8,128)(2,1)}), bf16[8,24,256]{2,1,0:T(8,128)(2,1)S(1)}, u32[]{:S(2)}, u32[]{:S(2)}) async-start(bf16[8,24,256]{2,1,0:T(8,128)(2,1)} %bitcast.12), calls=%async_computation.2 | async-start | bytes 196608 | tf_op jit(solution)/shard_map/all_to_all | solution.py:51
  53.1 0.9 fusion.6
  54.1 4.1 %all-to-all-done.2 = bf16[8,24,256]{2,1,0:T(8,128)(2,1)S(1)} async-done(((bf16[8,24,256]{2,1,0:T(8,128)(2,1)}), bf16[8,24,256]{2,1,0:T(8,128)(2,1)S(1)}, u32[]{:S(2)}, u32[]{:S(2)}) %all-to-all-start.2) | async-done | bytes 98336 | tf_op jit(solution)/shard_map/all_to_all | solution.py:51
  58.1 2.1 scatter_custom_fusion.1
  60.2 1.3 fusion
  61.5 125.4 %all-reduce.3.cloned.1.call-done = f32[256,256]{1,0:T(8,128)} async-done(((f32[256,256]{1,0:T(8,128)}), f32[256,256]{1,0:T(8,128)}) %all-reduce.3.cloned.1.call-update) | async-done | bytes 262160 | tf_op jit(solution)/shard_map/psum | solution.py:46
  186.9 1.7 broadcast_multiply_fusion
  188.6 35.0 %all-reduce.5.cloned.1.call-done = bf16[512,256]{1,0:T(8,128)(2,1)} async-done(((bf16[512,256]{1,0:T(8,128)(2,1)}), bf16[512,256]{1,0:T(8,128)(2,1)}) %all-reduce.5.cloned.1.call-update) | async-done | bytes 262160 | tf_op jit(solution)/shard_map/psum | solution.py:63
  223.6 1.5 add_convert_fusion
  (22 shorter events, 0.4 us)
Async XLA Ops:
  7.2 21.4 %copy-start = (bf16[1,1,4,8,128,128]{5,4,3,2,1,0:T(8,128)(2,1)S(1)}, bf16[1,1,4,8,128,128]{5,4,3,2,1,0:T(8,128)(2,1)}, u32[]{:S(2)}) copy-start(bf16[1,1,4,8,128,128]{5,4,3,2,1,0:T(8,128)(2,1)} %param.8) | copy-start | bytes 3145732
  7.2 27.8 %all-to-all-start = ((s32[8,1,24]{2,1,0:T(1,128)}), s32[8,1,24]{2,1,0:T(1,128)S(1)}, u32[]{:S(2)}, u32[]{:S(2)}) async-start(s32[8,1,24]{2,1,0:T(1,128)} %bitcast.46), calls=%async_computation | async-start | bytes 8192 | tf_op jit(solution)/shard_map/all_to_all | solution.py:30
  28.5 2.7 %copy-start.1 = (bf16[128,256]{1,0:T(8,128)(2,1)S(1)}, bf16[128,256]{1,0:T(8,128)(2,1)}, u32[]{:S(2)}) copy-start(bf16[128,256]{1,0:T(8,128)(2,1)} %param.6) | copy-start | bytes 196612
  34.9 12.0 %copy-start.2 = (bf16[256,256]{1,0:T(8,128)(2,1)S(1)}, bf16[256,256]{1,0:T(8,128)(2,1)}, u32[]{:S(2)}) copy-start(bf16[256,256]{1,0:T(8,128)(2,1)} %param.7) | copy-start | bytes 393220
  34.9 10.3 %all-to-all-start.1 = ((f32[8,24,256]{2,1,0:T(8,128)}), f32[8,24,256]{2,1,0:T(8,128)S(1)}, u32[]{:S(2)}, u32[]{:S(2)}) async-start(f32[8,24,256]{2,1,0:T(8,128)} %bitcast.8), calls=%async_computation.1 | async-start | bytes 393216 | tf_op jit(solution)/shard_map/all_to_all | solution.py:29
  39.0 8.8 %copy-start.3 = (bf16[128,256]{1,0:T(8,128)(2,1)S(1)}, bf16[128,256]{1,0:T(8,128)(2,1)}, u32[]{:S(2)}) copy-start(bf16[128,256]{1,0:T(8,128)(2,1)} %param.11) | copy-start | bytes 196612
  49.6 8.5 %all-to-all-start.2 = ((bf16[8,24,256]{2,1,0:T(8,128)(2,1)}), bf16[8,24,256]{2,1,0:T(8,128)(2,1)S(1)}, u32[]{:S(2)}, u32[]{:S(2)}) async-start(bf16[8,24,256]{2,1,0:T(8,128)(2,1)} %bitcast.12), calls=%async_computation.2 | async-start | bytes 196608 | tf_op jit(solution)/shard_map/all_to_all | solution.py:51
  53.0 133.9 %all-reduce.3.cloned.1.call-start = ((), (), s32[]{:S(2)}) async-start(), calls=%async_computation.3 | async-start | bytes 524288 | tf_op jit(solution)/shard_map/psum | solution.py:46
  54.0 169.6 %all-reduce.5.cloned.1.call-start = ((), (), s32[]{:S(2)}) async-start(), calls=%async_computation.4 | async-start | bytes 524288 | tf_op jit(solution)/shard_map/psum | solution.py:63
Sparse Core Ops, SparseCore 0:
  59.9 126.9 all-reduce.2
  189.3 34.3 all-reduce.4
where the time goes:
time: 233 us; the launch traced here: 232 us
  waiting for transfers between devices  169 us (73%)
  blocking collectives  14.5 us (6%)
  between operations  14.1 us (6%)
  starting transfers between devices  12.8 us (5%)
  local copies, waits for them, and re-layouts  8.3 us (4%)
  other arithmetic  6.93 us (3%)
  matrix products  5.84 us (3%)
    psum x1, waiting for transfers between devices, local(): grad_w = lax.psum(local_w, ('rows', 'rep')) * (1.0 / math.sqrt(node_count))  125 us
    psum x1, waiting for transfers between devices, local(): lax.psum(group_terms.astype(jnp.bfloat16), 'rep').astype(jnp.float32)  35 us
    all_gather x1, blocking collectives, local(): whole_group = lax.all_gather(features, 'rep', axis=0, tiled=True)  14.5 us
    all_to_all x1, starting transfers between devices, local(): lax.all_to_all(target, 'rows', split_axis=0, concat_axis=0, tiled=True)  5.31 us
    all_to_all x1, waiting for transfers between devices, local(): lax.all_to_all(outgoing, 'rows', split_axis=0, concat_axis=0, tiled=True)  4.86 us
  transfers between devices with their start and end apart: 5, of which 4 were waited for; matrix products, arithmetic and copies ran while one was open for 7% of the time, Pallas kernels for 0%

commit v1 on v0

v1 whole, which is shorter than its diff:
```python
import math

import jax
import jax.numpy as jnp
from jax import lax
from jax.experimental import pallas as pl
from jax.experimental.pallas import tpu as pltpu
from jax.sharding import PartitionSpec as P

BF16 = jnp.bfloat16
F32 = jnp.float32
PAD = 32
LANES = 128


def whole(count):
    return [pl.BlockSpec(memory_space=pltpu.VMEM)] * count


def params(slots):
    return pltpu.CompilerParams(vmem_limit_bytes=(4 << 20) + (16 << 10) * slots)


def dot(a, b, contract_a, contract_b):
    return lax.dot_general(
        a, b, (((contract_a,), (contract_b,)), ((), ())), preferred_element_type=F32
    )


def pick_kernel(source_ref, tiles_ref, picked_ref):
    slots = source_ref.shape[1]
    per_col, block = tiles_ref.shape[1], tiles_ref.shape[2]
    first = pl.program_id(0) * (per_col * block)
    named = jnp.transpose(jnp.broadcast_to(source_ref[...], (LANES, slots))) - first
    lane = lax.broadcasted_iota(jnp.int32, (slots, LANES), 1)
    hot = jnp.concatenate(
        [jnp.where(named == lane + k * LANES, 1.0, 0.0).astype(BF16) for k in range(per_col)],
        axis=1,
    )
    rows = tiles_ref[0].reshape(per_col * block, block)
    picked_ref[0] = dot(hot, rows, 1, 0).astype(BF16)


def partial_kernel(reps, picked_ref, landing_ref, *refs):
    out_ref = refs[-1]
    rep = lax.axis_index("rep")
    total = dot(picked_ref[rep], refs[0][...], 1, 0)
    for step in range(1, reps):
        total += dot(picked_ref[lax.rem(rep + reps - step, reps)], refs[step][...], 1, 0)
    out_ref[...] = total.reshape(out_ref.shape).astype(BF16) + landing_ref[...]


def layer_kernel(
    slot_count, chunk, incoming_ref, features_ref, weight_ref, cotangent_ref, output_ref, back_ref, send_ref
):
    peers, _, width = incoming_ref.shape
    rows = features_ref.shape[0]
    wide = width // PAD
    incoming = incoming_ref[...].reshape(peers * PAD, width)
    groups = pl.cdiv(peers, wide)
    notes = jnp.sum(incoming_ref[:, 16:PAD, :].astype(F32), axis=0)
    row = lax.broadcasted_iota(jnp.int32, (rows, width), 0)
    lane = lax.broadcasted_iota(jnp.int32, (rows, width), 1)
    valid = lax.rem(lane, PAD) < slot_count
    hots = []
    for e in range(groups):
        at = slot_count - 16 + e
        landing = notes[at : at + 1, :].astype(jnp.int32)
        hots.append(jnp.where(valid & (landing == row), 1.0, 0.0).astype(BF16))
    hot = hots[0] if groups == 1 else jnp.concatenate(hots, axis=1)
    hot = hot[:, : peers * PAD]
    weight = weight_ref[...]
    aggregated = (features_ref[...].astype(F32) + dot(hot, incoming, 1, 0)).astype(BF16)
    preact = dot(aggregated, weight, 1, 0)
    sigmoid = jax.nn.sigmoid(preact)
    output_ref[...] = (preact * sigmoid).astype(BF16)
    pre_grad = (
        cotangent_ref[...].astype(F32) * sigmoid * (1.0 + preact * (1.0 - sigmoid))
    ).astype(BF16)
    back_in = dot(pre_grad, weight, 1, 1).astype(BF16)
    back_ref[...] = back_in
    requested = dot(hot, back_in, 0, 0).reshape(peers, PAD, width)
    local_w = dot(aggregated, pre_grad, 0, 0)
    if peers * chunk > width:
        local_w = jnp.concatenate(
            [local_w, jnp.zeros((peers * chunk - width, width), F32)], axis=0
        )
    send_ref[...] = jnp.concatenate(
        [requested, local_w.reshape(peers, chunk, width)], axis=1
    ).astype(BF16)


def terms_kernel(reps, picked_ref, returned_ref, back_ref, kept_ref, *send_refs):
    peers, depth, width = returned_ref.shape
    rep = lax.axis_index("rep")
    rows = returned_ref[:, :PAD, :].reshape(peers * PAD, width)
    part = jnp.sum(returned_ref[:, PAD:, :].astype(F32), axis=0)
    own = dot(picked_ref[rep], rows, 0, 0) + back_ref[...].astype(F32)
    kept_ref[...] = jnp.concatenate([own, part], axis=0)
    for step in range(1, reps):
        term = dot(picked_ref[lax.rem(rep + step, reps)], rows, 0, 0)
        send_refs[step - 1][...] = jnp.concatenate([term, part], axis=0).astype(BF16)


def finish_kernel(reps, peers, kept_ref, *refs):
    got, (grad_x_ref, chunk_ref, parts_ref) = refs[: reps - 1], refs[reps - 1 :]
    rows = grad_x_ref.shape[0]
    rep = lax.axis_index("rep")
    total = kept_ref[:rows, :]
    parts_ref[rep] = kept_ref[rows:, :].astype(BF16).astype(F32)
    for step in range(1, reps):
        arrived = got[step - 1][...].astype(F32)
        total += arrived[:rows]
        parts_ref[lax.rem(rep + reps - step, reps)] = arrived[rows:]
    grad_x_ref[...] = total.astype(BF16)
    chunk = parts_ref[0]
    for other in range(1, reps):
        chunk += parts_ref[other]
    chunk_ref[...] = jnp.broadcast_to(chunk.astype(BF16)[None], chunk_ref.shape)


def local(features, weight, tiles, send_src, send_dst, cotangent):
    blocks = tiles[0, 0]
    source = send_src[0, 0]
    target = send_dst[0, 0]
    peers, slot_count = target.shape
    rows, width = features.shape
    cols, per_col, block = blocks.shape[:3]
    reps = lax.axis_size("rep")
    slots = peers * PAD
    chunk = max(16, width // peers)
    wide = width // PAD
    mine = lax.axis_index("rows")

    def shifted(value, step):
        return lax.ppermute(value, "rep", [(i, (i + step) % reps) for i in range(reps)])

    gathered = [features] + [shifted(features, step) for step in range(1, reps)]

    named = jnp.where(target < rows, source, -1)
    named = jnp.pad(named, ((0, 0), (0, PAD - slot_count)), constant_values=-1).reshape(1, slots)
    picked = pl.pallas_call(
        pick_kernel,
        grid=(cols,),
        out_shape=jax.ShapeDtypeStruct((cols, slots, block), BF16),
        in_specs=[
            pl.BlockSpec((1, slots), lambda b: (0, 0)),
            pl.BlockSpec((1, per_col, block, block), lambda b: (b, 0, 0, 0)),
        ],
        out_specs=pl.BlockSpec((1, slots, block), lambda b: (b, 0, 0)),
        compiler_params=params(slots),
        name="pick",
    )(named, blocks)

    lane = jnp.arange(width)
    tiled = jnp.tile(jnp.pad(target, ((0, 0), (0, PAD - slot_count))), (1, wide))
    tiled = jnp.where(lane // PAD == mine % wide, tiled, 0)
    note_row = jnp.arange(PAD) == slot_count + mine // wide
    landing = jnp.where(note_row[None, :, None], tiled[:, None, :], 0).astype(BF16)

    outgoing = pl.pallas_call(
        lambda *refs: partial_kernel(reps, *refs),
        out_shape=jax.ShapeDtypeStruct((peers, PAD, width), BF16),
        in_specs=whole(2 + reps),
        out_specs=whole(1)[0],
        compiler_params=params(slots),
        name="partial",
    )(picked, landing, *gathered)

    incoming = lax.all_to_all(outgoing, "rows", split_axis=0, concat_axis=0, tiled=True)

    output, back_in, requested = pl.pallas_call(
        lambda *refs: layer_kernel(slot_count, chunk, *refs),
        out_shape=(
            jax.ShapeDtypeStruct((rows, width), BF16),
            jax.ShapeDtypeStruct((rows, width), BF16),
            jax.ShapeDtypeStruct((peers, PAD + chunk, width), BF16),
        ),
        in_specs=whole(4),
        out_specs=tuple(whole(3)),
        compiler_params=params(slots),
        name="layer",
    )(incoming, features, weight, cotangent)

    returned = lax.all_to_all(requested, "rows", split_axis=0, concat_axis=0, tiled=True)

    kept, *sends = pl.pallas_call(
        lambda *refs: terms_kernel(reps, *refs),
        out_shape=(jax.ShapeDtypeStruct((rows + chunk, width), F32),)
        + (jax.ShapeDtypeStruct((rows + chunk, width), BF16),) * (reps - 1),
        in_specs=whole(3),
        out_specs=tuple(whole(reps)),
        compiler_params=params(slots),
        name="terms",
    )(picked, returned, back_in)

    arrived = [shifted(sends[step - 1], step) for step in range(1, reps)]

    grad_x, share = pl.pallas_call(
        lambda *refs: finish_kernel(reps, peers, *refs),
        out_shape=(
            jax.ShapeDtypeStruct((rows, width), BF16),
            jax.ShapeDtypeStruct((peers, chunk, width), BF16),
        ),
        in_specs=whole(reps),
        out_specs=tuple(whole(2)),
        scratch_shapes=[pltpu.VMEM((reps, chunk, width), F32)],
        compiler_params=params(slots),
        name="finish",
    )(kept, *arrived)

    shares = lax.all_to_all(share, "rows", split_axis=0, concat_axis=0, tiled=True)
    node_count = rows * lax.axis_size("rows") * reps
    grad_w = shares.reshape(peers * chunk, width)[:width].astype(F32) * (
        1.0 / math.sqrt(node_count)
    )
    return (output, grad_w, grad_x)


def solution(mesh):
    placed = (
        P(("rows", "rep"), None),
        P(),
        P("rows", "rep", None, None, None, None),
        P("rows", "rep", None, None),
        P("rows", "rep", None, None),
        P(("rows", "rep"), None),
    )
    return jax.shard_map(
        local,
        mesh=mesh,
        in_specs=placed,
        out_specs=(P(("rows", "rep"), None), P(), P(("rows", "rep"), None)),
        check_vma=False,
    )
```

time: 233 us -> 51.2 us (0.22)
  waiting for transfers between devices: 169 us -> 5.66 us
  between operations: 14.1 us -> 0.7 us
  blocking collectives: 14.5 us -> 26.4 us
  other arithmetic: 6.93 us -> 0.83 us
  matrix products: 5.84 us -> 0 us
  local copies, waits for them, and re-layouts: 8.3 us -> 2.69 us
  Pallas kernels: 0 us -> 3.74 us
    psum x2 -> x0, waiting for transfers between devices: 160 us -> none  [the longest x1 125 us: local(): grad_w = lax.psum(local_w, ('rows', 'rep')) * (1.0 / math.sqrt(node_count))]
    all_to_all x0 -> x3, blocking collectives: none -> 26.4 us  [the longest x1 9.33 us: local(): lax.all_to_all(requested, 'rows', split_axis=0, concat_axis=0, tiled=True)]
    all_gather x1 -> x0, blocking collectives: 14.5 us -> none  [local(): whole_group = lax.all_gather(features, 'rep', axis=0, tiled=True)]
    all_to_all x3 -> x0, starting transfers between devices: 12.8 us -> none  [the longest x1 5.31 us: local(): lax.all_to_all(target, 'rows', split_axis=0, concat_axis=0, tiled=True)]
    ppermute x0 -> x6, starting transfers between devices: none -> 10.9 us  [shifted(): lax.ppermute(value, 'rep', [(i, (i + step) % reps) for i in range(reps)])]
    all_to_all x3 -> x0, waiting for transfers between devices: 8.93 us -> none  [the longest x1 4.86 us: local(): lax.all_to_all(outgoing, 'rows', split_axis=0, concat_axis=0, tiled=True)]
    dot_general x5 -> x0, matrix products: 5.84 us -> none  [the longest x1 2.63 us: local(): jnp.einsum('bkij,bjf->bkif', blocks, whole_group.reshape(col_blocks, bloc...]
    ppermute x0 -> x6, waiting for transfers between devices: none -> 5.66 us  [shifted(): lax.ppermute(value, 'rep', [(i, (i + step) % reps) for i in range(reps)])]
  transfers between devices with their start and end apart: 5 -> 6, of which waited for: 4 -> 3; matrix products, arithmetic and copies ran while one was open for 7% -> 1% of each run, Pallas kernels for 0% -> 3%
where the time goes in v1:
time: 51.2 us; the launch traced here: 50.9 us
  blocking collectives  26.4 us (52%)
  starting transfers between devices  10.9 us (21%)
  waiting for transfers between devices  5.66 us (11%)
  Pallas kernels  3.74 us (7%)
  local copies, waits for them, and re-layouts  2.69 us (5%)
  other arithmetic  0.83 us (2%)
  between operations  0.7 us (1%)
    ppermute x6, starting transfers between devices, shifted(): lax.ppermute(value, 'rep', [(i, (i + step) % reps) for i in range(reps)])  10.9 us
    all_to_all x1, blocking collectives, local(): lax.all_to_all(requested, 'rows', split_axis=0, concat_axis=0, tiled=True)  9.33 us
    all_to_all x1, blocking collectives, local(): lax.all_to_all(outgoing, 'rows', split_axis=0, concat_axis=0, tiled=True)  9.18 us
    all_to_all x1, blocking collectives, local(): lax.all_to_all(share, 'rows', split_axis=0, concat_axis=0, tiled=True)  7.91 us
    ppermute x6, waiting for transfers between devices, shifted(): lax.ppermute(value, 'rep', [(i, (i + step) % reps) for i in range(reps)])  5.66 us
    unnamed x12, local copies, waits for them, and re-layouts  2.51 us
    pallas_call x1, Pallas kernels, local(): pl.pallas_call(pick_kernel, grid=(cols,), out_shape=jax.ShapeDtypeStruct(...  1.55 us
  transfers between devices with their start and end apart: 6, of which 3 were waited for; matrix products, arithmetic and copies ran while one was open for 1% of the time, Pallas kernels for 3%

profile of v1, /device:TPU:0, one launch (start us, length us, event | category | flops | bytes accessed | tf_op | source)
XLA Modules:
  0.0 50.9 jit_solution(12755362225697360390)
XLA Ops:
  0.6 5.1 %collective-permute-start.2 = (bf16[128,256]{1,0:T(8,128)(2,1)}, bf16[128,256]{1,0:T(8,128)(2,1)S(1)}, u32[]{:S(2)}, u32[]{:S(2)}) collective-permute-start(bf16[128,256]{1,0:T(8,128)(2,1)} %refs_1_.1), channel_id=1, source_target_pairs={{0,3},{1,0},{2,1},{3,2},{4,7},{5,4},{6,5},{7,6},{8,11},{9,8},{10,9... | collective-permute-start | bytes 196616 | tf_op jit(solution)/shard_map/ppermute | solution.py:136
  5.7 1.0 %collective-permute-start = (bf16[128,256]{1,0:T(8,128)(2,1)}, bf16[128,256]{1,0:T(8,128)(2,1)S(1)}, u32[]{:S(2)}, u32[]{:S(2)}) collective-permute-start(bf16[128,256]{1,0:T(8,128)(2,1)} %refs_1_.1), channel_id=1, source_target_pairs={{0,1},{1,2},{2,3},{3,0},{4,5},{5,6},{6,7},{7,4},{8,9},{9,10},{10,1... | collective-permute-start | bytes 196616 | tf_op jit(solution)/shard_map/ppermute | solution.py:136
  6.8 0.7 %copy-done.4 = s32[1,1,8,24]{3,2,1,0:T(8,128)S(1)} copy-done((s32[1,1,8,24]{3,2,1,0:T(8,128)S(1)}, s32[1,1,8,24]{3,2,1,0:T(8,128)}, u32[]{:S(2)}) %copy-start.4) | copy-done | bytes 792
  7.4 0.1 tile.10
  7.5 0.1 select_convert_fusion.refs_1_
  7.6 0.6 %copy-done.5 = s32[1,1,8,24]{3,2,1,0:T(8,128)S(1)} copy-done((s32[1,1,8,24]{3,2,1,0:T(8,128)S(1)}, s32[1,1,8,24]{3,2,1,0:T(8,128)}, u32[]{:S(2)}) %copy-start.5) | copy-done | bytes 792
  8.2 0.1 reshape.37.source_ref
  8.3 1.2 %copy-done = bf16[1,1,4,8,128,128]{5,4,3,2,1,0:T(8,128)(2,1)S(1)} copy-done((bf16[1,1,4,8,128,128]{5,4,3,2,1,0:T(8,128)(2,1)S(1)}, bf16[1,1,4,8,128,128]{5,4,3,2,1,0:T(8,128)(2,1)}, u32[]{:S(2)}) %copy-start) | copy-done | bytes 1048600
  9.5 1.6 %pick.1.refs_0_ = bf16[4,256,128]{2,1,0:T(8,128)(2,1)S(1)} custom-call(s32[1,256]{1,0:T(1,128)S(1)} %reshape.37.source_ref, bf16[4,8,128,128]{3,2,1,0:T(8,128)(2,1)S(1)} %bitcast.6), custom_call_target="tpu_custom_call" | custom-call | tf_op jit(solution)/shard_map/pick/pallas_call | solution.py:142
  11.1 1.3 %collective-permute-done.1.refs_4_ = bf16[128,256]{1,0:T(8,128)(2,1)S(1)} collective-permute-done((bf16[128,256]{1,0:T(8,128)(2,1)}, bf16[128,256]{1,0:T(8,128)(2,1)S(1)}, u32[]{:S(2)}, u32[]{:S(2)}) %collective-permute-start.1) | collective-permute-done | bytes 65568 | tf_op jit(solution)/shard_map/ppermute | solution.py:136
  12.4 0.3 partial.1
  12.7 0.0 copy-start.2
  12.7 9.2 %all_to_all.15.refs_0_ = bf16[8,32,256]{2,1,0:T(8,128)(2,1)S(1)} all-to-all(bf16[8,32,256]{2,1,0:T(8,128)(2,1)S(1)} %partial.1), channel_id=1, replica_groups=mesh['rows'=8,'rep'=4] {'rows'}, dimensions={0} | all-to-all | bytes 262144 | tf_op jit(solution)/shard_map/all_to_all | solution.py:170
  21.9 0.9 %layer.1 = (bf16[128,256]{1,0:T(8,128)(2,1)}, bf16[128,256]{1,0:T(8,128)(2,1)S(1)}, bf16[8,64,256]{2,1,0:T(8,128)(2,1)S(1)}) custom-call(bf16[8,32,256]{2,1,0:T(8,128)(2,1)S(1)} %all_to_all.15.refs_0_, bf16[128,256]{1,0:T(8,128)(2,1)S(1)} %copy-done.1, bf16[256,256]{1,0:T(8,128)(2,1)S(1)} %copy-done.2, bf16[128,256]{1,0:T(8,128)(2,1)S(1)} %copy-done.3), custom_call_target="tpu_custom_call" | custom-call | tf_op jit(solution)/shard_map/layer/pallas_call | solution.py:172
  22.9 9.3 %all_to_all.16.refs_1_ = bf16[8,64,256]{2,1,0:T(8,128)(2,1)S(1)} all-to-all(bf16[8,64,256]{2,1,0:T(8,128)(2,1)S(1)} %get-tuple-element.13), channel_id=1, replica_groups=mesh['rows'=8,'rep'=4] {'rows'}, dimensions={0} | all-to-all | bytes 524288 | tf_op jit(solution)/shard_map/all_to_all | solution.py:185
  32.2 0.3 terms.1
  32.5 1.3 %collective-permute-start.3 = (bf16[160,256]{1,0:T(8,128)(2,1)S(1)}, bf16[160,256]{1,0:T(8,128)(2,1)S(1)}, u32[]{:S(2)}, u32[]{:S(2)}) collective-permute-start(bf16[160,256]{1,0:T(8,128)(2,1)S(1)} %get-tuple-element.16), channel_id=1, source_target_pairs={{0,1},{1,2},{2,3},{3,0},{4,5},{5,6},{6,7},{7,4},{8,9},{9,10},{10,1... | collective-permute-start | bytes 245768 | tf_op jit(solution)/shard_map/ppermute | solution.py:136
  33.8 1.3 %collective-permute-start.4 = (bf16[160,256]{1,0:T(8,128)(2,1)S(1)}, bf16[160,256]{1,0:T(8,128)(2,1)S(1)}, u32[]{:S(2)}, u32[]{:S(2)}) collective-permute-start(bf16[160,256]{1,0:T(8,128)(2,1)S(1)} %get-tuple-element.17), channel_id=1, source_target_pairs={{0,2},{1,3},{2,0},{3,1},{4,6},{5,7},{6,4},{7,5},{8,10},{9,11},{10,... | collective-permute-start | bytes 245768 | tf_op jit(solution)/shard_map/ppermute | solution.py:136
  35.0 2.2 %collective-permute-start.5 = (bf16[160,256]{1,0:T(8,128)(2,1)S(1)}, bf16[160,256]{1,0:T(8,128)(2,1)S(1)}, u32[]{:S(2)}, u32[]{:S(2)}) collective-permute-start(bf16[160,256]{1,0:T(8,128)(2,1)S(1)} %get-tuple-element.18), channel_id=1, source_target_pairs={{0,3},{1,0},{2,1},{3,2},{4,7},{5,4},{6,5},{7,6},{8,11},{9,8},{10,9... | collective-permute-start | bytes 245768 | tf_op jit(solution)/shard_map/ppermute | solution.py:136
  37.2 2.5 %collective-permute-done.3.refs_1_ = bf16[160,256]{1,0:T(8,128)(2,1)S(1)} collective-permute-done((bf16[160,256]{1,0:T(8,128)(2,1)S(1)}, bf16[160,256]{1,0:T(8,128)(2,1)S(1)}, u32[]{:S(2)}, u32[]{:S(2)}) %collective-permute-start.3) | collective-permute-done | bytes 81952 | tf_op jit(solution)/shard_map/ppermute | solution.py:136
  39.8 1.8 %collective-permute-done.4.refs_2_ = bf16[160,256]{1,0:T(8,128)(2,1)S(1)} collective-permute-done((bf16[160,256]{1,0:T(8,128)(2,1)S(1)}, bf16[160,256]{1,0:T(8,128)(2,1)S(1)}, u32[]{:S(2)}, u32[]{:S(2)}) %collective-permute-start.4) | collective-permute-done | bytes 81952 | tf_op jit(solution)/shard_map/ppermute | solution.py:136
  41.6 0.7 %finish.1 = (bf16[128,256]{1,0:T(8,128)(2,1)}, bf16[8,32,256]{2,1,0:T(8,128)(2,1)S(1)}) custom-call(f32[160,256]{1,0:T(8,128)S(1)} %get-tuple-element.15.refs_0_, bf16[160,256]{1,0:T(8,128)(2,1)S(1)} %collective-permute-done.3.refs_1_, bf16[160,256]{1,0:T(8,128)(2,1)S(1)} %collective-permute-done.4.refs_2_, bf16[160,256]{1,0:T(8,128)(2,1)S(1)} %collective-permute-done.5.refs_3_), custom_call_target="tpu_custom_call" | custom-call | tf_op jit(solution)/shard_map/finish/pallas_call | solution.py:199
  42.3 7.9 %all_to_all.17 = bf16[8,32,256]{2,1,0:T(8,128)(2,1)S(1)} all-to-all(bf16[8,32,256]{2,1,0:T(8,128)(2,1)S(1)} %get-tuple-element.19), channel_id=1, replica_groups=mesh['rows'=8,'rep'=4] {'rows'}, dimensions={0} | all-to-all | bytes 262144 | tf_op jit(solution)/shard_map/all_to_all | solution.py:212
  50.2 0.7 %convert_multiply_fusion = f32[8,32,256]{2,1,0:T(8,128)} fusion(bf16[8,32,256]{2,1,0:T(8,128)(2,1)S(1)} %all_to_all.17), kind=kLoop, calls=%fused_computation | loop fusion | flops 131072 | bytes 393216 | tf_op jit(solution)/shard_map/mul | solution.py:214
  (19 shorter events, 0.1 us)
Async XLA Ops:
  0.6 10.5 %collective-permute-start.2 = (bf16[128,256]{1,0:T(8,128)(2,1)}, bf16[128,256]{1,0:T(8,128)(2,1)S(1)}, u32[]{:S(2)}, u32[]{:S(2)}) collective-permute-start(bf16[128,256]{1,0:T(8,128)(2,1)} %refs_1_.1), channel_id=1, source_target_pairs={{0,3},{1,0},{2,1},{3,2},{4,7},{5,4},{6,5},{7,6},{8,11},{9,8},{10,9... | collective-permute-start | bytes 196616 | tf_op jit(solution)/shard_map/ppermute | solution.py:136
  5.7 6.7 %collective-permute-start.1 = (bf16[128,256]{1,0:T(8,128)(2,1)}, bf16[128,256]{1,0:T(8,128)(2,1)S(1)}, u32[]{:S(2)}, u32[]{:S(2)}) collective-permute-start(bf16[128,256]{1,0:T(8,128)(2,1)} %refs_1_.1), channel_id=1, source_target_pairs={{0,2},{1,3},{2,0},{3,1},{4,6},{5,7},{6,4},{7,5},{8,10},{9,11},{10,... | collective-permute-start | bytes 196616 | tf_op jit(solution)/shard_map/ppermute | solution.py:136
  5.7 6.7 %collective-permute-start = (bf16[128,256]{1,0:T(8,128)(2,1)}, bf16[128,256]{1,0:T(8,128)(2,1)S(1)}, u32[]{:S(2)}, u32[]{:S(2)}) collective-permute-start(bf16[128,256]{1,0:T(8,128)(2,1)} %refs_1_.1), channel_id=1, source_target_pairs={{0,1},{1,2},{2,3},{3,0},{4,5},{5,6},{6,7},{7,4},{8,9},{9,10},{10,1... | collective-permute-start | bytes 196616 | tf_op jit(solution)/shard_map/ppermute | solution.py:136
  6.7 0.7 %copy-start.4 = (s32[1,1,8,24]{3,2,1,0:T(8,128)S(1)}, s32[1,1,8,24]{3,2,1,0:T(8,128)}, u32[]{:S(2)}) copy-start(s32[1,1,8,24]{3,2,1,0:T(8,128)} %param.10) | copy-start | bytes 2308
  7.5 0.7 %copy-start.5 = (s32[1,1,8,24]{3,2,1,0:T(8,128)S(1)}, s32[1,1,8,24]{3,2,1,0:T(8,128)}, u32[]{:S(2)}) copy-start(s32[1,1,8,24]{3,2,1,0:T(8,128)} %param.9) | copy-start | bytes 2308
  8.3 1.2 %copy-start = (bf16[1,1,4,8,128,128]{5,4,3,2,1,0:T(8,128)(2,1)S(1)}, bf16[1,1,4,8,128,128]{5,4,3,2,1,0:T(8,128)(2,1)}, u32[]{:S(2)}) copy-start(bf16[1,1,4,8,128,128]{5,4,3,2,1,0:T(8,128)(2,1)} %param.8) | copy-start | bytes 3145732
  9.5 2.9 %copy-start.1 = (bf16[128,256]{1,0:T(8,128)(2,1)S(1)}, bf16[128,256]{1,0:T(8,128)(2,1)}, u32[]{:S(2)}) copy-start(bf16[128,256]{1,0:T(8,128)(2,1)} %refs_1_.1) | copy-start | bytes 196612
  12.7 9.2 %copy-start.2 = (bf16[256,256]{1,0:T(8,128)(2,1)S(1)}, bf16[256,256]{1,0:T(8,128)(2,1)}, u32[]{:S(2)}) copy-start(bf16[256,256]{1,0:T(8,128)(2,1)} %refs_2_.3) | copy-start | bytes 393220
  12.7 9.2 %copy-start.3 = (bf16[128,256]{1,0:T(8,128)(2,1)S(1)}, bf16[128,256]{1,0:T(8,128)(2,1)}, u32[]{:S(2)}) copy-start(bf16[128,256]{1,0:T(8,128)(2,1)} %refs_3_.1) | copy-start | bytes 196612
  32.5 7.3 %collective-permute-start.3 = (bf16[160,256]{1,0:T(8,128)(2,1)S(1)}, bf16[160,256]{1,0:T(8,128)(2,1)S(1)}, u32[]{:S(2)}, u32[]{:S(2)}) collective-permute-start(bf16[160,256]{1,0:T(8,128)(2,1)S(1)} %get-tuple-element.16), channel_id=1, source_target_pairs={{0,1},{1,2},{2,3},{3,0},{4,5},{5,6},{6,7},{7,4},{8,9},{9,10},{10,1... | collective-permute-start | bytes 245768 | tf_op jit(solution)/shard_map/ppermute | solution.py:136
  33.8 7.8 %collective-permute-start.4 = (bf16[160,256]{1,0:T(8,128)(2,1)S(1)}, bf16[160,256]{1,0:T(8,128)(2,1)S(1)}, u32[]{:S(2)}, u32[]{:S(2)}) collective-permute-start(bf16[160,256]{1,0:T(8,128)(2,1)S(1)} %get-tuple-element.17), channel_id=1, source_target_pairs={{0,2},{1,3},{2,0},{3,1},{4,6},{5,7},{6,4},{7,5},{8,10},{9,11},{10,... | collective-permute-start | bytes 245768 | tf_op jit(solution)/shard_map/ppermute | solution.py:136
  35.0 6.6 %collective-permute-start.5 = (bf16[160,256]{1,0:T(8,128)(2,1)S(1)}, bf16[160,256]{1,0:T(8,128)(2,1)S(1)}, u32[]{:S(2)}, u32[]{:S(2)}) collective-permute-start(bf16[160,256]{1,0:T(8,128)(2,1)S(1)} %get-tuple-element.18), channel_id=1, source_target_pairs={{0,3},{1,0},{2,1},{3,2},{4,7},{5,4},{6,5},{7,6},{8,11},{9,8},{10,9... | collective-permute-start | bytes 245768 | tf_op jit(solution)/shard_map/ppermute | solution.py:136

commit v2 on v1

v2 whole, which is shorter than its diff:
```python
import math

import jax
import jax.numpy as jnp
from jax import lax
from jax.experimental import pallas as pl
from jax.experimental.pallas import tpu as pltpu
from jax.sharding import PartitionSpec as P

BF16 = jnp.bfloat16
F32 = jnp.float32
PAD = 32
LANES = 128
PAIR = 2


def whole(count):
    return [pl.BlockSpec(memory_space=pltpu.VMEM)] * count


def params(slots):
    return pltpu.CompilerParams(vmem_limit_bytes=(4 << 20) + (16 << 10) * slots)


def dot(a, b, contract_a, contract_b):
    return lax.dot_general(
        a, b, (((contract_a,), (contract_b,)), ((), ())), preferred_element_type=F32
    )


def target_of(index, step, count):
    if count & (count - 1) == 0:
        return index ^ step
    return lax.rem(index + step, count) if isinstance(index, jax.Array) else (index + step) % count


def origin_of(index, step, count):
    if count & (count - 1) == 0:
        return index ^ step
    return lax.rem(index + count - step, count)


def step_to(index, other, count):
    if count & (count - 1) == 0:
        return index ^ other
    return lax.rem(other + count - index, count)


def place(step, mate, chips, wide):
    at = mate * chips + step
    return at // wide, at % wide


def pick_kernel(source_ref, tiles_ref, picked_ref):
    slots = source_ref.shape[1]
    per_col, block = tiles_ref.shape[1], tiles_ref.shape[2]
    first = pl.program_id(0) * (per_col * block)
    named = jnp.transpose(jnp.broadcast_to(source_ref[...], (LANES, slots))) - first
    lane = lax.broadcasted_iota(jnp.int32, (slots, LANES), 1)
    hot = jnp.concatenate(
        [jnp.where(named == lane + k * LANES, 1.0, 0.0).astype(BF16) for k in range(per_col)],
        axis=1,
    )
    rows = tiles_ref[0].reshape(per_col * block, block)
    picked_ref[0] = dot(hot, rows, 1, 0).astype(BF16)


def partial_kernel(reps, chips, picked_ref, landing_ref, *refs):
    features, sends, total_ref = refs[:reps], refs[reps:-1], refs[-1]
    rep = lax.axis_index("rep")
    chip = lax.div(lax.axis_index("rows"), PAIR)
    depth = PAIR * PAD
    total = landing_ref[...].astype(F32)
    for step in range(reps):
        total += dot(picked_ref[origin_of(rep, step, reps)], features[step][...], 1, 0)
    total_ref[...] = total
    for step in range(chips):
        first = pl.multiple_of(target_of(chip, step, chips) * depth, depth)
        sends[step][...] = total_ref[pl.ds(first, depth), :].astype(BF16)


def layer_kernel(chips, slot_count, chunk, *refs):
    got, refs = refs[: PAIR * chips], refs[PAIR * chips :]
    features_ref, mate_features_ref, cotangent_ref, mate_cotangent_ref, weight_ref = refs[:5]
    output_ref, back_ref, *sends, grad_ref = refs[5:]
    rows, width = features_ref.shape
    wide = width // PAD
    core = lax.rem(lax.axis_index("rows"), PAIR)
    chip = lax.div(lax.axis_index("rows"), PAIR)
    groups = pl.cdiv(PAIR * chips, wide)
    row = lax.broadcasted_iota(jnp.int32, (rows, width), 0)
    lane = lax.broadcasted_iota(jnp.int32, (rows, width), 1)
    valid = lax.rem(lane, PAD) < slot_count
    weight = weight_ref[...]
    hots, aggregates = [], []
    for half, own in ((core, features_ref), (1 - core, mate_features_ref)):
        first = pl.multiple_of(half * PAD, PAD)
        blocks = [ref[pl.ds(first, PAD), :] for ref in got]
        notes = [jnp.zeros((1, width), F32)] * groups
        for at, block in enumerate(blocks):
            mate = at // chips
            notes[at // wide] += block[16:].astype(F32)[slot_count - 16 + mate :][:1]
        parts = [
            jnp.where(valid & (note.astype(jnp.int32) == row), 1.0, 0.0).astype(BF16)
            for note in notes
        ]
        hot = parts[0] if groups == 1 else jnp.concatenate(parts, axis=1)
        hot = hot[:, : PAIR * chips * PAD]
        arrived = dot(hot, jnp.concatenate(blocks, axis=0), 1, 0)
        hots.append(hot[:, : chips * PAD])
        aggregates.append((own[...].astype(F32) + arrived).astype(BF16))
    aggregated = jnp.concatenate(aggregates, axis=0)
    preact = dot(aggregated, weight, 1, 0)
    sigmoid = jax.nn.sigmoid(preact)
    output_ref[...] = (preact * sigmoid)[:rows].astype(BF16)
    cotangent = jnp.concatenate([cotangent_ref[...], mate_cotangent_ref[...]], axis=0)
    pre_grad = (cotangent.astype(F32) * sigmoid * (1.0 + preact * (1.0 - sigmoid))).astype(BF16)
    back_in = dot(pre_grad, weight, 1, 1).astype(BF16)
    back_ref[...] = back_in[:rows]
    grad_ref[:width] = dot(aggregated, pre_grad, 0, 0)
    if grad_ref.shape[0] > width:
        grad_ref[width:] = jnp.zeros((grad_ref.shape[0] - width, width), F32)
    asked = [dot(hot, back_in[h * rows : (h + 1) * rows], 0, 0) for h, hot in enumerate(hots)]
    for step in range(chips):
        from_own, from_mate = (part[step * PAD : (step + 1) * PAD].astype(BF16) for part in asked)
        first = target_of(chip, step, chips) * PAIR + core
        first = pl.multiple_of(first * chunk, chunk)
        sends[step][pl.ds(pl.multiple_of(core * PAD, PAD), PAD), :] = from_own
        sends[step][pl.ds(pl.multiple_of((1 - core) * PAD, PAD), PAD), :] = from_mate
        sends[step][PAIR * PAD :, :] = grad_ref[pl.ds(first, chunk), :].astype(BF16)


def terms_kernel(reps, chips, picked_ref, back_ref, *refs):
    returned, kept_ref, sends, rows_ref = refs[:chips], refs[chips], refs[chips + 1 : -1], refs[-1]
    rep = lax.axis_index("rep")
    chip = lax.div(lax.axis_index("rows"), PAIR)
    depth = PAIR * PAD
    part = returned[0][depth:, :].astype(F32)
    for step in range(1, chips):
        part += returned[step][depth:, :].astype(F32)
    for step in range(chips):
        first = pl.multiple_of(origin_of(chip, step, chips) * depth, depth)
        rows_ref[pl.ds(first, depth), :] = returned[step][:depth, :]
    rows = rows_ref[...]
    own = dot(picked_ref[rep], rows, 0, 0) + back_ref[...].astype(F32)
    kept_ref[...] = jnp.concatenate([own, part], axis=0)
    for step in range(1, reps):
        term = dot(picked_ref[lax.rem(rep + step, reps)], rows, 0, 0)
        sends[step - 1][...] = jnp.concatenate([term, part], axis=0).astype(BF16)


def finish_kernel(reps, kept_ref, *refs):
    got, (grad_x_ref, chunk_ref, parts_ref) = refs[: reps - 1], refs[reps - 1 :]
    rows = grad_x_ref.shape[0]
    rep = lax.axis_index("rep")
    total = kept_ref[:rows, :]
    parts_ref[rep] = kept_ref[rows:, :].astype(BF16).astype(F32)
    for step in range(1, reps):
        arrived = got[step - 1][...].astype(F32)
        total += arrived[:rows]
        parts_ref[lax.rem(rep + reps - step, reps)] = arrived[rows:]
    grad_x_ref[...] = total.astype(BF16)
    chunk = parts_ref[0]
    for other in range(1, reps):
        chunk += parts_ref[other]
    chunk_ref[...] = jnp.broadcast_to(chunk.astype(BF16)[None], chunk_ref.shape)


def local(features, weight, tiles, send_src, send_dst, cotangent):
    blocks = tiles[0, 0]
    source = send_src[0, 0]
    target = send_dst[0, 0]
    peers, slot_count = target.shape
    rows, width = features.shape
    cols, per_col, block = blocks.shape[:3]
    reps = lax.axis_size("rep")
    chips = peers // PAIR
    slots = peers * PAD
    chunk = max(16, width // peers)
    wide = width // PAD
    chip = lax.axis_index("rows") // PAIR

    def over_rep(value, step):
        return lax.ppermute(value, "rep", [(i, target_of(i, step, reps)) for i in range(reps)])

    def over_chips(value, step):
        pairs = [
            (i * PAIR + core, target_of(i, step, chips) * PAIR + core)
            for i in range(chips)
            for core in range(PAIR)
        ]
        return lax.ppermute(value, "rows", pairs)

    def to_mate(value):
        return lax.ppermute(value, "rows", [(i, i ^ 1) for i in range(peers)])

    gathered = [features] + [over_rep(features, step) for step in range(1, reps)]

    named = jnp.where(target < rows, source, -1)
    named = jnp.pad(named, ((0, 0), (0, PAD - slot_count)), constant_values=-1).reshape(1, slots)
    picked = pl.pallas_call(
        pick_kernel,
        grid=(cols,),
        out_shape=jax.ShapeDtypeStruct((cols, slots, block), BF16),
        in_specs=[
            pl.BlockSpec((1, slots), lambda b: (0, 0)),
            pl.BlockSpec((1, per_col, block, block), lambda b: (b, 0, 0, 0)),
        ],
        out_specs=pl.BlockSpec((1, slots, block), lambda b: (b, 0, 0)),
        compiler_params=params(slots),
        name="pick",
    )(named, blocks)

    tiled = jnp.tile(jnp.pad(target, ((0, 0), (0, PAD - slot_count))), (1, wide))
    at = step_to(chip, jnp.arange(peers) // PAIR, chips)
    row, lane = jnp.arange(PAD)[None, :, None], jnp.arange(width)[None, None, :]
    noted = jnp.zeros((), jnp.bool_)
    for mate in range(PAIR):
        spot = (mate * chips + at[:, None, None]) % wide
        noted = noted | ((row == slot_count + mate) & (lane // PAD == spot))
    landing = jnp.where(noted, tiled[:, None, :], 0).astype(BF16).reshape(slots, width)

    message = jax.ShapeDtypeStruct((PAIR * PAD, width), BF16)
    outgoing = pl.pallas_call(
        lambda *refs: partial_kernel(reps, chips, *refs),
        out_shape=(message,) * chips,
        in_specs=whole(2 + reps),
        out_specs=tuple(whole(chips)),
        scratch_shapes=[pltpu.VMEM((slots, width), F32)],
        compiler_params=params(slots),
        name="partial",
    )(picked, landing, *gathered)

    direct = [outgoing[0]] + [over_chips(outgoing[step], step) for step in range(1, chips)]
    shared = [to_mate(value) for value in direct]
    early_features, early_cotangent, _ = lax.optimization_barrier(
        (features, cotangent, outgoing[0])
    )

    output, back_in, *requested = pl.pallas_call(
        lambda *refs: layer_kernel(chips, slot_count, chunk, *refs),
        out_shape=(
            jax.ShapeDtypeStruct((rows, width), BF16),
            jax.ShapeDtypeStruct((rows, width), BF16),
        )
        + (jax.ShapeDtypeStruct((PAIR * PAD + chunk, width), BF16),) * chips,
        in_specs=whole(PAIR * chips + 5),
        out_specs=tuple(whole(2 + chips)),
        scratch_shapes=[pltpu.VMEM((max(width, peers * chunk), width), F32)],
        compiler_params=params(slots),
        name="layer",
    )(
        *direct,
        *shared,
        features,
        to_mate(early_features),
        cotangent,
        to_mate(early_cotangent),
        weight,
    )

    returned = [requested[0]] + [over_chips(requested[step], step) for step in range(1, chips)]

    kept, *sends = pl.pallas_call(
        lambda *refs: terms_kernel(reps, chips, *refs),
        out_shape=(jax.ShapeDtypeStruct((rows + chunk, width), F32),)
        + (jax.ShapeDtypeStruct((rows + chunk, width), BF16),) * (reps - 1),
        in_specs=whole(2 + chips),
        out_specs=tuple(whole(reps)),
        scratch_shapes=[pltpu.VMEM((slots, width), BF16)],
        compiler_params=params(slots),
        name="terms",
    )(picked, back_in, *returned)

    arrived = [
        lax.ppermute(sends[step - 1], "rep", [(i, (i + step) % reps) for i in range(reps)])
        for step in range(1, reps)
    ]

    grad_x, share = pl.pallas_call(
        lambda *refs: finish_kernel(reps, *refs),
        out_shape=(
            jax.ShapeDtypeStruct((rows, width), BF16),
            jax.ShapeDtypeStruct((peers, chunk, width), BF16),
        ),
        in_specs=whole(reps),
        out_specs=tuple(whole(2)),
        scratch_shapes=[pltpu.VMEM((reps, chunk, width), F32)],
        compiler_params=params(slots),
        name="finish",
    )(kept, *arrived)

    shares = lax.all_to_all(share, "rows", split_axis=0, concat_axis=0, tiled=True)
    node_count = rows * lax.axis_size("rows") * reps
    grad_w = shares.reshape(peers * chunk, width)[:width].astype(F32) * (
        1.0 / math.sqrt(node_count)
    )
    return (output, grad_w, grad_x)


def solution(mesh):
    placed = (
        P(("rows", "rep"), None),
        P(),
        P("rows", "rep", None, None, None, None),
        P("rows", "rep", None, None),
        P("rows", "rep", None, None),
        P(("rows", "rep"), None),
    )
    return jax.shard_map(
        local,
        mesh=mesh,
        in_specs=placed,
        out_specs=(P(("rows", "rep"), None), P(), P(("rows", "rep"), None)),
        check_vma=False,
    )
```

time: 51.2 us -> 48.5 us (0.947)
  blocking collectives: 26.4 us -> 8.94 us
  waiting for transfers between devices: 5.66 us -> 13.1 us
  starting transfers between devices: 10.9 us -> 18.3 us
    all_to_all x2 -> x0, blocking collectives: 18.5 us -> none  [the longest x1 9.33 us: local(): lax.all_to_all(requested, 'rows', split_axis=0, concat_axis=0, tiled=True)]
    ppermute x6 -> x18, waiting for transfers between devices: 5.66 us -> 13.1 us  [the longest x6 6.77 us: over_chips(): return lax.ppermute(value, 'rows', pairs)]
    ppermute x6 -> x18, starting transfers between devices: 10.9 us -> 18.3 us  [the longest x6 7.04 us: over_chips(): return lax.ppermute(value, 'rows', pairs)]
    all_to_all x1, blocking collectives: 7.91 us -> 8.94 us  [local(): lax.all_to_all(share, 'rows', split_axis=0, concat_axis=0, tiled=True)]
    unnamed x12, local copies, waits for them, and re-layouts: 2.51 us -> 1.92 us
  transfers between devices with their start and end apart: 6 -> 18, of which waited for: 3 -> 12; matrix products, arithmetic and copies ran while one was open for 1% -> 1% of each run, Pallas kernels for 3% -> 3%
where the time goes in v2:
time: 48.5 us; the launch traced here: 48.2 us
  starting transfers between devices  18.3 us (38%)
  waiting for transfers between devices  13.1 us (27%)
  blocking collectives  8.94 us (18%)
  Pallas kernels  3.91 us (8%)
  local copies, waits for them, and re-layouts  2.28 us (5%)
  other arithmetic  0.97 us (2%)
  between operations  0.73 us (2%)
    all_to_all x1, blocking collectives, local(): lax.all_to_all(share, 'rows', split_axis=0, concat_axis=0, tiled=True)  8.94 us
    ppermute x6, starting transfers between devices, over_chips(): return lax.ppermute(value, 'rows', pairs)  7.04 us
    ppermute x6, waiting for transfers between devices, over_chips(): return lax.ppermute(value, 'rows', pairs)  6.77 us
    ppermute x3, starting transfers between devices, over_rep(): lax.ppermute(value, 'rep', [(i, target_of(i, step, reps)) for i in range(...  5.76 us
    ppermute x3, starting transfers between devices, local(): lax.ppermute(sends[step - 1], 'rep', [(i, (i + step) % reps) for i in ran...  4.89 us
    ppermute x3, waiting for transfers between devices, local(): lax.ppermute(sends[step - 1], 'rep', [(i, (i + step) % reps) for i in ran...  4.43 us
    unnamed x12, local copies, waits for them, and re-layouts  1.92 us
    pallas_call x1, Pallas kernels, local(): pl.pallas_call(pick_kernel, grid=(cols,), out_shape=jax.ShapeDtypeStruct(...  1.55 us
  transfers between devices with their start and end apart: 18, of which 12 were waited for; matrix products, arithmetic and copies ran while one was open for 1% of the time, Pallas kernels for 3%

profile of v2, /device:TPU:0, one launch (start us, length us, event | category | flops | bytes accessed | tf_op | source)
XLA Modules:
  0.0 48.2 jit_solution(16046337048275653390)
XLA Ops:
  0.6 5.1 %collective-permute-start.2 = (bf16[128,256]{1,0:T(8,128)(2,1)}, bf16[128,256]{1,0:T(8,128)(2,1)S(1)}, u32[]{:S(2)}, u32[]{:S(2)}) collective-permute-start(bf16[128,256]{1,0:T(8,128)(2,1)} %refs_8_.1), channel_id=1, source_target_pairs={{0,3},{1,2},{2,1},{3,0},{4,7},{5,6},{6,5},{7,4},{8,11},{9,10},{10,... | collective-permute-start | bytes 196616 | tf_op jit(solution)/shard_map/ppermute | solution.py:184
  5.7 0.6 %collective-permute-start = (bf16[128,256]{1,0:T(8,128)(2,1)}, bf16[128,256]{1,0:T(8,128)(2,1)S(1)}, u32[]{:S(2)}, u32[]{:S(2)}) collective-permute-start(bf16[128,256]{1,0:T(8,128)(2,1)} %refs_8_.1), channel_id=1, source_target_pairs={{0,1},{1,0},{2,3},{3,2},{4,5},{5,4},{6,7},{7,6},{8,9},{9,8},{10,11... | collective-permute-start | bytes 196616 | tf_op jit(solution)/shard_map/ppermute | solution.py:184
  6.5 0.6 %copy-done.5 = s32[1,1,8,24]{3,2,1,0:T(8,128)S(1)} copy-done((s32[1,1,8,24]{3,2,1,0:T(8,128)S(1)}, s32[1,1,8,24]{3,2,1,0:T(8,128)}, u32[]{:S(2)}) %copy-start.5) | copy-done | bytes 792
  7.5 1.2 %copy-done = bf16[1,1,4,8,128,128]{5,4,3,2,1,0:T(8,128)(2,1)S(1)} copy-done((bf16[1,1,4,8,128,128]{5,4,3,2,1,0:T(8,128)(2,1)S(1)}, bf16[1,1,4,8,128,128]{5,4,3,2,1,0:T(8,128)(2,1)}, u32[]{:S(2)}) %copy-start) | copy-done | bytes 1048600
  8.8 1.6 %pick.1.refs_0_ = bf16[4,256,128]{2,1,0:T(8,128)(2,1)S(1)} custom-call(s32[1,256]{1,0:T(1,128)S(1)} %reshape.182.source_ref, bf16[4,8,128,128]{3,2,1,0:T(8,128)(2,1)S(1)} %bitcast.20), custom_call_target="tpu_custom_call" | custom-call | tf_op jit(solution)/shard_map/pick/pallas_call | solution.py:201
  10.5 1.0 %collective-permute-done.1.refs_4_ = bf16[128,256]{1,0:T(8,128)(2,1)S(1)} collective-permute-done((bf16[128,256]{1,0:T(8,128)(2,1)}, bf16[128,256]{1,0:T(8,128)(2,1)S(1)}, u32[]{:S(2)}, u32[]{:S(2)}) %collective-permute-start.1) | collective-permute-done | bytes 65568 | tf_op jit(solution)/shard_map/ppermute | solution.py:184
  11.9 1.6 %collective-permute-start.3 = (bf16[64,256]{1,0:T(8,128)(2,1)S(1)}, bf16[64,256]{1,0:T(8,128)(2,1)S(1)}, u32[]{:S(2)}, u32[]{:S(2)}) collective-permute-start(bf16[64,256]{1,0:T(8,128)(2,1)S(1)} %get-tuple-element.22), channel_id=1, source_target_pairs={{0,8},{4,12},{8,0},{12,4},{16,24},{20,28},{24,16},{28,20},{1,9},{5... | collective-permute-start | bytes 98312 | tf_op jit(solution)/shard_map/ppermute | solution.py:192
  13.4 1.5 %collective-permute-start.4 = (bf16[64,256]{1,0:T(8,128)(2,1)S(1)}, bf16[64,256]{1,0:T(8,128)(2,1)S(1)}, u32[]{:S(2)}, u32[]{:S(2)}) collective-permute-start(bf16[64,256]{1,0:T(8,128)(2,1)S(1)} %get-tuple-element.23), channel_id=1, source_target_pairs={{0,16},{4,20},{8,24},{12,28},{16,0},{20,4},{24,8},{28,12},{1,17},{... | collective-permute-start | bytes 98312 | tf_op jit(solution)/shard_map/ppermute | solution.py:192
  15.9 1.4 %collective-permute-done.4.refs_2_ = bf16[64,256]{1,0:T(8,128)(2,1)S(1)} collective-permute-done((bf16[64,256]{1,0:T(8,128)(2,1)S(1)}, bf16[64,256]{1,0:T(8,128)(2,1)S(1)}, u32[]{:S(2)}, u32[]{:S(2)}) %collective-permute-start.4) | collective-permute-done | bytes 32800 | tf_op jit(solution)/shard_map/ppermute | solution.py:192
  17.4 2.4 %collective-permute-done.5.refs_3_ = bf16[64,256]{1,0:T(8,128)(2,1)S(1)} collective-permute-done((bf16[64,256]{1,0:T(8,128)(2,1)S(1)}, bf16[64,256]{1,0:T(8,128)(2,1)S(1)}, u32[]{:S(2)}, u32[]{:S(2)}) %collective-permute-start.5) | collective-permute-done | bytes 32800 | tf_op jit(solution)/shard_map/ppermute | solution.py:192
  20.3 0.7 %collective-permute-done.8.refs_6_ = bf16[64,256]{1,0:T(8,128)(2,1)S(1)} collective-permute-done((bf16[64,256]{1,0:T(8,128)(2,1)S(1)}, bf16[64,256]{1,0:T(8,128)(2,1)S(1)}, u32[]{:S(2)}, u32[]{:S(2)}) %collective-permute-start.8) | collective-permute-done | bytes 32800 | tf_op jit(solution)/shard_map/ppermute | solution.py:195
  21.2 1.1 %layer.1 = (bf16[128,256]{1,0:T(8,128)(2,1)}, bf16[128,256]{1,0:T(8,128)(2,1)S(1)}, bf16[96,256]{1,0:T(8,128)(2,1)S(1)}, bf16[96,256]{1,0:T(8,128)(2,1)S(1)}, bf...) custom-call(bf16[64,256]{1,0:T(8,128)(2,1)S(1)} %get-tuple-element.21.refs_0_, ...), custom_call_target="tpu_custom_call" | custom-call | tf_op jit(solution)/shard_map/layer/pallas_call | solution.py:240
  23.3 2.4 %collective-permute-start.14 = (bf16[96,256]{1,0:T(8,128)(2,1)S(1)}, bf16[96,256]{1,0:T(8,128)(2,1)S(1)}, u32[]{:S(2)}, u32[]{:S(2)}) collective-permute-start(bf16[96,256]{1,0:T(8,128)(2,1)S(1)} %get-tuple-element.32), channel_id=1, source_target_pairs={{0,24},{4,28},{8,16},{12,20},{16,8},{20,12},{24,0},{28,4},{1,25},{... | collective-permute-start | bytes 147464 | tf_op jit(solution)/shard_map/ppermute | solution.py:192
  25.8 0.6 %collective-permute-done.12.refs_3_ = bf16[96,256]{1,0:T(8,128)(2,1)S(1)} collective-permute-done((bf16[96,256]{1,0:T(8,128)(2,1)S(1)}, bf16[96,256]{1,0:T(8,128)(2,1)S(1)}, u32[]{:S(2)}, u32[]{:S(2)}) %collective-permute-start.12) | collective-permute-done | bytes 49184 | tf_op jit(solution)/shard_map/ppermute | solution.py:192
  26.4 1.1 %collective-permute-done.13.refs_4_ = bf16[96,256]{1,0:T(8,128)(2,1)S(1)} collective-permute-done((bf16[96,256]{1,0:T(8,128)(2,1)S(1)}, bf16[96,256]{1,0:T(8,128)(2,1)S(1)}, u32[]{:S(2)}, u32[]{:S(2)}) %collective-permute-start.13) | collective-permute-done | bytes 49184 | tf_op jit(solution)/shard_map/ppermute | solution.py:192
  27.4 0.9 %collective-permute-done.14.refs_5_ = bf16[96,256]{1,0:T(8,128)(2,1)S(1)} collective-permute-done((bf16[96,256]{1,0:T(8,128)(2,1)S(1)}, bf16[96,256]{1,0:T(8,128)(2,1)S(1)}, u32[]{:S(2)}, u32[]{:S(2)}) %collective-permute-start.14) | collective-permute-done | bytes 49184 | tf_op jit(solution)/shard_map/ppermute | solution.py:192
  28.6 1.1 %collective-permute-start.15 = (bf16[160,256]{1,0:T(8,128)(2,1)S(1)}, bf16[160,256]{1,0:T(8,128)(2,1)S(1)}, u32[]{:S(2)}, u32[]{:S(2)}) collective-permute-start(bf16[160,256]{1,0:T(8,128)(2,1)S(1)} %get-tuple-element.34), channel_id=1, source_target_pairs={{0,1},{1,2},{2,3},{3,0},{4,5},{5,6},{6,7},{7,4},{8,9},{9,10},{10,1... | collective-permute-start | bytes 245768 | tf_op jit(solution)/shard_map/ppermute | solution.py:276
  29.7 2.8 %collective-permute-start.16 = (bf16[160,256]{1,0:T(8,128)(2,1)S(1)}, bf16[160,256]{1,0:T(8,128)(2,1)S(1)}, u32[]{:S(2)}, u32[]{:S(2)}) collective-permute-start(bf16[160,256]{1,0:T(8,128)(2,1)S(1)} %get-tuple-element.35), channel_id=1, source_target_pairs={{0,2},{1,3},{2,0},{3,1},{4,6},{5,7},{6,4},{7,5},{8,10},{9,11},{10,... | collective-permute-start | bytes 245768 | tf_op jit(solution)/shard_map/ppermute | solution.py:276
  32.6 0.9 %collective-permute-start.17 = (bf16[160,256]{1,0:T(8,128)(2,1)S(1)}, bf16[160,256]{1,0:T(8,128)(2,1)S(1)}, u32[]{:S(2)}, u32[]{:S(2)}) collective-permute-start(bf16[160,256]{1,0:T(8,128)(2,1)S(1)} %get-tuple-element.36), channel_id=1, source_target_pairs={{0,3},{1,0},{2,1},{3,2},{4,7},{5,4},{6,5},{7,6},{8,11},{9,8},{10,9... | collective-permute-start | bytes 245768 | tf_op jit(solution)/shard_map/ppermute | solution.py:276
  33.5 1.9 %collective-permute-done.15.refs_1_ = bf16[160,256]{1,0:T(8,128)(2,1)S(1)} collective-permute-done((bf16[160,256]{1,0:T(8,128)(2,1)S(1)}, bf16[160,256]{1,0:T(8,128)(2,1)S(1)}, u32[]{:S(2)}, u32[]{:S(2)}) %collective-permute-start.15) | collective-permute-done | bytes 81952 | tf_op jit(solution)/shard_map/ppermute | solution.py:276
  35.4 2.4 %collective-permute-done.16.refs_2_ = bf16[160,256]{1,0:T(8,128)(2,1)S(1)} collective-permute-done((bf16[160,256]{1,0:T(8,128)(2,1)S(1)}, bf16[160,256]{1,0:T(8,128)(2,1)S(1)}, u32[]{:S(2)}, u32[]{:S(2)}) %collective-permute-start.16) | collective-permute-done | bytes 81952 | tf_op jit(solution)/shard_map/ppermute | solution.py:276
  37.9 0.7 %finish.1 = (bf16[128,256]{1,0:T(8,128)(2,1)}, bf16[8,32,256]{2,1,0:T(8,128)(2,1)S(1)}) custom-call(f32[160,256]{1,0:T(8,128)S(1)} %get-tuple-element.33.refs_0_, bf16[160,256]{1,0:T(8,128)(2,1)S(1)} %collective-permute-done.15.refs_1_, bf16[160,256]{1,0:T(8,128)(2,1)S(1)} %collective-permute-done.16.refs_2_, ...), custom_call_target="tpu_custom_call" | custom-call | tf_op jit(solution)/shard_map/finish/pallas_call | solution.py:280
  38.6 8.9 %all_to_all.5 = bf16[8,32,256]{2,1,0:T(8,128)(2,1)S(1)} all-to-all(bf16[8,32,256]{2,1,0:T(8,128)(2,1)S(1)} %get-tuple-element.37), channel_id=1, replica_groups=mesh['rows'=8,'rep'=4] {'rows'}, dimensions={0} | all-to-all | bytes 262144 | tf_op jit(solution)/shard_map/all_to_all | solution.py:293
  47.5 0.7 %convert_multiply_fusion = f32[8,32,256]{2,1,0:T(8,128)} fusion(bf16[8,32,256]{2,1,0:T(8,128)(2,1)S(1)} %all_to_all.5), kind=kLoop, calls=%fused_computation.2 | loop fusion | flops 131072 | bytes 393216 | tf_op jit(solution)/shard_map/mul | solution.py:295
  (47 shorter events, 4.2 us)
Async XLA Ops:
  0.6 9.9 %collective-permute-start.2 = (bf16[128,256]{1,0:T(8,128)(2,1)}, bf16[128,256]{1,0:T(8,128)(2,1)S(1)}, u32[]{:S(2)}, u32[]{:S(2)}) collective-permute-start(bf16[128,256]{1,0:T(8,128)(2,1)} %refs_8_.1), channel_id=1, source_target_pairs={{0,3},{1,2},{2,1},{3,0},{4,7},{5,6},{6,5},{7,4},{8,11},{9,10},{10,... | collective-permute-start | bytes 196616 | tf_op jit(solution)/shard_map/ppermute | solution.py:184
  5.7 5.8 %collective-permute-start.1 = (bf16[128,256]{1,0:T(8,128)(2,1)}, bf16[128,256]{1,0:T(8,128)(2,1)S(1)}, u32[]{:S(2)}, u32[]{:S(2)}) collective-permute-start(bf16[128,256]{1,0:T(8,128)(2,1)} %refs_8_.1), channel_id=1, source_target_pairs={{0,2},{1,3},{2,0},{3,1},{4,6},{5,7},{6,4},{7,5},{8,10},{9,11},{10,... | collective-permute-start | bytes 196616 | tf_op jit(solution)/shard_map/ppermute | solution.py:184
  5.7 5.8 %collective-permute-start = (bf16[128,256]{1,0:T(8,128)(2,1)}, bf16[128,256]{1,0:T(8,128)(2,1)S(1)}, u32[]{:S(2)}, u32[]{:S(2)}) collective-permute-start(bf16[128,256]{1,0:T(8,128)(2,1)} %refs_8_.1), channel_id=1, source_target_pairs={{0,1},{1,0},{2,3},{3,2},{4,5},{5,4},{6,7},{7,6},{8,9},{9,8},{10,11... | collective-permute-start | bytes 196616 | tf_op jit(solution)/shard_map/ppermute | solution.py:184
  6.4 0.7 %copy-start.5 = (s32[1,1,8,24]{3,2,1,0:T(8,128)S(1)}, s32[1,1,8,24]{3,2,1,0:T(8,128)}, u32[]{:S(2)}) copy-start(s32[1,1,8,24]{3,2,1,0:T(8,128)} %param.9) | copy-start | bytes 2308
  6.5 0.7 %copy-start.4 = (s32[1,1,8,24]{3,2,1,0:T(8,128)S(1)}, s32[1,1,8,24]{3,2,1,0:T(8,128)}, u32[]{:S(2)}) copy-start(s32[1,1,8,24]{3,2,1,0:T(8,128)} %param.10) | copy-start | bytes 2308
  7.5 1.2 %copy-start = (bf16[1,1,4,8,128,128]{5,4,3,2,1,0:T(8,128)(2,1)S(1)}, bf16[1,1,4,8,128,128]{5,4,3,2,1,0:T(8,128)(2,1)}, u32[]{:S(2)}) copy-start(bf16[1,1,4,8,128,128]{5,4,3,2,1,0:T(8,128)(2,1)} %param.8) | copy-start | bytes 3145732
  10.3 1.2 %copy-start.1 = (bf16[128,256]{1,0:T(8,128)(2,1)S(1)}, bf16[128,256]{1,0:T(8,128)(2,1)}, u32[]{:S(2)}) copy-start(bf16[128,256]{1,0:T(8,128)(2,1)} %refs_8_.1) | copy-start | bytes 196612
  10.5 5.4 %copy-start.3 = (bf16[128,256]{1,0:T(8,128)(2,1)S(1)}, bf16[128,256]{1,0:T(8,128)(2,1)}, u32[]{:S(2)}) copy-start(bf16[128,256]{1,0:T(8,128)(2,1)} %refs_10_.1) | copy-start | bytes 196612
  10.5 10.6 %copy-start.2 = (bf16[256,256]{1,0:T(8,128)(2,1)S(1)}, bf16[256,256]{1,0:T(8,128)(2,1)}, u32[]{:S(2)}) copy-start(bf16[256,256]{1,0:T(8,128)(2,1)} %refs_12_.1) | copy-start | bytes 393220
  11.9 4.0 %collective-permute-start.3 = (bf16[64,256]{1,0:T(8,128)(2,1)S(1)}, bf16[64,256]{1,0:T(8,128)(2,1)S(1)}, u32[]{:S(2)}, u32[]{:S(2)}) collective-permute-start(bf16[64,256]{1,0:T(8,128)(2,1)S(1)} %get-tuple-element.22), channel_id=1, source_target_pairs={{0,8},{4,12},{8,0},{12,4},{16,24},{20,28},{24,16},{28,20},{1,9},{5... | collective-permute-start | bytes 98312 | tf_op jit(solution)/shard_map/ppermute | solution.py:192
  13.4 6.3 %collective-permute-start.6 = (bf16[64,256]{1,0:T(8,128)(2,1)S(1)}, bf16[64,256]{1,0:T(8,128)(2,1)S(1)}, u32[]{:S(2)}, u32[]{:S(2)}) collective-permute-start(bf16[64,256]{1,0:T(8,128)(2,1)S(1)} %get-tuple-element.21.refs_0_), channel_id=1, source_target_pairs={{0,4},{4,0},{8,12},{12,8},{16,20},{20,16},{24,28},{28,24},{1,5},{5... | collective-permute-start | bytes 98312 | tf_op jit(solution)/shard_map/ppermute | solution.py:195
  13.4 3.9 %collective-permute-start.4 = (bf16[64,256]{1,0:T(8,128)(2,1)S(1)}, bf16[64,256]{1,0:T(8,128)(2,1)S(1)}, u32[]{:S(2)}, u32[]{:S(2)}) collective-permute-start(bf16[64,256]{1,0:T(8,128)(2,1)S(1)} %get-tuple-element.23), channel_id=1, source_target_pairs={{0,16},{4,20},{8,24},{12,28},{16,0},{20,4},{24,8},{28,12},{1,17},{... | collective-permute-start | bytes 98312 | tf_op jit(solution)/shard_map/ppermute | solution.py:192
  15.0 4.8 %collective-permute-start.5 = (bf16[64,256]{1,0:T(8,128)(2,1)S(1)}, bf16[64,256]{1,0:T(8,128)(2,1)S(1)}, u32[]{:S(2)}, u32[]{:S(2)}) collective-permute-start(bf16[64,256]{1,0:T(8,128)(2,1)S(1)} %get-tuple-element.24), channel_id=1, source_target_pairs={{0,24},{4,28},{8,16},{12,20},{16,8},{20,12},{24,0},{28,4},{1,25},{... | collective-permute-start | bytes 98312 | tf_op jit(solution)/shard_map/ppermute | solution.py:192
  15.4 5.7 %collective-permute-start.10 = (bf16[128,256]{1,0:T(8,128)(2,1)S(1)}, bf16[128,256]{1,0:T(8,128)(2,1)S(1)}, u32[]{:S(2)}, u32[]{:S(2)}) collective-permute-start(bf16[128,256]{1,0:T(8,128)(2,1)S(1)} %copy-done.1), channel_id=1, source_target_pairs={{0,4},{4,0},{8,12},{12,8},{16,20},{20,16},{24,28},{28,24},{1,5},{5... | collective-permute-start | bytes 196616 | tf_op jit(solution)/shard_map/ppermute | solution.py:195
  15.9 5.3 %collective-permute-start.11 = (bf16[128,256]{1,0:T(8,128)(2,1)S(1)}, bf16[128,256]{1,0:T(8,128)(2,1)S(1)}, u32[]{:S(2)}, u32[]{:S(2)}) collective-permute-start(bf16[128,256]{1,0:T(8,128)(2,1)S(1)} %copy-done.3), channel_id=1, source_target_pairs={{0,4},{4,0},{8,12},{12,8},{16,20},{20,16},{24,28},{28,24},{1,5},{5... | collective-permute-start | bytes 196616 | tf_op jit(solution)/shard_map/ppermute | solution.py:195
  17.3 2.9 %collective-permute-start.7 = (bf16[64,256]{1,0:T(8,128)(2,1)S(1)}, bf16[64,256]{1,0:T(8,128)(2,1)S(1)}, u32[]{:S(2)}, u32[]{:S(2)}) collective-permute-start(bf16[64,256]{1,0:T(8,128)(2,1)S(1)} %collective-permute-done.3.refs_1_), channel_id=1, source_target_pairs={{0,4},{4,0},{8,12},{12,8},{16,20},{20,16},{24,28},{28,24},{1,5},{5... | collective-permute-start | bytes 98312 | tf_op jit(solution)/shard_map/ppermute | solution.py:195
  19.8 1.2 %collective-permute-start.8 = (bf16[64,256]{1,0:T(8,128)(2,1)S(1)}, bf16[64,256]{1,0:T(8,128)(2,1)S(1)}, u32[]{:S(2)}, u32[]{:S(2)}) collective-permute-start(bf16[64,256]{1,0:T(8,128)(2,1)S(1)} %collective-permute-done.4.refs_2_), channel_id=1, source_target_pairs={{0,4},{4,0},{8,12},{12,8},{16,20},{20,16},{24,28},{28,24},{1,5},{5... | collective-permute-start | bytes 98312 | tf_op jit(solution)/shard_map/ppermute | solution.py:195
  19.8 1.4 %collective-permute-start.9 = (bf16[64,256]{1,0:T(8,128)(2,1)S(1)}, bf16[64,256]{1,0:T(8,128)(2,1)S(1)}, u32[]{:S(2)}, u32[]{:S(2)}) collective-permute-start(bf16[64,256]{1,0:T(8,128)(2,1)S(1)} %collective-permute-done.5.refs_3_), channel_id=1, source_target_pairs={{0,4},{4,0},{8,12},{12,8},{16,20},{20,16},{24,28},{28,24},{1,5},{5... | collective-permute-start | bytes 98312 | tf_op jit(solution)/shard_map/ppermute | solution.py:195
  22.3 4.1 %collective-permute-start.12 = (bf16[96,256]{1,0:T(8,128)(2,1)S(1)}, bf16[96,256]{1,0:T(8,128)(2,1)S(1)}, u32[]{:S(2)}, u32[]{:S(2)}) collective-permute-start(bf16[96,256]{1,0:T(8,128)(2,1)S(1)} %get-tuple-element.30), channel_id=1, source_target_pairs={{0,8},{4,12},{8,0},{12,4},{16,24},{20,28},{24,16},{28,20},{1,9},{5... | collective-permute-start | bytes 147464 | tf_op jit(solution)/shard_map/ppermute | solution.py:192
  22.8 4.6 %collective-permute-start.13 = (bf16[96,256]{1,0:T(8,128)(2,1)S(1)}, bf16[96,256]{1,0:T(8,128)(2,1)S(1)}, u32[]{:S(2)}, u32[]{:S(2)}) collective-permute-start(bf16[96,256]{1,0:T(8,128)(2,1)S(1)} %get-tuple-element.31), channel_id=1, source_target_pairs={{0,16},{4,20},{8,24},{12,28},{16,0},{20,4},{24,8},{28,12},{1,17},{... | collective-permute-start | bytes 147464 | tf_op jit(solution)/shard_map/ppermute | solution.py:192
  23.3 5.0 %collective-permute-start.14 = (bf16[96,256]{1,0:T(8,128)(2,1)S(1)}, bf16[96,256]{1,0:T(8,128)(2,1)S(1)}, u32[]{:S(2)}, u32[]{:S(2)}) collective-permute-start(bf16[96,256]{1,0:T(8,128)(2,1)S(1)} %get-tuple-element.32), channel_id=1, source_target_pairs={{0,24},{4,28},{8,16},{12,20},{16,8},{20,12},{24,0},{28,4},{1,25},{... | collective-permute-start | bytes 147464 | tf_op jit(solution)/shard_map/ppermute | solution.py:192
  28.6 6.8 %collective-permute-start.15 = (bf16[160,256]{1,0:T(8,128)(2,1)S(1)}, bf16[160,256]{1,0:T(8,128)(2,1)S(1)}, u32[]{:S(2)}, u32[]{:S(2)}) collective-permute-start(bf16[160,256]{1,0:T(8,128)(2,1)S(1)} %get-tuple-element.34), channel_id=1, source_target_pairs={{0,1},{1,2},{2,3},{3,0},{4,5},{5,6},{6,7},{7,4},{8,9},{9,10},{10,1... | collective-permute-start | bytes 245768 | tf_op jit(solution)/shard_map/ppermute | solution.py:276
  29.7 8.0 %collective-permute-start.16 = (bf16[160,256]{1,0:T(8,128)(2,1)S(1)}, bf16[160,256]{1,0:T(8,128)(2,1)S(1)}, u32[]{:S(2)}, u32[]{:S(2)}) collective-permute-start(bf16[160,256]{1,0:T(8,128)(2,1)S(1)} %get-tuple-element.35), channel_id=1, source_target_pairs={{0,2},{1,3},{2,0},{3,1},{4,6},{5,7},{6,4},{7,5},{8,10},{9,11},{10,... | collective-permute-start | bytes 245768 | tf_op jit(solution)/shard_map/ppermute | solution.py:276
  32.6 5.3 %collective-permute-start.17 = (bf16[160,256]{1,0:T(8,128)(2,1)S(1)}, bf16[160,256]{1,0:T(8,128)(2,1)S(1)}, u32[]{:S(2)}, u32[]{:S(2)}) collective-permute-start(bf16[160,256]{1,0:T(8,128)(2,1)S(1)} %get-tuple-element.36), channel_id=1, source_target_pairs={{0,3},{1,0},{2,1},{3,2},{4,7},{5,4},{6,5},{7,6},{8,11},{9,8},{10,9... | collective-permute-start | bytes 245768 | tf_op jit(solution)/shard_map/ppermute | solution.py:276

commit v3 on v2

--- a/solution.py
+++ b/solution.py
@@ -149,21 +149,38 @@
         sends[step - 1][...] = jnp.concatenate([term, part], axis=0).astype(BF16)
 
 
-def finish_kernel(reps, kept_ref, *refs):
-    got, (grad_x_ref, chunk_ref, parts_ref) = refs[: reps - 1], refs[reps - 1 :]
-    rows = grad_x_ref.shape[0]
+def chunk_kernel(reps, kept_ref, *refs):
+    got, (chunk_ref, parts_ref) = refs[: reps - 1], refs[reps - 1 :]
+    depth = chunk_ref.shape[0]
+    rows = kept_ref.shape[0] - depth
     rep = lax.axis_index("rep")
-    total = kept_ref[:rows, :]
     parts_ref[rep] = kept_ref[rows:, :].astype(BF16).astype(F32)
     for step in range(1, reps):
-        arrived = got[step - 1][...].astype(F32)
-        total += arrived[:rows]
-        parts_ref[lax.rem(rep + reps - step, reps)] = arrived[rows:]
-    grad_x_ref[...] = total.astype(BF16)
+        parts_ref[lax.rem(rep + reps - step, reps)] = got[step - 1][rows:, :].astype(F32)
     chunk = parts_ref[0]
     for other in range(1, reps):
         chunk += parts_ref[other]
-    chunk_ref[...] = jnp.broadcast_to(chunk.astype(BF16)[None], chunk_ref.shape)
+    chunk_ref[...] = chunk.astype(BF16)
+
+
+def grad_x_kernel(kept_ref, *refs):
+    got, grad_x_ref = refs[:-1], refs[-1]
+    rows = grad_x_ref.shape[0]
+    total = kept_ref[:rows, :]
+    for ref in got:
+        total += ref[:rows, :].astype(F32)
+    grad_x_ref[...] = total.astype(BF16)
+
+
+def grad_w_kernel(chips, scale, *refs):
+    got, grad_w_ref = refs[:-1], refs[-1]
+    chunk = got[0].shape[0]
+    core = lax.rem(lax.axis_index("rows"), PAIR)
+    chip = lax.div(lax.axis_index("rows"), PAIR)
+    for at, ref in enumerate(got):
+        half = core if at < chips else 1 - core
+        first = (origin_of(chip, at % chips, chips) * PAIR + half) * chunk
+        grad_w_ref[pl.ds(pl.multiple_of(first, chunk), chunk), :] = ref[...].astype(F32) * scale
 
 
 def local(features, weight, tiles, send_src, send_dst, cotangent):
@@ -277,24 +294,37 @@
         for step in range(1, reps)
     ]
 
-    grad_x, share = pl.pallas_call(
-        lambda *refs: finish_kernel(reps, *refs),
-        out_shape=(
-            jax.ShapeDtypeStruct((rows, width), BF16),
-            jax.ShapeDtypeStruct((peers, chunk, width), BF16),
-        ),
+    share = pl.pallas_call(
+        lambda *refs: chunk_kernel(reps, *refs),
+        out_shape=jax.ShapeDtypeStruct((chunk, width), BF16),
         in_specs=whole(reps),
-        out_specs=tuple(whole(2)),
+        out_specs=whole(1)[0],
         scratch_shapes=[pltpu.VMEM((reps, chunk, width), F32)],
         compiler_params=params(slots),
-        name="finish",
+        name="chunk",
     )(kept, *arrived)
 
-    shares = lax.all_to_all(share, "rows", split_axis=0, concat_axis=0, tiled=True)
+    shares = [share] + [over_chips(share, step) for step in range(1, chips)]
+    shares += [to_mate(value) for value in shares]
+
+    grad_x = pl.pallas_call(
+        grad_x_kernel,
+        out_shape=jax.ShapeDtypeStruct((rows, width), BF16),
+        in_specs=whole(reps),
+        out_specs=whole(1)[0],
+        compiler_params=params(slots),
+        name="grad_x",
+    )(kept, *arrived)
+
     node_count = rows * lax.axis_size("rows") * reps
-    grad_w = shares.reshape(peers * chunk, width)[:width].astype(F32) * (
-        1.0 / math.sqrt(node_count)
-    )
+    grad_w = pl.pallas_call(
+        lambda *refs: grad_w_kernel(chips, 1.0 / math.sqrt(node_count), *refs),
+        out_shape=jax.ShapeDtypeStruct((peers * chunk, width), F32),
+        in_specs=whole(PAIR * chips),
+        out_specs=whole(1)[0],
+        compiler_params=params(slots),
+        name="grad_w",
+    )(*shares)[:width]
     return (output, grad_w, grad_x)
 
 

time: 48.5 us -> 46.8 us (0.965)
  blocking collectives: 8.94 us -> 0 us
  waiting for transfers between devices: 13.1 us -> 16.8 us
  starting transfers between devices: 18.3 us -> 21.9 us
  Pallas kernels: 3.91 us -> 4.66 us
  other arithmetic: 0.97 us -> 0.24 us
    all_to_all x1 -> x0, blocking collectives: 8.94 us -> none  [local(): lax.all_to_all(share, 'rows', split_axis=0, concat_axis=0, tiled=True)]
    ppermute x6 -> x9, starting transfers between devices: 7.04 us -> 10.6 us  [over_chips(): return lax.ppermute(value, 'rows', pairs)]
    ppermute x6 -> x9, waiting for transfers between devices: 6.77 us -> 9.97 us  [over_chips(): return lax.ppermute(value, 'rows', pairs)]
    pallas_call x1 -> x3, Pallas kernels: 0.67 us -> 1.42 us  [the longest x1 0.73 us: local(): pl.pallas_call(lambda *refs: grad_w_kernel(chips, 1.0 / math.sqrt(node_co...]
    mul x1 -> x0, other arithmetic: 0.73 us -> none  [local(): shares.reshape(peers * chunk, width)[:width].astype(F32)]
    ppermute x6 -> x10, waiting for transfers between devices: 0.87 us -> 1.38 us  [to_mate(): return lax.ppermute(value, 'rows', [(i, i ^ 1) for i in range(peers)])]
  transfers between devices with their start and end apart: 18 -> 25, of which waited for: 12 -> 16; matrix products, arithmetic and copies ran while one was open for 1% -> 1% of each run, Pallas kernels for 3% -> 5%
where the time goes in v3:
time: 46.8 us; the launch traced here: 46.6 us
  starting transfers between devices  21.9 us (47%)
  waiting for transfers between devices  16.8 us (36%)
  Pallas kernels  4.66 us (10%)
  local copies, waits for them, and re-layouts  2.28 us (5%)
  between operations  0.75 us (2%)
    ppermute x9, starting transfers between devices, over_chips(): return lax.ppermute(value, 'rows', pairs)  10.6 us
    ppermute x9, waiting for transfers between devices, over_chips(): return lax.ppermute(value, 'rows', pairs)  9.97 us
    ppermute x3, starting transfers between devices, over_rep(): lax.ppermute(value, 'rep', [(i, target_of(i, step, reps)) for i in range(...  5.76 us
    ppermute x3, starting transfers between devices, local(): lax.ppermute(sends[step - 1], 'rep', [(i, (i + step) % reps) for i in ran...  4.89 us
    ppermute x3, waiting for transfers between devices, local(): lax.ppermute(sends[step - 1], 'rep', [(i, (i + step) % reps) for i in ran...  4.43 us
    unnamed x12, local copies, waits for them, and re-layouts  1.92 us
    pallas_call x1, Pallas kernels, local(): pl.pallas_call(pick_kernel, grid=(cols,), out_shape=jax.ShapeDtypeStruct(...  1.55 us
    ppermute x10, waiting for transfers between devices, to_mate(): return lax.ppermute(value, 'rows', [(i, i ^ 1) for i in range(peers)])  1.38 us
  transfers between devices with their start and end apart: 25, of which 16 were waited for; matrix products, arithmetic and copies ran while one was open for 1% of the time, Pallas kernels for 5%

profile of v3, /device:TPU:0, one launch (start us, length us, event | category | flops | bytes accessed | tf_op | source)
XLA Modules:
  0.0 46.6 jit_solution(1704284179848971544)
XLA Ops:
  0.6 5.1 %collective-permute-start.2 = (bf16[128,256]{1,0:T(8,128)(2,1)}, bf16[128,256]{1,0:T(8,128)(2,1)S(1)}, u32[]{:S(2)}, u32[]{:S(2)}) collective-permute-start(bf16[128,256]{1,0:T(8,128)(2,1)} %refs_8_.1), channel_id=1, source_target_pairs={{0,3},{1,2},{2,1},{3,0},{4,7},{5,6},{6,5},{7,4},{8,11},{9,10},{10,... | collective-permute-start | bytes 196616 | tf_op jit(solution)/shard_map/ppermute | solution.py:201
  5.7 0.6 %collective-permute-start = (bf16[128,256]{1,0:T(8,128)(2,1)}, bf16[128,256]{1,0:T(8,128)(2,1)S(1)}, u32[]{:S(2)}, u32[]{:S(2)}) collective-permute-start(bf16[128,256]{1,0:T(8,128)(2,1)} %refs_8_.1), channel_id=1, source_target_pairs={{0,1},{1,0},{2,3},{3,2},{4,5},{5,4},{6,7},{7,6},{8,9},{9,8},{10,11... | collective-permute-start | bytes 196616 | tf_op jit(solution)/shard_map/ppermute | solution.py:201
  7.5 1.2 %copy-done = bf16[1,1,4,8,128,128]{5,4,3,2,1,0:T(8,128)(2,1)S(1)} copy-done((bf16[1,1,4,8,128,128]{5,4,3,2,1,0:T(8,128)(2,1)S(1)}, bf16[1,1,4,8,128,128]{5,4,3,2,1,0:T(8,128)(2,1)}, u32[]{:S(2)}) %copy-start) | copy-done | bytes 1048600
  8.8 1.6 %pick.1.refs_0_ = bf16[4,256,128]{2,1,0:T(8,128)(2,1)S(1)} custom-call(s32[1,256]{1,0:T(1,128)S(1)} %reshape.178.source_ref, bf16[4,8,128,128]{3,2,1,0:T(8,128)(2,1)S(1)} %bitcast.19), custom_call_target="tpu_custom_call" | custom-call | tf_op jit(solution)/shard_map/pick/pallas_call | solution.py:218
  10.5 1.0 %collective-permute-done.1.refs_4_ = bf16[128,256]{1,0:T(8,128)(2,1)S(1)} collective-permute-done((bf16[128,256]{1,0:T(8,128)(2,1)}, bf16[128,256]{1,0:T(8,128)(2,1)S(1)}, u32[]{:S(2)}, u32[]{:S(2)}) %collective-permute-start.1) | collective-permute-done | bytes 65568 | tf_op jit(solution)/shard_map/ppermute | solution.py:201
  11.9 1.6 %collective-permute-start.3 = (bf16[64,256]{1,0:T(8,128)(2,1)S(1)}, bf16[64,256]{1,0:T(8,128)(2,1)S(1)}, u32[]{:S(2)}, u32[]{:S(2)}) collective-permute-start(bf16[64,256]{1,0:T(8,128)(2,1)S(1)} %get-tuple-element.20), channel_id=1, source_target_pairs={{0,8},{4,12},{8,0},{12,4},{16,24},{20,28},{24,16},{28,20},{1,9},{5... | collective-permute-start | bytes 98312 | tf_op jit(solution)/shard_map/ppermute | solution.py:209
  13.4 1.5 %collective-permute-start.4 = (bf16[64,256]{1,0:T(8,128)(2,1)S(1)}, bf16[64,256]{1,0:T(8,128)(2,1)S(1)}, u32[]{:S(2)}, u32[]{:S(2)}) collective-permute-start(bf16[64,256]{1,0:T(8,128)(2,1)S(1)} %get-tuple-element.21), channel_id=1, source_target_pairs={{0,16},{4,20},{8,24},{12,28},{16,0},{20,4},{24,8},{28,12},{1,17},{... | collective-permute-start | bytes 98312 | tf_op jit(solution)/shard_map/ppermute | solution.py:209
  15.9 1.4 %collective-permute-done.4.refs_2_ = bf16[64,256]{1,0:T(8,128)(2,1)S(1)} collective-permute-done((bf16[64,256]{1,0:T(8,128)(2,1)S(1)}, bf16[64,256]{1,0:T(8,128)(2,1)S(1)}, u32[]{:S(2)}, u32[]{:S(2)}) %collective-permute-start.4) | collective-permute-done | bytes 32800 | tf_op jit(solution)/shard_map/ppermute | solution.py:209
  17.4 2.4 %collective-permute-done.5.refs_3_ = bf16[64,256]{1,0:T(8,128)(2,1)S(1)} collective-permute-done((bf16[64,256]{1,0:T(8,128)(2,1)S(1)}, bf16[64,256]{1,0:T(8,128)(2,1)S(1)}, u32[]{:S(2)}, u32[]{:S(2)}) %collective-permute-start.5) | collective-permute-done | bytes 32800 | tf_op jit(solution)/shard_map/ppermute | solution.py:209
  20.3 0.7 %collective-permute-done.8.refs_6_ = bf16[64,256]{1,0:T(8,128)(2,1)S(1)} collective-permute-done((bf16[64,256]{1,0:T(8,128)(2,1)S(1)}, bf16[64,256]{1,0:T(8,128)(2,1)S(1)}, u32[]{:S(2)}, u32[]{:S(2)}) %collective-permute-start.8) | collective-permute-done | bytes 32800 | tf_op jit(solution)/shard_map/ppermute | solution.py:212
  21.2 1.1 %layer.1 = (bf16[128,256]{1,0:T(8,128)(2,1)}, bf16[128,256]{1,0:T(8,128)(2,1)S(1)}, bf16[96,256]{1,0:T(8,128)(2,1)S(1)}, bf16[96,256]{1,0:T(8,128)(2,1)S(1)}, bf...) custom-call(bf16[64,256]{1,0:T(8,128)(2,1)S(1)} %get-tuple-element.19.refs_0_, ...), custom_call_target="tpu_custom_call" | custom-call | tf_op jit(solution)/shard_map/layer/pallas_call | solution.py:257
  23.3 2.4 %collective-permute-start.14 = (bf16[96,256]{1,0:T(8,128)(2,1)S(1)}, bf16[96,256]{1,0:T(8,128)(2,1)S(1)}, u32[]{:S(2)}, u32[]{:S(2)}) collective-permute-start(bf16[96,256]{1,0:T(8,128)(2,1)S(1)} %get-tuple-element.30), channel_id=1, source_target_pairs={{0,24},{4,28},{8,16},{12,20},{16,8},{20,12},{24,0},{28,4},{1,25},{... | collective-permute-start | bytes 147464 | tf_op jit(solution)/shard_map/ppermute | solution.py:209
  26.4 1.1 %collective-permute-done.13.refs_4_ = bf16[96,256]{1,0:T(8,128)(2,1)S(1)} collective-permute-done((bf16[96,256]{1,0:T(8,128)(2,1)S(1)}, bf16[96,256]{1,0:T(8,128)(2,1)S(1)}, u32[]{:S(2)}, u32[]{:S(2)}) %collective-permute-start.13) | collective-permute-done | bytes 49184 | tf_op jit(solution)/shard_map/ppermute | solution.py:209
  27.4 0.9 %collective-permute-done.14.refs_5_ = bf16[96,256]{1,0:T(8,128)(2,1)S(1)} collective-permute-done((bf16[96,256]{1,0:T(8,128)(2,1)S(1)}, bf16[96,256]{1,0:T(8,128)(2,1)S(1)}, u32[]{:S(2)}, u32[]{:S(2)}) %collective-permute-start.14) | collective-permute-done | bytes 49184 | tf_op jit(solution)/shard_map/ppermute | solution.py:209
  28.6 1.1 %collective-permute-start.15 = (bf16[160,256]{1,0:T(8,128)(2,1)S(1)}, bf16[160,256]{1,0:T(8,128)(2,1)S(1)}, u32[]{:S(2)}, u32[]{:S(2)}) collective-permute-start(bf16[160,256]{1,0:T(8,128)(2,1)S(1)} %get-tuple-element.32), channel_id=1, source_target_pairs={{0,1},{1,2},{2,3},{3,0},{4,5},{5,6},{6,7},{7,4},{8,9},{9,10},{10,1... | collective-permute-start | bytes 245768 | tf_op jit(solution)/shard_map/ppermute | solution.py:293
  29.7 2.8 %collective-permute-start.16 = (bf16[160,256]{1,0:T(8,128)(2,1)S(1)}, bf16[160,256]{1,0:T(8,128)(2,1)S(1)}, u32[]{:S(2)}, u32[]{:S(2)}) collective-permute-start(bf16[160,256]{1,0:T(8,128)(2,1)S(1)} %get-tuple-element.33), channel_id=1, source_target_pairs={{0,2},{1,3},{2,0},{3,1},{4,6},{5,7},{6,4},{7,5},{8,10},{9,11},{10,... | collective-permute-start | bytes 245768 | tf_op jit(solution)/shard_map/ppermute | solution.py:293
  32.6 0.9 %collective-permute-start.17 = (bf16[160,256]{1,0:T(8,128)(2,1)S(1)}, bf16[160,256]{1,0:T(8,128)(2,1)S(1)}, u32[]{:S(2)}, u32[]{:S(2)}) collective-permute-start(bf16[160,256]{1,0:T(8,128)(2,1)S(1)} %get-tuple-element.34), channel_id=1, source_target_pairs={{0,3},{1,0},{2,1},{3,2},{4,7},{5,4},{6,5},{7,6},{8,11},{9,8},{10,9... | collective-permute-start | bytes 245768 | tf_op jit(solution)/shard_map/ppermute | solution.py:293
  33.5 1.9 %collective-permute-done.15.refs_1_.refs_0_ = bf16[160,256]{1,0:T(8,128)(2,1)S(1)} collective-permute-done((bf16[160,256]{1,0:T(8,128)(2,1)S(1)}, bf16[160,256]{1,0:T(8,128)(2,1)S(1)}, u32[]{:S(2)}, u32[]{:S(2)}) %collective-permute-start.15) | collective-permute-done | bytes 81952 | tf_op jit(solution)/shard_map/ppermute | solution.py:293
  35.4 2.4 %collective-permute-done.16.refs_2_.refs_1_ = bf16[160,256]{1,0:T(8,128)(2,1)S(1)} collective-permute-done((bf16[160,256]{1,0:T(8,128)(2,1)S(1)}, bf16[160,256]{1,0:T(8,128)(2,1)S(1)}, u32[]{:S(2)}, u32[]{:S(2)}) %collective-permute-start.16) | collective-permute-done | bytes 81952 | tf_op jit(solution)/shard_map/ppermute | solution.py:293
  37.9 2.4 %collective-permute-start.20 = (bf16[32,256]{1,0:T(8,128)(2,1)S(1)}, bf16[32,256]{1,0:T(8,128)(2,1)S(1)}, u32[]{:S(2)}, u32[]{:S(2)}) collective-permute-start(bf16[32,256]{1,0:T(8,128)(2,1)S(1)} %chunk.1.refs_0_), channel_id=1, source_target_pairs={{0,24},{4,28},{8,16},{12,20},{16,8},{20,12},{24,0},{28,4},{1,25},{... | collective-permute-start | bytes 49160 | tf_op jit(solution)/shard_map/ppermute | solution.py:209
  41.5 1.2 %collective-permute-done.20.refs_3_ = bf16[32,256]{1,0:T(8,128)(2,1)S(1)} collective-permute-done((bf16[32,256]{1,0:T(8,128)(2,1)S(1)}, bf16[32,256]{1,0:T(8,128)(2,1)S(1)}, u32[]{:S(2)}, u32[]{:S(2)}) %collective-permute-start.20) | collective-permute-done | bytes 16416 | tf_op jit(solution)/shard_map/ppermute | solution.py:209
  42.7 1.4 %collective-permute-done.19.refs_2_ = bf16[32,256]{1,0:T(8,128)(2,1)S(1)} collective-permute-done((bf16[32,256]{1,0:T(8,128)(2,1)S(1)}, bf16[32,256]{1,0:T(8,128)(2,1)S(1)}, u32[]{:S(2)}, u32[]{:S(2)}) %collective-permute-start.19) | collective-permute-done | bytes 16416 | tf_op jit(solution)/shard_map/ppermute | solution.py:209
  44.7 0.7 %grad_x.1 = bf16[128,256]{1,0:T(8,128)(2,1)} custom-call(f32[160,256]{1,0:T(8,128)S(1)} %get-tuple-element.31.refs_0_.kept_ref, bf16[160,256]{1,0:T(8,128)(2,1)S(1)} %collective-permute-done.15.refs_1_.refs_0_, bf16[160,256]{1,0:T(8,128)(2,1)S(1)} %collective-permute-done.16.refs_2_.refs_1_, bf16[160,256]{1,0:T(8,128)(2,1)S(1)} %collective-permute-done.17.refs_3_.refs_2_), custom_call_target="tpu_custom_call" | custom-call | tf_op jit(solution)/shard_map/grad_x/pallas_call | solution.py:310
  45.9 0.7 %grad_w.1 = f32[256,256]{1,0:T(8,128)} custom-call(bf16[32,256]{1,0:T(8,128)(2,1)S(1)} %chunk.1.refs_0_, bf16[32,256]{1,0:T(8,128)(2,1)S(1)} %collective-permute-done.18.refs_1_, bf16[32,256]{1,0:T(8,128)(2,1)S(1)} %collective-permute-done.19.refs_2_, bf16[32,256]{1,0:T(8,128)(2,1)S(1)} %collective-permute-done.20.refs_3_, ...), custom_call_target="tpu_custom_call" | custom-call | tf_op jit(solution)/shard_map/grad_w/pallas_call | solution.py:320
  (61 shorter events, 7.7 us)
Async XLA Ops:
  0.6 9.9 %collective-permute-start.2 = (bf16[128,256]{1,0:T(8,128)(2,1)}, bf16[128,256]{1,0:T(8,128)(2,1)S(1)}, u32[]{:S(2)}, u32[]{:S(2)}) collective-permute-start(bf16[128,256]{1,0:T(8,128)(2,1)} %refs_8_.1), channel_id=1, source_target_pairs={{0,3},{1,2},{2,1},{3,0},{4,7},{5,6},{6,5},{7,4},{8,11},{9,10},{10,... | collective-permute-start | bytes 196616 | tf_op jit(solution)/shard_map/ppermute | solution.py:201
  5.7 5.8 %collective-permute-start.1 = (bf16[128,256]{1,0:T(8,128)(2,1)}, bf16[128,256]{1,0:T(8,128)(2,1)S(1)}, u32[]{:S(2)}, u32[]{:S(2)}) collective-permute-start(bf16[128,256]{1,0:T(8,128)(2,1)} %refs_8_.1), channel_id=1, source_target_pairs={{0,2},{1,3},{2,0},{3,1},{4,6},{5,7},{6,4},{7,5},{8,10},{9,11},{10,... | collective-permute-start | bytes 196616 | tf_op jit(solution)/shard_map/ppermute | solution.py:201
  5.7 5.8 %collective-permute-start = (bf16[128,256]{1,0:T(8,128)(2,1)}, bf16[128,256]{1,0:T(8,128)(2,1)S(1)}, u32[]{:S(2)}, u32[]{:S(2)}) collective-permute-start(bf16[128,256]{1,0:T(8,128)(2,1)} %refs_8_.1), channel_id=1, source_target_pairs={{0,1},{1,0},{2,3},{3,2},{4,5},{5,4},{6,7},{7,6},{8,9},{9,8},{10,11... | collective-permute-start | bytes 196616 | tf_op jit(solution)/shard_map/ppermute | solution.py:201
  11.9 4.0 %collective-permute-start.3 = (bf16[64,256]{1,0:T(8,128)(2,1)S(1)}, bf16[64,256]{1,0:T(8,128)(2,1)S(1)}, u32[]{:S(2)}, u32[]{:S(2)}) collective-permute-start(bf16[64,256]{1,0:T(8,128)(2,1)S(1)} %get-tuple-element.20), channel_id=1, source_target_pairs={{0,8},{4,12},{8,0},{12,4},{16,24},{20,28},{24,16},{28,20},{1,9},{5... | collective-permute-start | bytes 98312 | tf_op jit(solution)/shard_map/ppermute | solution.py:209
  13.4 6.3 %collective-permute-start.6 = (bf16[64,256]{1,0:T(8,128)(2,1)S(1)}, bf16[64,256]{1,0:T(8,128)(2,1)S(1)}, u32[]{:S(2)}, u32[]{:S(2)}) collective-permute-start(bf16[64,256]{1,0:T(8,128)(2,1)S(1)} %get-tuple-element.19.refs_0_), channel_id=1, source_target_pairs={{0,4},{4,0},{8,12},{12,8},{16,20},{20,16},{24,28},{28,24},{1,5},{5... | collective-permute-start | bytes 98312 | tf_op jit(solution)/shard_map/ppermute | solution.py:212
  13.4 3.9 %collective-permute-start.4 = (bf16[64,256]{1,0:T(8,128)(2,1)S(1)}, bf16[64,256]{1,0:T(8,128)(2,1)S(1)}, u32[]{:S(2)}, u32[]{:S(2)}) collective-permute-start(bf16[64,256]{1,0:T(8,128)(2,1)S(1)} %get-tuple-element.21), channel_id=1, source_target_pairs={{0,16},{4,20},{8,24},{12,28},{16,0},{20,4},{24,8},{28,12},{1,17},{... | collective-permute-start | bytes 98312 | tf_op jit(solution)/shard_map/ppermute | solution.py:209
  15.0 4.8 %collective-permute-start.5 = (bf16[64,256]{1,0:T(8,128)(2,1)S(1)}, bf16[64,256]{1,0:T(8,128)(2,1)S(1)}, u32[]{:S(2)}, u32[]{:S(2)}) collective-permute-start(bf16[64,256]{1,0:T(8,128)(2,1)S(1)} %get-tuple-element.22), channel_id=1, source_target_pairs={{0,24},{4,28},{8,16},{12,20},{16,8},{20,12},{24,0},{28,4},{1,25},{... | collective-permute-start | bytes 98312 | tf_op jit(solution)/shard_map/ppermute | solution.py:209
  15.4 5.7 %collective-permute-start.10 = (bf16[128,256]{1,0:T(8,128)(2,1)S(1)}, bf16[128,256]{1,0:T(8,128)(2,1)S(1)}, u32[]{:S(2)}, u32[]{:S(2)}) collective-permute-start(bf16[128,256]{1,0:T(8,128)(2,1)S(1)} %copy-done.1), channel_id=1, source_target_pairs={{0,4},{4,0},{8,12},{12,8},{16,20},{20,16},{24,28},{28,24},{1,5},{5... | collective-permute-start | bytes 196616 | tf_op jit(solution)/shard_map/ppermute | solution.py:212
  15.9 5.3 %collective-permute-start.11 = (bf16[128,256]{1,0:T(8,128)(2,1)S(1)}, bf16[128,256]{1,0:T(8,128)(2,1)S(1)}, u32[]{:S(2)}, u32[]{:S(2)}) collective-permute-start(bf16[128,256]{1,0:T(8,128)(2,1)S(1)} %copy-done.3), channel_id=1, source_target_pairs={{0,4},{4,0},{8,12},{12,8},{16,20},{20,16},{24,28},{28,24},{1,5},{5... | collective-permute-start | bytes 196616 | tf_op jit(solution)/shard_map/ppermute | solution.py:212
  17.3 2.9 %collective-permute-start.7 = (bf16[64,256]{1,0:T(8,128)(2,1)S(1)}, bf16[64,256]{1,0:T(8,128)(2,1)S(1)}, u32[]{:S(2)}, u32[]{:S(2)}) collective-permute-start(bf16[64,256]{1,0:T(8,128)(2,1)S(1)} %collective-permute-done.3.refs_1_), channel_id=1, source_target_pairs={{0,4},{4,0},{8,12},{12,8},{16,20},{20,16},{24,28},{28,24},{1,5},{5... | collective-permute-start | bytes 98312 | tf_op jit(solution)/shard_map/ppermute | solution.py:212
  19.8 1.2 %collective-permute-start.8 = (bf16[64,256]{1,0:T(8,128)(2,1)S(1)}, bf16[64,256]{1,0:T(8,128)(2,1)S(1)}, u32[]{:S(2)}, u32[]{:S(2)}) collective-permute-start(bf16[64,256]{1,0:T(8,128)(2,1)S(1)} %collective-permute-done.4.refs_2_), channel_id=1, source_target_pairs={{0,4},{4,0},{8,12},{12,8},{16,20},{20,16},{24,28},{28,24},{1,5},{5... | collective-permute-start | bytes 98312 | tf_op jit(solution)/shard_map/ppermute | solution.py:212
  19.8 1.4 %collective-permute-start.9 = (bf16[64,256]{1,0:T(8,128)(2,1)S(1)}, bf16[64,256]{1,0:T(8,128)(2,1)S(1)}, u32[]{:S(2)}, u32[]{:S(2)}) collective-permute-start(bf16[64,256]{1,0:T(8,128)(2,1)S(1)} %collective-permute-done.5.refs_3_), channel_id=1, source_target_pairs={{0,4},{4,0},{8,12},{12,8},{16,20},{20,16},{24,28},{28,24},{1,5},{5... | collective-permute-start | bytes 98312 | tf_op jit(solution)/shard_map/ppermute | solution.py:212
  22.3 4.1 %collective-permute-start.12 = (bf16[96,256]{1,0:T(8,128)(2,1)S(1)}, bf16[96,256]{1,0:T(8,128)(2,1)S(1)}, u32[]{:S(2)}, u32[]{:S(2)}) collective-permute-start(bf16[96,256]{1,0:T(8,128)(2,1)S(1)} %get-tuple-element.28), channel_id=1, source_target_pairs={{0,8},{4,12},{8,0},{12,4},{16,24},{20,28},{24,16},{28,20},{1,9},{5... | collective-permute-start | bytes 147464 | tf_op jit(solution)/shard_map/ppermute | solution.py:209
  22.8 4.6 %collective-permute-start.13 = (bf16[96,256]{1,0:T(8,128)(2,1)S(1)}, bf16[96,256]{1,0:T(8,128)(2,1)S(1)}, u32[]{:S(2)}, u32[]{:S(2)}) collective-permute-start(bf16[96,256]{1,0:T(8,128)(2,1)S(1)} %get-tuple-element.29), channel_id=1, source_target_pairs={{0,16},{4,20},{8,24},{12,28},{16,0},{20,4},{24,8},{28,12},{1,17},{... | collective-permute-start | bytes 147464 | tf_op jit(solution)/shard_map/ppermute | solution.py:209
  23.3 5.0 %collective-permute-start.14 = (bf16[96,256]{1,0:T(8,128)(2,1)S(1)}, bf16[96,256]{1,0:T(8,128)(2,1)S(1)}, u32[]{:S(2)}, u32[]{:S(2)}) collective-permute-start(bf16[96,256]{1,0:T(8,128)(2,1)S(1)} %get-tuple-element.30), channel_id=1, source_target_pairs={{0,24},{4,28},{8,16},{12,20},{16,8},{20,12},{24,0},{28,4},{1,25},{... | collective-permute-start | bytes 147464 | tf_op jit(solution)/shard_map/ppermute | solution.py:209
  28.6 6.8 %collective-permute-start.15 = (bf16[160,256]{1,0:T(8,128)(2,1)S(1)}, bf16[160,256]{1,0:T(8,128)(2,1)S(1)}, u32[]{:S(2)}, u32[]{:S(2)}) collective-permute-start(bf16[160,256]{1,0:T(8,128)(2,1)S(1)} %get-tuple-element.32), channel_id=1, source_target_pairs={{0,1},{1,2},{2,3},{3,0},{4,5},{5,6},{6,7},{7,4},{8,9},{9,10},{10,1... | collective-permute-start | bytes 245768 | tf_op jit(solution)/shard_map/ppermute | solution.py:293
  29.7 8.0 %collective-permute-start.16 = (bf16[160,256]{1,0:T(8,128)(2,1)S(1)}, bf16[160,256]{1,0:T(8,128)(2,1)S(1)}, u32[]{:S(2)}, u32[]{:S(2)}) collective-permute-start(bf16[160,256]{1,0:T(8,128)(2,1)S(1)} %get-tuple-element.33), channel_id=1, source_target_pairs={{0,2},{1,3},{2,0},{3,1},{4,6},{5,7},{6,4},{7,5},{8,10},{9,11},{10,... | collective-permute-start | bytes 245768 | tf_op jit(solution)/shard_map/ppermute | solution.py:293
  32.6 5.3 %collective-permute-start.17 = (bf16[160,256]{1,0:T(8,128)(2,1)S(1)}, bf16[160,256]{1,0:T(8,128)(2,1)S(1)}, u32[]{:S(2)}, u32[]{:S(2)}) collective-permute-start(bf16[160,256]{1,0:T(8,128)(2,1)S(1)} %get-tuple-element.34), channel_id=1, source_target_pairs={{0,3},{1,0},{2,1},{3,2},{4,7},{5,4},{6,5},{7,6},{8,11},{9,8},{10,9... | collective-permute-start | bytes 245768 | tf_op jit(solution)/shard_map/ppermute | solution.py:293
  37.9 4.8 %collective-permute-start.20 = (bf16[32,256]{1,0:T(8,128)(2,1)S(1)}, bf16[32,256]{1,0:T(8,128)(2,1)S(1)}, u32[]{:S(2)}, u32[]{:S(2)}) collective-permute-start(bf16[32,256]{1,0:T(8,128)(2,1)S(1)} %chunk.1.refs_0_), channel_id=1, source_target_pairs={{0,24},{4,28},{8,16},{12,20},{16,8},{20,12},{24,0},{28,4},{1,25},{... | collective-permute-start | bytes 49160 | tf_op jit(solution)/shard_map/ppermute | solution.py:209
  40.3 3.7 %collective-permute-start.19 = (bf16[32,256]{1,0:T(8,128)(2,1)S(1)}, bf16[32,256]{1,0:T(8,128)(2,1)S(1)}, u32[]{:S(2)}, u32[]{:S(2)}) collective-permute-start(bf16[32,256]{1,0:T(8,128)(2,1)S(1)} %chunk.1.refs_0_), channel_id=1, source_target_pairs={{0,16},{4,20},{8,24},{12,28},{16,0},{20,4},{24,8},{28,12},{1,17},{... | collective-permute-start | bytes 49160 | tf_op jit(solution)/shard_map/ppermute | solution.py:209
  41.0 3.7 %collective-permute-start.18 = (bf16[32,256]{1,0:T(8,128)(2,1)S(1)}, bf16[32,256]{1,0:T(8,128)(2,1)S(1)}, u32[]{:S(2)}, u32[]{:S(2)}) collective-permute-start(bf16[32,256]{1,0:T(8,128)(2,1)S(1)} %chunk.1.refs_0_), channel_id=1, source_target_pairs={{0,8},{4,12},{8,0},{12,4},{16,24},{20,28},{24,16},{28,20},{1,9},{5... | collective-permute-start | bytes 49160 | tf_op jit(solution)/shard_map/ppermute | solution.py:209
  41.5 3.9 %collective-permute-start.21 = (bf16[32,256]{1,0:T(8,128)(2,1)S(1)}, bf16[32,256]{1,0:T(8,128)(2,1)S(1)}, u32[]{:S(2)}, u32[]{:S(2)}) collective-permute-start(bf16[32,256]{1,0:T(8,128)(2,1)S(1)} %chunk.1.refs_0_), channel_id=1, source_target_pairs={{0,4},{4,0},{8,12},{12,8},{16,20},{20,16},{24,28},{28,24},{1,5},{5... | collective-permute-start | bytes 49160 | tf_op jit(solution)/shard_map/ppermute | solution.py:212
  42.7 2.6 %collective-permute-start.24 = (bf16[32,256]{1,0:T(8,128)(2,1)S(1)}, bf16[32,256]{1,0:T(8,128)(2,1)S(1)}, u32[]{:S(2)}, u32[]{:S(2)}) collective-permute-start(bf16[32,256]{1,0:T(8,128)(2,1)S(1)} %collective-permute-done.20.refs_3_), channel_id=1, source_target_pairs={{0,4},{4,0},{8,12},{12,8},{16,20},{20,16},{24,28},{28,24},{1,5},{5... | collective-permute-start | bytes 49160 | tf_op jit(solution)/shard_map/ppermute | solution.py:212
  44.1 1.3 %collective-permute-start.23 = (bf16[32,256]{1,0:T(8,128)(2,1)S(1)}, bf16[32,256]{1,0:T(8,128)(2,1)S(1)}, u32[]{:S(2)}, u32[]{:S(2)}) collective-permute-start(bf16[32,256]{1,0:T(8,128)(2,1)S(1)} %collective-permute-done.19.refs_2_), channel_id=1, source_target_pairs={{0,4},{4,0},{8,12},{12,8},{16,20},{20,16},{24,28},{28,24},{1,5},{5... | collective-permute-start | bytes 49160 | tf_op jit(solution)/shard_map/ppermute | solution.py:212
  (7 other events, 21.0 us)

commit v4 on v3

v4 whole, which is shorter than its diff:
```python
import math

import jax
import jax.numpy as jnp
from jax import lax
from jax.experimental import pallas as pl
from jax.experimental.pallas import tpu as pltpu
from jax.sharding import PartitionSpec as P

BF16 = jnp.bfloat16
F32 = jnp.float32
PAD = 32
LANES = 128
PAIR = 2


def whole(count):
    return [pl.BlockSpec(memory_space=pltpu.VMEM)] * count


def params(slots):
    return pltpu.CompilerParams(vmem_limit_bytes=(4 << 20) + (16 << 10) * slots)


def dot(a, b, contract_a, contract_b):
    return lax.dot_general(
        a, b, (((contract_a,), (contract_b,)), ((), ())), preferred_element_type=F32
    )


LOW, HIGH, BOTH = (1, 0, 3, 2), (2, 3, 0, 1), (3, 2, 1, 0)
PLAN = dict(
    A=(LOW, BOTH, HIGH), B=(BOTH, LOW, HIGH), C=(LOW, HIGH, BOTH), D=(HIGH, LOW, BOTH)
)


def targets(name, step, count):
    if step == 0:
        return tuple(range(count))
    if count == len(PLAN[name]) + 1:
        return PLAN[name][step - 1]
    return tuple((i + step) % count for i in range(count))


def entry(table, index):
    found = table[0]
    for i in range(1, len(table)):
        found = jnp.where(index == i, table[i], found)
    return found


def target_of(name, index, step, count):
    return entry(targets(name, step, count), index)


def origin_of(name, index, step, count):
    sent = targets(name, step, count)
    return entry(tuple(sent.index(i) for i in range(count)), index)


def step_to(name, index, other, count):
    found = jnp.zeros_like(other)
    for step in range(1, count):
        found = jnp.where(target_of(name, index, step, count) == other, step, found)
    return found


def asked_at(step, count):
    back = targets("C", step, count)
    for at in range(count):
        there = targets("B", at, count)
        if all(there[back[i]] == i for i in range(count)):
            return at
    raise ValueError("B and C differ")


def inputs_kernel(
    chips, source_ref, target_ref, features_ref, tiles_ref, picked_ref, base_ref, held, named_ref, sems
):
    cols, per_col, block = held.shape[:3]
    copies = [pltpu.make_async_copy(tiles_ref.at[b], held.at[b], sems.at[b]) for b in range(cols)]
    for copy in copies:
        copy.start()
    peers, slot_count = source_ref.shape
    slots, width = base_ref.shape
    wide = width // PAD
    chip = lax.div(lax.axis_index("rows"), PAIR)
    target = target_ref[...]
    named_ref[...] = jnp.full(named_ref.shape, -1, jnp.int32)
    named_ref[:, :slot_count] = jnp.where(target < features_ref.shape[0], source_ref[...], -1)
    spread = jnp.broadcast_to(named_ref[...][:, None, :], (peers, PAD, LANES)).reshape(slots, LANES)
    slot = lax.rem(lax.broadcasted_iota(jnp.int32, (slots, LANES), 0), PAD)
    lane = lax.broadcasted_iota(jnp.int32, (slots, LANES), 1)
    column = jnp.sum(jnp.where(lane == slot, spread, 0).astype(F32), axis=1, keepdims=True)
    offset = jnp.broadcast_to(column, (slots, LANES)) - lane.astype(F32)

    named_ref[...] = jnp.zeros(named_ref.shape, jnp.int32)
    named_ref[:, :slot_count] = target
    notes = named_ref[...]
    tiled = notes
    for turn in range(1, LANES // PAD):
        tiled += pltpu.roll(notes, turn * PAD, 1)
    tiled = jnp.concatenate([tiled] * (width // LANES), axis=1)
    tiled = jnp.broadcast_to(tiled[:, None, :], (peers, PAD, width)).reshape(slots, width)
    row = lax.broadcasted_iota(jnp.int32, (slots, width), 0)
    spot = lax.div(lax.broadcasted_iota(jnp.int32, (slots, width), 1), PAD)
    at = step_to("B", chip, lax.div(row, PAD * PAIR), chips)
    keep = jnp.zeros((slots, width), jnp.bool_)
    for mate in range(PAIR):
        here = lax.rem(row, PAD) == slot_count + mate
        keep = keep | (here & (lax.rem(mate * chips + at, wide) == spot))
    landing = jnp.where(keep, tiled, 0).astype(F32)

    for b in range(cols):
        first = b * per_col
        hot = jnp.concatenate(
            [
                jnp.where(offset == float((first + k) * block), 1.0, 0.0).astype(BF16)
                for k in range(per_col)
            ],
            axis=1,
        )
        copies[b].wait()
        rows = held[b].reshape(per_col * block, block)
        picked_ref[b] = dot(hot, rows, 1, 0).astype(BF16)
    base_ref[...] = landing + dot(picked_ref[lax.axis_index("rep")], features_ref[...], 1, 0)


def partial_kernel(reps, chips, picked_ref, base_ref, *refs):
    features, sends, total_ref = refs[: reps - 1], refs[reps - 1 : -1], refs[-1]
    rep = lax.axis_index("rep")
    chip = lax.div(lax.axis_index("rows"), PAIR)
    depth = PAIR * PAD
    total = base_ref[...]
    for step in range(1, reps):
        total += dot(picked_ref[origin_of("A", rep, step, reps)], features[step - 1][...], 1, 0)
    total_ref[...] = total
    for step in range(chips):
        first = pl.multiple_of(target_of("B", chip, step, chips) * depth, depth)
        sends[step][...] = total_ref[pl.ds(first, depth), :].astype(BF16)


def layer_kernel(chips, slot_count, *refs):
    got, refs = refs[: PAIR * chips], refs[PAIR * chips :]
    features_ref, mate_features_ref, cotangent_ref, mate_cotangent_ref, weight_ref = refs[:5]
    output_ref, back_ref, *sends, grad_ref = refs[5:]
    rows, width = features_ref.shape
    wide = width // PAD
    core = lax.rem(lax.axis_index("rows"), PAIR)
    groups = pl.cdiv(PAIR * chips, wide)
    row = lax.broadcasted_iota(jnp.int32, (rows, width), 0)
    lane = lax.broadcasted_iota(jnp.int32, (rows, width), 1)
    valid = lax.rem(lane, PAD) < slot_count
    weight = weight_ref[...]
    hots, aggregates = [], []
    for half, own in ((core, features_ref), (1 - core, mate_features_ref)):
        first = pl.multiple_of(half * PAD, PAD)
        blocks = [ref[pl.ds(first, PAD), :] for ref in got]
        notes = [jnp.zeros((1, width), F32)] * groups
        for at, block in enumerate(blocks):
            mate = at // chips
            notes[at // wide] += block[16:].astype(F32)[slot_count - 16 + mate :][:1]
        parts = [
            jnp.where(valid & (note.astype(jnp.int32) == row), 1.0, 0.0).astype(BF16)
            for note in notes
        ]
        hot = parts[0] if groups == 1 else jnp.concatenate(parts, axis=1)
        hot = hot[:, : PAIR * chips * PAD]
        arrived = dot(hot, jnp.concatenate(blocks, axis=0), 1, 0)
        hots.append(hot[:, : chips * PAD])
        aggregates.append((own[...].astype(F32) + arrived).astype(BF16))
    aggregated = jnp.concatenate(aggregates, axis=0)
    preact = dot(aggregated, weight, 1, 0)
    sigmoid = jax.nn.sigmoid(preact)
    output_ref[...] = (preact * sigmoid)[:rows].astype(BF16)
    cotangent = jnp.concatenate([cotangent_ref[...], mate_cotangent_ref[...]], axis=0)
    pre_grad = (cotangent.astype(F32) * sigmoid * (1.0 + preact * (1.0 - sigmoid))).astype(BF16)
    back_in = dot(pre_grad, weight, 1, 1).astype(BF16)
    back_ref[...] = back_in[:rows]
    grad_ref[...] = dot(aggregated, pre_grad, 0, 0)
    part = width // PAIR
    grad = grad_ref[pl.ds(pl.multiple_of(core * part, part), part), :].astype(BF16)
    asked = [dot(hot, back_in[h * rows : (h + 1) * rows], 0, 0) for h, hot in enumerate(hots)]
    for step in range(chips):
        first = asked_at(step, chips) * PAD
        from_own, from_mate = (part[first : first + PAD].astype(BF16) for part in asked)
        sends[step][pl.ds(pl.multiple_of(core * PAD, PAD), PAD), :] = from_own
        sends[step][pl.ds(pl.multiple_of((1 - core) * PAD, PAD), PAD), :] = from_mate
        sends[step][PAIR * PAD :, :] = grad


def terms_kernel(reps, chips, picked_ref, back_ref, *refs):
    returned, kept_ref, sends = refs[:chips], refs[chips], refs[chips + 1 : -2]
    rows_ref, parts_ref = refs[-2:]
    rep = lax.axis_index("rep")
    chip = lax.div(lax.axis_index("rows"), PAIR)
    depth = PAIR * PAD
    for step in range(chips):
        origin = origin_of("C", chip, step, chips)
        rows_ref[pl.ds(pl.multiple_of(origin * depth, depth), depth), :] = returned[step][:depth, :]
        parts_ref[origin] = returned[step][depth:, :].astype(F32)
    part = parts_ref[0]
    for other in range(1, chips):
        part += parts_ref[other]
    rows = rows_ref[...]
    for step in range(1, reps):
        term = dot(picked_ref[target_of("D", rep, step, reps)], rows, 0, 0)
        sends[step - 1][...] = jnp.concatenate([term, part], axis=0).astype(BF16)
    own = dot(picked_ref[rep], rows, 0, 0) + back_ref[...].astype(F32)
    kept_ref[...] = jnp.concatenate([own, part], axis=0)


def chunk_kernel(reps, kept_ref, *refs):
    got, (chunk_ref, parts_ref) = refs[: reps - 1], refs[reps - 1 :]
    depth = chunk_ref.shape[0]
    rows = kept_ref.shape[0] - depth
    rep = lax.axis_index("rep")
    parts_ref[rep] = kept_ref[rows:, :].astype(BF16).astype(F32)
    for step in range(1, reps):
        parts_ref[origin_of("D", rep, step, reps)] = got[step - 1][rows:, :].astype(F32)
    chunk = parts_ref[0]
    for other in range(1, reps):
        chunk += parts_ref[other]
    chunk_ref[...] = chunk.astype(BF16)


def grad_x_kernel(kept_ref, *refs):
    got, grad_x_ref = refs[:-1], refs[-1]
    rows = grad_x_ref.shape[0]
    total = kept_ref[:rows, :]
    for ref in got:
        total += ref[:rows, :].astype(F32)
    grad_x_ref[...] = total.astype(BF16)


def grad_w_kernel(scale, own_ref, mate_ref, grad_w_ref):
    part = own_ref.shape[0]
    core = lax.rem(lax.axis_index("rows"), PAIR)
    for half, ref in ((core, own_ref), (1 - core, mate_ref)):
        first = pl.multiple_of(half * part, part)
        grad_w_ref[pl.ds(first, part), :] = ref[...].astype(F32) * scale


def local(features, weight, tiles, send_src, send_dst, cotangent):
    blocks = tiles[0, 0]
    source = send_src[0, 0]
    target = send_dst[0, 0]
    peers, slot_count = target.shape
    rows, width = features.shape
    cols, per_col, block = blocks.shape[:3]
    reps = lax.axis_size("rep")
    chips = peers // PAIR
    slots = peers * PAD
    chunk = width // PAIR

    def over_rep(name, value, step):
        return lax.ppermute(value, "rep", list(enumerate(targets(name, step, reps))))

    def over_chips(name, value, step):
        pairs = [
            (i * PAIR + core, to * PAIR + core)
            for i, to in enumerate(targets(name, step, chips))
            for core in range(PAIR)
        ]
        return lax.ppermute(value, "rows", pairs)

    def to_mate(value):
        return lax.ppermute(value, "rows", [(i, i ^ 1) for i in range(peers)])

    gathered = [over_rep("A", features, step) for step in range(1, reps)]

    picked, base = pl.pallas_call(
        lambda *refs: inputs_kernel(chips, *refs),
        out_shape=(
            jax.ShapeDtypeStruct((cols, slots, block), BF16),
            jax.ShapeDtypeStruct((slots, width), F32),
        ),
        in_specs=whole(3) + [pl.BlockSpec(memory_space=pl.ANY)],
        out_specs=tuple(whole(2)),
        scratch_shapes=[
            pltpu.VMEM((cols, per_col, block, block), BF16),
            pltpu.VMEM((peers, LANES), jnp.int32),
            pltpu.SemaphoreType.DMA((cols,)),
        ],
        compiler_params=params(slots),
        name="inputs",
    )(source, target, features, blocks)

    message = jax.ShapeDtypeStruct((PAIR * PAD, width), BF16)
    outgoing = pl.pallas_call(
        lambda *refs: partial_kernel(reps, chips, *refs),
        out_shape=(message,) * chips,
        in_specs=whole(1 + reps),
        out_specs=tuple(whole(chips)),
        scratch_shapes=[pltpu.VMEM((slots, width), F32)],
        compiler_params=params(slots),
        name="partial",
    )(picked, base, *gathered)

    direct = [outgoing[0]] + [over_chips("B", outgoing[step], step) for step in range(1, chips)]
    shared = [to_mate(value) for value in direct]
    early_features, early_cotangent, _ = lax.optimization_barrier(
        (features, cotangent, outgoing[0])
    )

    output, back_in, *requested = pl.pallas_call(
        lambda *refs: layer_kernel(chips, slot_count, *refs),
        out_shape=(
            jax.ShapeDtypeStruct((rows, width), BF16),
            jax.ShapeDtypeStruct((rows, width), BF16),
        )
        + (jax.ShapeDtypeStruct((PAIR * PAD + chunk, width), BF16),) * chips,
        in_specs=whole(PAIR * chips + 5),
        out_specs=tuple(whole(2 + chips)),
        scratch_shapes=[pltpu.VMEM((width, width), F32)],
        compiler_params=params(slots),
        name="layer",
    )(
        *direct,
        *shared,
        features,
        to_mate(early_features),
        cotangent,
        to_mate(early_cotangent),
        weight,
    )

    returned = [requested[0]] + [over_chips("C", requested[step], step) for step in range(1, chips)]

    kept, *sends = pl.pallas_call(
        lambda *refs: terms_kernel(reps, chips, *refs),
        out_shape=(jax.ShapeDtypeStruct((rows + chunk, width), F32),)
        + (jax.ShapeDtypeStruct((rows + chunk, width), BF16),) * (reps - 1),
        in_specs=whole(2 + chips),
        out_specs=tuple(whole(reps)),
        scratch_shapes=[
            pltpu.VMEM((slots, width), BF16),
            pltpu.VMEM((chips, chunk, width), F32),
        ],
        compiler_params=params(slots),
        name="terms",
    )(picked, back_in, *returned)

    arrived = [over_rep("D", sends[step - 1], step) for step in range(1, reps)]

    share = pl.pallas_call(
        lambda *refs: chunk_kernel(reps, *refs),
        out_shape=jax.ShapeDtypeStruct((chunk, width), BF16),
        in_specs=whole(reps),
        out_specs=whole(1)[0],
        scratch_shapes=[pltpu.VMEM((reps, chunk, width), F32)],
        compiler_params=params(slots),
        name="chunk",
    )(kept, *arrived)

    grad_x = pl.pallas_call(
        grad_x_kernel,
        out_shape=jax.ShapeDtypeStruct((rows, width), BF16),
        in_specs=whole(reps),
        out_specs=whole(1)[0],
        compiler_params=params(slots),
        name="grad_x",
    )(kept, *arrived)

    node_count = rows * lax.axis_size("rows") * reps
    grad_w = pl.pallas_call(
        lambda *refs: grad_w_kernel(1.0 / math.sqrt(node_count), *refs),
        out_shape=jax.ShapeDtypeStruct((width, width), F32),
        in_specs=whole(2),
        out_specs=whole(1)[0],
        compiler_params=params(slots),
        name="grad_w",
    )(share, to_mate(share))
    return (output, grad_w, grad_x)


def solution(mesh):
    placed = (
        P(("rows", "rep"), None),
        P(),
        P("rows", "rep", None, None, None, None),
        P("rows", "rep", None, None),
        P("rows", "rep", None, None),
        P(("rows", "rep"), None),
    )
    return jax.shard_map(
        local,
        mesh=mesh,
        in_specs=placed,
        out_specs=(P(("rows", "rep"), None), P(), P(("rows", "rep"), None)),
        check_vma=False,
    )
```

time: 46.8 us -> 43.5 us (0.929)
  starting transfers between devices: 21.9 us -> 17.8 us
  local copies, waits for them, and re-layouts: 2.28 us -> 2.77 us
    ppermute x9 -> x6, starting transfers between devices: 10.6 us -> 7.04 us  [over_chips(): return lax.ppermute(value, 'rows', pairs)]
    ppermute x6, waiting for transfers between devices: 5.47 us -> 7.48 us  [over_rep(): lax.ppermute(value, 'rep', list(enumerate(targets(name, step, reps))))]
    ppermute x9 -> x6, waiting for transfers between devices: 9.97 us -> 8.28 us  [over_chips(): return lax.ppermute(value, 'rows', pairs)]
    unnamed x12 -> x14, local copies, waits for them, and re-layouts: 1.92 us -> 2.77 us
    ppermute x6, starting transfers between devices: 10.6 us -> 10.1 us  [over_rep(): lax.ppermute(value, 'rep', list(enumerate(targets(name, step, reps))))]
    ppermute x10 -> x7, waiting for transfers between devices: 1.38 us -> 1.44 us  [to_mate(): return lax.ppermute(value, 'rows', [(i, i ^ 1) for i in range(peers)])]
  transfers between devices with their start and end apart: 25 -> 19, of which waited for: 16 -> 12; matrix products, arithmetic and copies ran while one was open for 1% -> 0% of each run, Pallas kernels for 5% -> 5%
where the time goes in v4:
time: 43.5 us; the launch traced here: 43.1 us
  starting transfers between devices  17.8 us (41%)
  waiting for transfers between devices  17.2 us (40%)
  Pallas kernels  4.64 us (11%)
  local copies, waits for them, and re-layouts  2.77 us (6%)
  between operations  0.72 us (2%)
    ppermute x6, starting transfers between devices, over_rep(): lax.ppermute(value, 'rep', list(enumerate(targets(name, step, reps))))  10.1 us
    ppermute x6, waiting for transfers between devices, over_chips(): return lax.ppermute(value, 'rows', pairs)  8.28 us
    ppermute x6, waiting for transfers between devices, over_rep(): lax.ppermute(value, 'rep', list(enumerate(targets(name, step, reps))))  7.48 us
    ppermute x6, starting transfers between devices, over_chips(): return lax.ppermute(value, 'rows', pairs)  7.04 us
    unnamed x14, local copies, waits for them, and re-layouts  2.77 us
    pallas_call x1, Pallas kernels, local(): pl.pallas_call(lambda *refs: inputs_kernel(chips, *refs), out_shape=(jax....  1.56 us
    ppermute x7, waiting for transfers between devices, to_mate(): return lax.ppermute(value, 'rows', [(i, i ^ 1) for i in range(peers)])  1.44 us
    pallas_call x1, Pallas kernels, local(): pl.pallas_call(lambda *refs: layer_kernel(chips, slot_count, *refs), out_...  1.01 us
  transfers between devices with their start and end apart: 19, of which 12 were waited for; matrix products, arithmetic and copies ran while one was open for 0% of the time, Pallas kernels for 5%

profile of v4, /device:TPU:0, one launch (start us, length us, event | category | flops | bytes accessed | tf_op | source)
XLA Modules:
  0.0 43.1 jit_solution(3359051103670269941)
XLA Ops:
  0.6 4.1 %collective-permute-start.2 = (bf16[128,256]{1,0:T(8,128)(2,1)}, bf16[128,256]{1,0:T(8,128)(2,1)S(1)}, u32[]{:S(2)}, u32[]{:S(2)}) collective-permute-start(bf16[128,256]{1,0:T(8,128)(2,1)} %refs_8_.1), channel_id=1, source_target_pairs={{0,2},{1,3},{2,0},{3,1},{4,6},{5,7},{6,4},{7,5},{8,10},{9,11},{10,... | collective-permute-start | bytes 196616 | tf_op jit(solution)/shard_map/ppermute | solution.py:257
  4.7 1.3 %collective-permute-start.1 = (bf16[128,256]{1,0:T(8,128)(2,1)}, bf16[128,256]{1,0:T(8,128)(2,1)S(1)}, u32[]{:S(2)}, u32[]{:S(2)}) collective-permute-start(bf16[128,256]{1,0:T(8,128)(2,1)} %refs_8_.1), channel_id=1, source_target_pairs={{0,3},{1,2},{2,1},{3,0},{4,7},{5,6},{6,5},{7,4},{8,11},{9,10},{10,... | collective-permute-start | bytes 196616 | tf_op jit(solution)/shard_map/ppermute | solution.py:257
  6.3 1.2 %copy-done = bf16[1,1,4,8,128,128]{5,4,3,2,1,0:T(8,128)(2,1)S(1)} copy-done((bf16[1,1,4,8,128,128]{5,4,3,2,1,0:T(8,128)(2,1)S(1)}, bf16[1,1,4,8,128,128]{5,4,3,2,1,0:T(8,128)(2,1)}, u32[]{:S(2)}) %copy-start) | copy-done | bytes 1048600
  7.6 0.8 %copy-done.1 = bf16[128,256]{1,0:T(8,128)(2,1)S(1)} copy-done((bf16[128,256]{1,0:T(8,128)(2,1)S(1)}, bf16[128,256]{1,0:T(8,128)(2,1)}, u32[]{:S(2)}) %copy-start.1) | copy-done | bytes 65560
  8.4 0.7 %copy-done.6 = s32[1,1,8,24]{3,2,1,0:T(8,128)S(1)} copy-done((s32[1,1,8,24]{3,2,1,0:T(8,128)S(1)}, s32[1,1,8,24]{3,2,1,0:T(8,128)}, u32[]{:S(2)}) %copy-start.6) | copy-done | bytes 792
  9.1 1.6 %inputs.1 = (bf16[4,256,128]{2,1,0:T(8,128)(2,1)S(1)}, f32[256,256]{1,0:T(8,128)S(1)}) custom-call(s32[8,24]{1,0:T(8,128)S(1)} %bitcast.4, s32[8,24]{1,0:T(8,128)S(1)} %bitcast.5, bf16[128,256]{1,0:T(8,128)(2,1)S(1)} %copy-done.1, bf16[4,8,128,128]{3,2,1,0:T(8,128)(2,1)S(1)} %bitcast.3), custom_call_target="tpu_custom_call" | custom-call | tf_op jit(solution)/shard_map/inputs/pallas_call | solution.py:272
  11.6 2.5 %collective-permute-start.3 = (bf16[64,256]{1,0:T(8,128)(2,1)S(1)}, bf16[64,256]{1,0:T(8,128)(2,1)S(1)}, u32[]{:S(2)}, u32[]{:S(2)}) collective-permute-start(bf16[64,256]{1,0:T(8,128)(2,1)S(1)} %get-tuple-element.24), channel_id=1, source_target_pairs={{0,24},{4,28},{8,16},{12,20},{16,8},{20,12},{24,0},{28,4},{1,25},{... | collective-permute-start | bytes 98312 | tf_op jit(solution)/shard_map/ppermute | solution.py:265
  14.1 0.5 %collective-permute-start.4 = (bf16[64,256]{1,0:T(8,128)(2,1)S(1)}, bf16[64,256]{1,0:T(8,128)(2,1)S(1)}, u32[]{:S(2)}, u32[]{:S(2)}) collective-permute-start(bf16[64,256]{1,0:T(8,128)(2,1)S(1)} %get-tuple-element.25), channel_id=1, source_target_pairs={{0,8},{4,12},{8,0},{12,4},{16,24},{20,28},{24,16},{28,20},{1,9},{5... | collective-permute-start | bytes 98312 | tf_op jit(solution)/shard_map/ppermute | solution.py:265
  15.1 1.3 %collective-permute-done.3.refs_1_ = bf16[64,256]{1,0:T(8,128)(2,1)S(1)} collective-permute-done((bf16[64,256]{1,0:T(8,128)(2,1)S(1)}, bf16[64,256]{1,0:T(8,128)(2,1)S(1)}, u32[]{:S(2)}, u32[]{:S(2)}) %collective-permute-start.3) | collective-permute-done | bytes 32800 | tf_op jit(solution)/shard_map/ppermute | solution.py:265
  16.4 1.6 %collective-permute-done.4.refs_2_ = bf16[64,256]{1,0:T(8,128)(2,1)S(1)} collective-permute-done((bf16[64,256]{1,0:T(8,128)(2,1)S(1)}, bf16[64,256]{1,0:T(8,128)(2,1)S(1)}, u32[]{:S(2)}, u32[]{:S(2)}) %collective-permute-start.4) | collective-permute-done | bytes 32800 | tf_op jit(solution)/shard_map/ppermute | solution.py:265
  18.0 0.5 %collective-permute-done.5.refs_3_ = bf16[64,256]{1,0:T(8,128)(2,1)S(1)} collective-permute-done((bf16[64,256]{1,0:T(8,128)(2,1)S(1)}, bf16[64,256]{1,0:T(8,128)(2,1)S(1)}, u32[]{:S(2)}, u32[]{:S(2)}) %collective-permute-start.5) | collective-permute-done | bytes 32800 | tf_op jit(solution)/shard_map/ppermute | solution.py:265
  19.2 0.5 %collective-permute-done.8.refs_6_ = bf16[64,256]{1,0:T(8,128)(2,1)S(1)} collective-permute-done((bf16[64,256]{1,0:T(8,128)(2,1)S(1)}, bf16[64,256]{1,0:T(8,128)(2,1)S(1)}, u32[]{:S(2)}, u32[]{:S(2)}) %collective-permute-start.8) | collective-permute-done | bytes 32800 | tf_op jit(solution)/shard_map/ppermute | solution.py:268
  19.9 1.0 %layer.1 = (bf16[128,256]{1,0:T(8,128)(2,1)}, bf16[128,256]{1,0:T(8,128)(2,1)S(1)}, bf16[192,256]{1,0:T(8,128)(2,1)S(1)}, bf16[192,256]{1,0:T(8,128)(2,1)S(1)}, ...) custom-call(bf16[64,256]{1,0:T(8,128)(2,1)S(1)} %get-tuple-element.23.refs_0_, ...), custom_call_target="tpu_custom_call" | custom-call | tf_op jit(solution)/shard_map/layer/pallas_call | solution.py:306
  20.9 1.5 %collective-permute-start.12 = (bf16[192,256]{1,0:T(8,128)(2,1)S(1)}, bf16[192,256]{1,0:T(8,128)(2,1)S(1)}, u32[]{:S(2)}, u32[]{:S(2)}) collective-permute-start(bf16[192,256]{1,0:T(8,128)(2,1)S(1)} %get-tuple-element.32), channel_id=1, source_target_pairs={{0,8},{4,12},{8,0},{12,4},{16,24},{20,28},{24,16},{28,20},{1,9},{5... | collective-permute-start | bytes 294920 | tf_op jit(solution)/shard_map/ppermute | solution.py:265
  22.9 1.5 %collective-permute-start.14 = (bf16[192,256]{1,0:T(8,128)(2,1)S(1)}, bf16[192,256]{1,0:T(8,128)(2,1)S(1)}, u32[]{:S(2)}, u32[]{:S(2)}) collective-permute-start(bf16[192,256]{1,0:T(8,128)(2,1)S(1)} %get-tuple-element.34), channel_id=1, source_target_pairs={{0,24},{4,28},{8,16},{12,20},{16,8},{20,12},{24,0},{28,4},{1,25},{... | collective-permute-start | bytes 294920 | tf_op jit(solution)/shard_map/ppermute | solution.py:265
  24.4 1.6 %collective-permute-done.12.refs_3_ = bf16[192,256]{1,0:T(8,128)(2,1)S(1)} collective-permute-done((bf16[192,256]{1,0:T(8,128)(2,1)S(1)}, bf16[192,256]{1,0:T(8,128)(2,1)S(1)}, u32[]{:S(2)}, u32[]{:S(2)}) %collective-permute-start.12) | collective-permute-done | bytes 98336 | tf_op jit(solution)/shard_map/ppermute | solution.py:265
  26.0 3.3 %collective-permute-done.13.refs_4_ = bf16[192,256]{1,0:T(8,128)(2,1)S(1)} collective-permute-done((bf16[192,256]{1,0:T(8,128)(2,1)S(1)}, bf16[192,256]{1,0:T(8,128)(2,1)S(1)}, u32[]{:S(2)}, u32[]{:S(2)}) %collective-permute-start.13) | collective-permute-done | bytes 98336 | tf_op jit(solution)/shard_map/ppermute | solution.py:265
  29.6 2.7 %collective-permute-start.15 = (bf16[256,256]{1,0:T(8,128)(2,1)S(1)}, bf16[256,256]{1,0:T(8,128)(2,1)S(1)}, u32[]{:S(2)}, u32[]{:S(2)}) collective-permute-start(bf16[256,256]{1,0:T(8,128)(2,1)S(1)} %get-tuple-element.36), channel_id=1, source_target_pairs={{0,2},{1,3},{2,0},{3,1},{4,6},{5,7},{6,4},{7,5},{8,10},{9,11},{10,... | collective-permute-start | bytes 393224 | tf_op jit(solution)/shard_map/ppermute | solution.py:257
  32.4 0.9 %collective-permute-start.16 = (bf16[256,256]{1,0:T(8,128)(2,1)S(1)}, bf16[256,256]{1,0:T(8,128)(2,1)S(1)}, u32[]{:S(2)}, u32[]{:S(2)}) collective-permute-start(bf16[256,256]{1,0:T(8,128)(2,1)S(1)} %get-tuple-element.37), channel_id=1, source_target_pairs={{0,1},{1,0},{2,3},{3,2},{4,5},{5,4},{6,7},{7,6},{8,9},{9,8},{10,11... | collective-permute-start | bytes 393224 | tf_op jit(solution)/shard_map/ppermute | solution.py:257
  33.3 0.8 %collective-permute-start.17 = (bf16[256,256]{1,0:T(8,128)(2,1)S(1)}, bf16[256,256]{1,0:T(8,128)(2,1)S(1)}, u32[]{:S(2)}, u32[]{:S(2)}) collective-permute-start(bf16[256,256]{1,0:T(8,128)(2,1)S(1)} %get-tuple-element.38), channel_id=1, source_target_pairs={{0,3},{1,2},{2,1},{3,0},{4,7},{5,6},{6,5},{7,4},{8,11},{9,10},{10,... | collective-permute-start | bytes 393224 | tf_op jit(solution)/shard_map/ppermute | solution.py:257
  34.1 6.9 %collective-permute-done.15.refs_1_.refs_0_ = bf16[256,256]{1,0:T(8,128)(2,1)S(1)} collective-permute-done((bf16[256,256]{1,0:T(8,128)(2,1)S(1)}, bf16[256,256]{1,0:T(8,128)(2,1)S(1)}, u32[]{:S(2)}, u32[]{:S(2)}) %collective-permute-start.15) | collective-permute-done | bytes 131104 | tf_op jit(solution)/shard_map/ppermute | solution.py:257
  41.1 0.7 %grad_x.1 = bf16[128,256]{1,0:T(8,128)(2,1)} custom-call(f32[256,256]{1,0:T(8,128)S(1)} %get-tuple-element.35.refs_0_.kept_ref, bf16[256,256]{1,0:T(8,128)(2,1)S(1)} %collective-permute-done.15.refs_1_.refs_0_, bf16[256,256]{1,0:T(8,128)(2,1)S(1)} %collective-permute-done.16.refs_2_.refs_1_, bf16[256,256]{1,0:T(8,128)(2,1)S(1)} %collective-permute-done.17.refs_3_.refs_2_), custom_call_target="tpu_custom_call" | custom-call | tf_op jit(solution)/shard_map/grad_x/pallas_call | solution.py:356
  41.8 0.6 %collective-permute-done.18.refs_1_ = bf16[128,256]{1,0:T(8,128)(2,1)S(1)} collective-permute-done((bf16[128,256]{1,0:T(8,128)(2,1)S(1)}, bf16[128,256]{1,0:T(8,128)(2,1)S(1)}, u32[]{:S(2)}, u32[]{:S(2)}) %collective-permute-start.18) | collective-permute-done | bytes 65568 | tf_op jit(solution)/shard_map/ppermute | solution.py:268
  42.4 0.7 %grad_w.1 = f32[256,256]{1,0:T(8,128)} custom-call(bf16[128,256]{1,0:T(8,128)(2,1)S(1)} %chunk.1.refs_0_, bf16[128,256]{1,0:T(8,128)(2,1)S(1)} %collective-permute-done.18.refs_1_), custom_call_target="tpu_custom_call" | custom-call | tf_op jit(solution)/shard_map/grad_w/pallas_call | solution.py:366
  (35 shorter events, 3.5 us)
Async XLA Ops:
  0.6 5.7 %copy-start.5 = (s32[1,1,8,24]{3,2,1,0:T(8,128)S(1)}, s32[1,1,8,24]{3,2,1,0:T(8,128)}, u32[]{:S(2)}) copy-start(s32[1,1,8,24]{3,2,1,0:T(8,128)} %param.9) | copy-start | bytes 2308
  0.6 10.0 %collective-permute-start.2 = (bf16[128,256]{1,0:T(8,128)(2,1)}, bf16[128,256]{1,0:T(8,128)(2,1)S(1)}, u32[]{:S(2)}, u32[]{:S(2)}) collective-permute-start(bf16[128,256]{1,0:T(8,128)(2,1)} %refs_8_.1), channel_id=1, source_target_pairs={{0,2},{1,3},{2,0},{3,1},{4,6},{5,7},{6,4},{7,5},{8,10},{9,11},{10,... | collective-permute-start | bytes 196616 | tf_op jit(solution)/shard_map/ppermute | solution.py:257
  4.7 6.4 %collective-permute-start.1 = (bf16[128,256]{1,0:T(8,128)(2,1)}, bf16[128,256]{1,0:T(8,128)(2,1)S(1)}, u32[]{:S(2)}, u32[]{:S(2)}) collective-permute-start(bf16[128,256]{1,0:T(8,128)(2,1)} %refs_8_.1), channel_id=1, source_target_pairs={{0,3},{1,2},{2,1},{3,0},{4,7},{5,6},{6,5},{7,4},{8,11},{9,10},{10,... | collective-permute-start | bytes 196616 | tf_op jit(solution)/shard_map/ppermute | solution.py:257
  6.1 5.2 %collective-permute-start = (bf16[128,256]{1,0:T(8,128)(2,1)}, bf16[128,256]{1,0:T(8,128)(2,1)S(1)}, u32[]{:S(2)}, u32[]{:S(2)}) collective-permute-start(bf16[128,256]{1,0:T(8,128)(2,1)} %refs_8_.1), channel_id=1, source_target_pairs={{0,1},{1,0},{2,3},{3,2},{4,5},{5,4},{6,7},{7,6},{8,9},{9,8},{10,11... | collective-permute-start | bytes 196616 | tf_op jit(solution)/shard_map/ppermute | solution.py:257
  6.3 1.2 %copy-start = (bf16[1,1,4,8,128,128]{5,4,3,2,1,0:T(8,128)(2,1)S(1)}, bf16[1,1,4,8,128,128]{5,4,3,2,1,0:T(8,128)(2,1)}, u32[]{:S(2)}) copy-start(bf16[1,1,4,8,128,128]{5,4,3,2,1,0:T(8,128)(2,1)} %param.8) | copy-start | bytes 3145732
  11.3 5.2 %copy-start.4 = (bf16[128,256]{1,0:T(8,128)(2,1)S(1)}, bf16[128,256]{1,0:T(8,128)(2,1)}, u32[]{:S(2)}) copy-start(bf16[128,256]{1,0:T(8,128)(2,1)} %refs_10_.1) | copy-start | bytes 196612
  11.3 8.6 %copy-start.2 = (bf16[128,256]{1,0:T(8,128)(2,1)S(1)}, bf16[128,256]{1,0:T(8,128)(2,1)}, u32[]{:S(2)}) copy-start(bf16[128,256]{1,0:T(8,128)(2,1)} %refs_8_.1) | copy-start | bytes 196612
  11.3 8.6 %copy-start.3 = (bf16[256,256]{1,0:T(8,128)(2,1)S(1)}, bf16[256,256]{1,0:T(8,128)(2,1)}, u32[]{:S(2)}) copy-start(bf16[256,256]{1,0:T(8,128)(2,1)} %refs_12_.1) | copy-start | bytes 393220
  11.6 4.9 %collective-permute-start.3 = (bf16[64,256]{1,0:T(8,128)(2,1)S(1)}, bf16[64,256]{1,0:T(8,128)(2,1)S(1)}, u32[]{:S(2)}, u32[]{:S(2)}) collective-permute-start(bf16[64,256]{1,0:T(8,128)(2,1)S(1)} %get-tuple-element.24), channel_id=1, source_target_pairs={{0,24},{4,28},{8,16},{12,20},{16,8},{20,12},{24,0},{28,4},{1,25},{... | collective-permute-start | bytes 98312 | tf_op jit(solution)/shard_map/ppermute | solution.py:265
  14.1 4.5 %collective-permute-start.6 = (bf16[64,256]{1,0:T(8,128)(2,1)S(1)}, bf16[64,256]{1,0:T(8,128)(2,1)S(1)}, u32[]{:S(2)}, u32[]{:S(2)}) collective-permute-start(bf16[64,256]{1,0:T(8,128)(2,1)S(1)} %get-tuple-element.23.refs_0_), channel_id=1, source_target_pairs={{0,4},{4,0},{8,12},{12,8},{16,20},{20,16},{24,28},{28,24},{1,5},{5... | collective-permute-start | bytes 98312 | tf_op jit(solution)/shard_map/ppermute | solution.py:268
  14.1 3.9 %collective-permute-start.4 = (bf16[64,256]{1,0:T(8,128)(2,1)S(1)}, bf16[64,256]{1,0:T(8,128)(2,1)S(1)}, u32[]{:S(2)}, u32[]{:S(2)}) collective-permute-start(bf16[64,256]{1,0:T(8,128)(2,1)S(1)} %get-tuple-element.25), channel_id=1, source_target_pairs={{0,8},{4,12},{8,0},{12,4},{16,24},{20,28},{24,16},{28,20},{1,9},{5... | collective-permute-start | bytes 98312 | tf_op jit(solution)/shard_map/ppermute | solution.py:265
  14.6 3.9 %collective-permute-start.5 = (bf16[64,256]{1,0:T(8,128)(2,1)S(1)}, bf16[64,256]{1,0:T(8,128)(2,1)S(1)}, u32[]{:S(2)}, u32[]{:S(2)}) collective-permute-start(bf16[64,256]{1,0:T(8,128)(2,1)S(1)} %get-tuple-element.26), channel_id=1, source_target_pairs={{0,16},{4,20},{8,24},{12,28},{16,0},{20,4},{24,8},{28,12},{1,17},{... | collective-permute-start | bytes 98312 | tf_op jit(solution)/shard_map/ppermute | solution.py:265
  15.1 4.8 %collective-permute-start.10 = (bf16[128,256]{1,0:T(8,128)(2,1)S(1)}, bf16[128,256]{1,0:T(8,128)(2,1)S(1)}, u32[]{:S(2)}, u32[]{:S(2)}) collective-permute-start(bf16[128,256]{1,0:T(8,128)(2,1)S(1)} %copy-done.1), channel_id=1, source_target_pairs={{0,4},{4,0},{8,12},{12,8},{16,20},{20,16},{24,28},{28,24},{1,5},{5... | collective-permute-start | bytes 196616 | tf_op jit(solution)/shard_map/ppermute | solution.py:268
  16.4 3.5 %collective-permute-start.11 = (bf16[128,256]{1,0:T(8,128)(2,1)S(1)}, bf16[128,256]{1,0:T(8,128)(2,1)S(1)}, u32[]{:S(2)}, u32[]{:S(2)}) collective-permute-start(bf16[128,256]{1,0:T(8,128)(2,1)S(1)} %copy-done.4), channel_id=1, source_target_pairs={{0,4},{4,0},{8,12},{12,8},{16,20},{20,16},{24,28},{28,24},{1,5},{5... | collective-permute-start | bytes 196616 | tf_op jit(solution)/shard_map/ppermute | solution.py:268
  18.0 1.2 %collective-permute-start.7 = (bf16[64,256]{1,0:T(8,128)(2,1)S(1)}, bf16[64,256]{1,0:T(8,128)(2,1)S(1)}, u32[]{:S(2)}, u32[]{:S(2)}) collective-permute-start(bf16[64,256]{1,0:T(8,128)(2,1)S(1)} %collective-permute-done.3.refs_1_), channel_id=1, source_target_pairs={{0,4},{4,0},{8,12},{12,8},{16,20},{20,16},{24,28},{28,24},{1,5},{5... | collective-permute-start | bytes 98312 | tf_op jit(solution)/shard_map/ppermute | solution.py:268
  18.5 1.2 %collective-permute-start.8 = (bf16[64,256]{1,0:T(8,128)(2,1)S(1)}, bf16[64,256]{1,0:T(8,128)(2,1)S(1)}, u32[]{:S(2)}, u32[]{:S(2)}) collective-permute-start(bf16[64,256]{1,0:T(8,128)(2,1)S(1)} %collective-permute-done.4.refs_2_), channel_id=1, source_target_pairs={{0,4},{4,0},{8,12},{12,8},{16,20},{20,16},{24,28},{28,24},{1,5},{5... | collective-permute-start | bytes 98312 | tf_op jit(solution)/shard_map/ppermute | solution.py:268
  18.5 1.4 %collective-permute-start.9 = (bf16[64,256]{1,0:T(8,128)(2,1)S(1)}, bf16[64,256]{1,0:T(8,128)(2,1)S(1)}, u32[]{:S(2)}, u32[]{:S(2)}) collective-permute-start(bf16[64,256]{1,0:T(8,128)(2,1)S(1)} %collective-permute-done.5.refs_3_), channel_id=1, source_target_pairs={{0,4},{4,0},{8,12},{12,8},{16,20},{20,16},{24,28},{28,24},{1,5},{5... | collective-permute-start | bytes 98312 | tf_op jit(solution)/shard_map/ppermute | solution.py:268
  20.9 5.0 %collective-permute-start.12 = (bf16[192,256]{1,0:T(8,128)(2,1)S(1)}, bf16[192,256]{1,0:T(8,128)(2,1)S(1)}, u32[]{:S(2)}, u32[]{:S(2)}) collective-permute-start(bf16[192,256]{1,0:T(8,128)(2,1)S(1)} %get-tuple-element.32), channel_id=1, source_target_pairs={{0,8},{4,12},{8,0},{12,4},{16,24},{20,28},{24,16},{28,20},{1,9},{5... | collective-permute-start | bytes 294920 | tf_op jit(solution)/shard_map/ppermute | solution.py:265
  22.4 6.9 %collective-permute-start.13 = (bf16[192,256]{1,0:T(8,128)(2,1)S(1)}, bf16[192,256]{1,0:T(8,128)(2,1)S(1)}, u32[]{:S(2)}, u32[]{:S(2)}) collective-permute-start(bf16[192,256]{1,0:T(8,128)(2,1)S(1)} %get-tuple-element.33), channel_id=1, source_target_pairs={{0,16},{4,20},{8,24},{12,28},{16,0},{20,4},{24,8},{28,12},{1,17},{... | collective-permute-start | bytes 294920 | tf_op jit(solution)/shard_map/ppermute | solution.py:265
  22.9 6.4 %collective-permute-start.14 = (bf16[192,256]{1,0:T(8,128)(2,1)S(1)}, bf16[192,256]{1,0:T(8,128)(2,1)S(1)}, u32[]{:S(2)}, u32[]{:S(2)}) collective-permute-start(bf16[192,256]{1,0:T(8,128)(2,1)S(1)} %get-tuple-element.34), channel_id=1, source_target_pairs={{0,24},{4,28},{8,16},{12,20},{16,8},{20,12},{24,0},{28,4},{1,25},{... | collective-permute-start | bytes 294920 | tf_op jit(solution)/shard_map/ppermute | solution.py:265
  29.6 11.3 %collective-permute-start.15 = (bf16[256,256]{1,0:T(8,128)(2,1)S(1)}, bf16[256,256]{1,0:T(8,128)(2,1)S(1)}, u32[]{:S(2)}, u32[]{:S(2)}) collective-permute-start(bf16[256,256]{1,0:T(8,128)(2,1)S(1)} %get-tuple-element.36), channel_id=1, source_target_pairs={{0,2},{1,3},{2,0},{3,1},{4,6},{5,7},{6,4},{7,5},{8,10},{9,11},{10,... | collective-permute-start | bytes 393224 | tf_op jit(solution)/shard_map/ppermute | solution.py:257
  32.4 8.6 %collective-permute-start.16 = (bf16[256,256]{1,0:T(8,128)(2,1)S(1)}, bf16[256,256]{1,0:T(8,128)(2,1)S(1)}, u32[]{:S(2)}, u32[]{:S(2)}) collective-permute-start(bf16[256,256]{1,0:T(8,128)(2,1)S(1)} %get-tuple-element.37), channel_id=1, source_target_pairs={{0,1},{1,0},{2,3},{3,2},{4,5},{5,4},{6,7},{7,6},{8,9},{9,8},{10,11... | collective-permute-start | bytes 393224 | tf_op jit(solution)/shard_map/ppermute | solution.py:257
  33.3 7.7 %collective-permute-start.17 = (bf16[256,256]{1,0:T(8,128)(2,1)S(1)}, bf16[256,256]{1,0:T(8,128)(2,1)S(1)}, u32[]{:S(2)}, u32[]{:S(2)}) collective-permute-start(bf16[256,256]{1,0:T(8,128)(2,1)S(1)} %get-tuple-element.38), channel_id=1, source_target_pairs={{0,3},{1,2},{2,1},{3,0},{4,7},{5,6},{6,5},{7,4},{8,11},{9,10},{10,... | collective-permute-start | bytes 393224 | tf_op jit(solution)/shard_map/ppermute | solution.py:257
  41.0 1.3 %collective-permute-start.18 = (bf16[128,256]{1,0:T(8,128)(2,1)S(1)}, bf16[128,256]{1,0:T(8,128)(2,1)S(1)}, u32[]{:S(2)}, u32[]{:S(2)}) collective-permute-start(bf16[128,256]{1,0:T(8,128)(2,1)S(1)} %chunk.1.refs_0_), channel_id=1, source_target_pairs={{0,4},{4,0},{8,12},{12,8},{16,20},{20,16},{24,28},{28,24},{1,5},{5... | collective-permute-start | bytes 196616 | tf_op jit(solution)/shard_map/ppermute | solution.py:268
  (2 other events, 1.5 us)

commit v5 on v4

--- a/solution.py
+++ b/solution.py
@@ -12,6 +12,7 @@
 PAD = 32
 LANES = 128
 PAIR = 2
+MOST_ROWS = 4096
 
 
 def whole(count):
@@ -29,8 +30,9 @@
 
 
 LOW, HIGH, BOTH = (1, 0, 3, 2), (2, 3, 0, 1), (3, 2, 1, 0)
+RING, REVERSE = (2, 3, 1, 0), (3, 2, 0, 1)
 PLAN = dict(
-    A=(LOW, BOTH, HIGH), B=(BOTH, LOW, HIGH), C=(LOW, HIGH, BOTH), D=(HIGH, LOW, BOTH)
+    A=(LOW, BOTH, HIGH), B=(BOTH, LOW, HIGH), C=(LOW, HIGH, BOTH), D=(REVERSE, RING, LOW)
 )
 
 
@@ -75,12 +77,9 @@
 
 
 def inputs_kernel(
-    chips, source_ref, target_ref, features_ref, tiles_ref, picked_ref, base_ref, held, named_ref, sems
+    chips, plane, source_ref, target_ref, features_ref, tiles_ref, picked_ref, base_ref, named_ref
 ):
-    cols, per_col, block = held.shape[:3]
-    copies = [pltpu.make_async_copy(tiles_ref.at[b], held.at[b], sems.at[b]) for b in range(cols)]
-    for copy in copies:
-        copy.start()
+    cols, per_col, block = tiles_ref.shape[:3]
     peers, slot_count = source_ref.shape
     slots, width = base_ref.shape
     wide = width // PAD
@@ -103,12 +102,15 @@
     tiled = jnp.concatenate([tiled] * (width // LANES), axis=1)
     tiled = jnp.broadcast_to(tiled[:, None, :], (peers, PAD, width)).reshape(slots, width)
     row = lax.broadcasted_iota(jnp.int32, (slots, width), 0)
-    spot = lax.div(lax.broadcasted_iota(jnp.int32, (slots, width), 1), PAD)
-    at = step_to("B", chip, lax.div(row, PAD * PAIR), chips)
-    keep = jnp.zeros((slots, width), jnp.bool_)
-    for mate in range(PAIR):
-        here = lax.rem(row, PAD) == slot_count + mate
-        keep = keep | (here & (lax.rem(mate * chips + at, wide) == spot))
+    if plane:
+        keep = lax.rem(row, PAD) == slot_count
+    else:
+        spot = lax.div(lax.broadcasted_iota(jnp.int32, (slots, width), 1), PAD)
+        at = step_to("B", chip, lax.div(row, PAD * PAIR), chips)
+        keep = jnp.zeros((slots, width), jnp.bool_)
+        for mate in range(PAIR):
+            here = lax.rem(row, PAD) == slot_count + mate
+            keep = keep | (here & (lax.rem(mate * chips + at, wide) == spot))
     landing = jnp.where(keep, tiled, 0).astype(F32)
 
     for b in range(cols):
@@ -120,8 +122,7 @@
             ],
             axis=1,
         )
-        copies[b].wait()
-        rows = held[b].reshape(per_col * block, block)
+        rows = tiles_ref[b].reshape(per_col * block, block)
         picked_ref[b] = dot(hot, rows, 1, 0).astype(BF16)
     base_ref[...] = landing + dot(picked_ref[lax.axis_index("rep")], features_ref[...], 1, 0)
 
@@ -134,10 +135,78 @@
     total = base_ref[...]
     for step in range(1, reps):
         total += dot(picked_ref[origin_of("A", rep, step, reps)], features[step - 1][...], 1, 0)
+    if len(sends) == 1:
+        sends[0][...] = total.astype(BF16)
+        return
     total_ref[...] = total
     for step in range(chips):
         first = pl.multiple_of(target_of("B", chip, step, chips) * depth, depth)
         sends[step][...] = total_ref[pl.ds(first, depth), :].astype(BF16)
+
+
+def plane_kernel(reps, chips, slot_count, picked_ref, weight_ref, *refs):
+    peers = PAIR * chips
+    got, nodes, refs = refs[:peers], refs[peers : 2 * peers], refs[2 * peers :]
+    output_ref, kept_ref, *sends, aggregated_ref, grads_ref, block_ref, rows_ref = refs
+    rows, width = output_ref.shape
+    wide = width // PAD
+    rep = lax.axis_index("rep")
+    core = lax.rem(lax.axis_index("rows"), PAIR)
+    chip = lax.div(lax.axis_index("rows"), PAIR)
+    groups = pl.cdiv(peers, wide)
+    device = [
+        origin_of("B", chip, at % chips, chips) * PAIR + (core if at < chips else 1 - core)
+        for at in range(peers)
+    ]
+    row = lax.broadcasted_iota(jnp.int32, (rows, width), 0)
+    lane = lax.broadcasted_iota(jnp.int32, (rows, width), 1)
+    valid = lax.rem(lane, PAD) < slot_count
+    spot = lax.div(lax.broadcasted_iota(jnp.int32, (1, width), 1), PAD)
+    own_lanes = (lane < slot_count)[:, :LANES]
+    weight = weight_ref[...]
+    for at in range(peers):
+        first = pl.multiple_of(device[at] * PAD, PAD)
+        notes = [jnp.zeros((1, width), F32)] * groups
+        mine = None
+        for source in range(peers):
+            block = got[source][pl.ds(first, PAD), :]
+            block_ref[at, pl.ds(pl.multiple_of(device[source] * PAD, PAD), PAD), :] = block
+            note = block[16:].astype(F32)[slot_count - 16 :][:1]
+            mine = note if source == 0 else mine
+            for e in range(groups):
+                notes[e] = jnp.where(spot + e * wide == device[source], note, notes[e])
+        parts = [
+            jnp.where(valid & (note.astype(jnp.int32) == row), 1.0, 0.0).astype(BF16)
+            for note in notes
+        ]
+        hot = parts[0] if groups == 1 else jnp.concatenate(parts, axis=1)
+        arrived = dot(hot[:, : peers * PAD], block_ref[at], 1, 0)
+        aggregated = (nodes[at][:rows, :].astype(F32) + arrived).astype(BF16)
+        preact = dot(aggregated, weight, 1, 0)
+        sigmoid = jax.nn.sigmoid(preact)
+        pre_grad = (
+            nodes[at][rows:, :].astype(F32) * sigmoid * (1.0 + preact * (1.0 - sigmoid))
+        ).astype(BF16)
+        node = pl.multiple_of(device[at] * rows, rows)
+        aggregated_ref[pl.ds(node, rows), :] = aggregated
+        grads_ref[pl.ds(node, rows), :] = pre_grad
+        here = own_lanes & (mine.astype(jnp.int32)[:, :LANES] == row[:, :LANES])
+        asked = dot(jnp.where(here, 1.0, 0.0).astype(BF16), pre_grad, 0, 0)
+        rows_ref[pl.ds(first, PAD), :] = asked[:PAD].astype(BF16)
+        if at == 0:
+            output_ref[...] = (preact * sigmoid).astype(BF16)
+            back_in = dot(pre_grad, weight, 1, 1).astype(BF16)
+    part = width // PAIR
+    columns = aggregated_ref[:, :part]
+    for half in range(1, PAIR):
+        columns = jnp.where(core == half, aggregated_ref[:, half * part : (half + 1) * part], columns)
+    grad = dot(columns, grads_ref[...], 0, 0)
+    back = dot(rows_ref[...], weight, 1, 1).astype(BF16)
+    for step in range(1, reps):
+        term = dot(picked_ref[target_of("D", rep, step, reps)], back, 0, 0)
+        sends[step - 1][...] = jnp.concatenate([term, grad], axis=0).astype(BF16)
+    own = dot(picked_ref[rep], back, 0, 0) + back_in.astype(F32)
+    kept_ref[...] = jnp.concatenate([own, grad], axis=0)
 
 
 def layer_kernel(chips, slot_count, *refs):
@@ -252,6 +321,7 @@
     chips = peers // PAIR
     slots = peers * PAD
     chunk = width // PAIR
+    plane = peers * slots <= MOST_ROWS
 
     def over_rep(name, value, step):
         return lax.ppermute(value, "rep", list(enumerate(targets(name, step, reps))))
@@ -270,76 +340,111 @@
     gathered = [over_rep("A", features, step) for step in range(1, reps)]
 
     picked, base = pl.pallas_call(
-        lambda *refs: inputs_kernel(chips, *refs),
+        lambda *refs: inputs_kernel(chips, plane, *refs),
         out_shape=(
             jax.ShapeDtypeStruct((cols, slots, block), BF16),
             jax.ShapeDtypeStruct((slots, width), F32),
         ),
-        in_specs=whole(3) + [pl.BlockSpec(memory_space=pl.ANY)],
+        in_specs=whole(4),
         out_specs=tuple(whole(2)),
         scratch_shapes=[
-            pltpu.VMEM((cols, per_col, block, block), BF16),
             pltpu.VMEM((peers, LANES), jnp.int32),
-            pltpu.SemaphoreType.DMA((cols,)),
         ],
         compiler_params=params(slots),
         name="inputs",
     )(source, target, features, blocks)
 
-    message = jax.ShapeDtypeStruct((PAIR * PAD, width), BF16)
-    outgoing = pl.pallas_call(
-        lambda *refs: partial_kernel(reps, chips, *refs),
-        out_shape=(message,) * chips,
-        in_specs=whole(1 + reps),
-        out_specs=tuple(whole(chips)),
-        scratch_shapes=[pltpu.VMEM((slots, width), F32)],
-        compiler_params=params(slots),
-        name="partial",
-    )(picked, base, *gathered)
-
-    direct = [outgoing[0]] + [over_chips("B", outgoing[step], step) for step in range(1, chips)]
-    shared = [to_mate(value) for value in direct]
-    early_features, early_cotangent, _ = lax.optimization_barrier(
-        (features, cotangent, outgoing[0])
-    )
-
-    output, back_in, *requested = pl.pallas_call(
-        lambda *refs: layer_kernel(chips, slot_count, *refs),
-        out_shape=(
-            jax.ShapeDtypeStruct((rows, width), BF16),
-            jax.ShapeDtypeStruct((rows, width), BF16),
+    def partial(shape, count):
+        return pl.pallas_call(
+            lambda *refs: partial_kernel(reps, chips, *refs),
+            out_shape=(jax.ShapeDtypeStruct(shape, BF16),) * count,
+            in_specs=whole(1 + reps),
+            out_specs=tuple(whole(count)),
+            scratch_shapes=[pltpu.VMEM((slots, width), F32)],
+            compiler_params=params(slots),
+            name="partial",
+        )(picked, base, *gathered)
+
+    if plane:
+        (outgoing,) = partial((slots, width), 1)
+        both = jnp.concatenate([features, cotangent], axis=0)
+        if chips == 4:
+            low, high = (over_chips("B", both, step) for step in (2, 3))
+            nodes = [both, over_chips("B", high, 2), low, high]
+        else:
+            nodes = [both] + [over_chips("B", both, step) for step in range(1, chips)]
+        direct = [outgoing] + [over_chips("B", outgoing, step) for step in range(1, chips)]
+        *late, _ = lax.optimization_barrier((*nodes, outgoing))
+        hops = [to_mate(value) for value in late]
+        if chips > 1:
+            hops[0], hops[chips // 2], direct[1] = lax.optimization_barrier(
+                (hops[0], hops[chips // 2], direct[1])
+            )
+        nodes += hops
+        rows_in = direct + [to_mate(value) for value in direct]
+        output, kept, *sends = pl.pallas_call(
+            lambda *refs: plane_kernel(reps, chips, slot_count, *refs),
+            out_shape=(
+                jax.ShapeDtypeStruct((rows, width), BF16),
+                jax.ShapeDtypeStruct((rows + chunk, width), F32),
+            )
+            + (jax.ShapeDtypeStruct((rows + chunk, width), BF16),) * (reps - 1),
+            in_specs=whole(2 + 2 * peers),
+            out_specs=tuple(whole(1 + reps)),
+            scratch_shapes=[
+                pltpu.VMEM((peers * rows, width), BF16),
+                pltpu.VMEM((peers * rows, width), BF16),
+                pltpu.VMEM((peers, slots, width), BF16),
+                pltpu.VMEM((slots, width), BF16),
+            ],
+            compiler_params=params(slots),
+            name="plane",
+        )(picked, weight, *rows_in, *nodes)
+    else:
+        outgoing = partial((PAIR * PAD, width), chips)
+        direct = [outgoing[0]] + [over_chips("B", outgoing[step], step) for step in range(1, chips)]
+        shared = [to_mate(value) for value in direct]
+        early_features, early_cotangent, _ = lax.optimization_barrier(
+            (features, cotangent, outgoing[0])
         )
-        + (jax.ShapeDtypeStruct((PAIR * PAD + chunk, width), BF16),) * chips,
-        in_specs=whole(PAIR * chips + 5),
-        out_specs=tuple(whole(2 + chips)),
-        scratch_shapes=[pltpu.VMEM((width, width), F32)],
-        compiler_params=params(slots),
-        name="layer",
-    )(
-        *direct,
-        *shared,
-        features,
-        to_mate(early_features),
-        cotangent,
-        to_mate(early_cotangent),
-        weight,
-    )
-
-    returned = [requested[0]] + [over_chips("C", requested[step], step) for step in range(1, chips)]
-
-    kept, *sends = pl.pallas_call(
-        lambda *refs: terms_kernel(reps, chips, *refs),
-        out_shape=(jax.ShapeDtypeStruct((rows + chunk, width), F32),)
-        + (jax.ShapeDtypeStruct((rows + chunk, width), BF16),) * (reps - 1),
-        in_specs=whole(2 + chips),
-        out_specs=tuple(whole(reps)),
-        scratch_shapes=[
-            pltpu.VMEM((slots, width), BF16),
-            pltpu.VMEM((chips, chunk, width), F32),
-        ],
-        compiler_params=params(slots),
-        name="terms",
-    )(picked, back_in, *returned)
+
+        output, back_in, *requested = pl.pallas_call(
+            lambda *refs: layer_kernel(chips, slot_count, *refs),
+            out_shape=(
+                jax.ShapeDtypeStruct((rows, width), BF16),
+                jax.ShapeDtypeStruct((rows, width), BF16),
+            )
+            + (jax.ShapeDtypeStruct((PAIR * PAD + chunk, width), BF16),) * chips,
+            in_specs=whole(PAIR * chips + 5),
+            out_specs=tuple(whole(2 + chips)),
+            scratch_shapes=[pltpu.VMEM((width, width), F32)],
+            compiler_params=params(slots),
+            name="layer",
+        )(
+            *direct,
+            *shared,
+            features,
+            to_mate(early_features),
+            cotangent,
+            to_mate(early_cotangent),
+            weight,
+        )
+
+        returned = [requested[0]] + [over_chips("C", requested[step], step) for step in range(1, chips)]
+
+        kept, *sends = pl.pallas_call(
+            lambda *refs: terms_kernel(reps, chips, *refs),
+            out_shape=(jax.ShapeDtypeStruct((rows + chunk, width), F32),)
+            + (jax.ShapeDtypeStruct((rows + chunk, width), BF16),) * (reps - 1),
+            in_specs=whole(2 + chips),
+            out_specs=tuple(whole(reps)),
+            scratch_shapes=[
+                pltpu.VMEM((slots, width), BF16),
+                pltpu.VMEM((chips, chunk, width), F32),
+            ],
+            compiler_params=params(slots),
+            name="terms",
+        )(picked, back_in, *returned)
 
     arrived = [over_rep("D", sends[step - 1], step) for step in range(1, reps)]
 

time: 43.5 us -> 42.6 us (0.979)
  waiting for transfers between devices: 17.2 us -> 15.1 us
  starting transfers between devices: 17.8 us -> 19.2 us
  Pallas kernels: 4.64 us -> 5.28 us
  local copies, waits for them, and re-layouts: 2.77 us -> 2.13 us
    ppermute x6, waiting for transfers between devices: 8.28 us -> 4.27 us  [over_chips(): return lax.ppermute(value, 'rows', pairs)]
    ppermute x6, waiting for transfers between devices: 7.48 us -> 9.22 us  [over_rep(): lax.ppermute(value, 'rep', list(enumerate(targets(name, step, reps))))]
    ppermute x6, starting transfers between devices: 7.04 us -> 8.61 us  [over_chips(): return lax.ppermute(value, 'rows', pairs)]
    ppermute x6, starting transfers between devices: 10.1 us -> 8.84 us  [over_rep(): lax.ppermute(value, 'rep', list(enumerate(targets(name, step, reps))))]
    ppermute x7 -> x9, starting transfers between devices: 0.59 us -> 1.72 us  [to_mate(): return lax.ppermute(value, 'rows', [(i, i ^ 1) for i in range(peers)])]
    pallas_call x4 -> x3, Pallas kernels: 3.18 us -> 3.82 us  [the longest x1 2.65 us: local(): pl.pallas_call(lambda *refs: plane_kernel(reps, chips, slot_count, *refs)...]
    unnamed x14 -> x13, local copies, waits for them, and re-layouts: 2.77 us -> 2.13 us
    ppermute x7 -> x9, waiting for transfers between devices: 1.44 us -> 1.6 us  [to_mate(): return lax.ppermute(value, 'rows', [(i, i ^ 1) for i in range(peers)])]
  transfers between devices with their start and end apart: 19 -> 21, of which waited for: 12 -> 11; matrix products, arithmetic and copies ran while one was open for 0% -> 0% of each run, Pallas kernels for 5% -> 4%
where the time goes in v5:
time: 42.6 us; the launch traced here: 42.4 us
  starting transfers between devices  19.2 us (45%)
  waiting for transfers between devices  15.1 us (35%)
  Pallas kernels  5.28 us (12%)
  local copies, waits for them, and re-layouts  2.13 us (5%)
  between operations  0.74 us (2%)
    ppermute x6, waiting for transfers between devices, over_rep(): lax.ppermute(value, 'rep', list(enumerate(targets(name, step, reps))))  9.22 us
    ppermute x6, starting transfers between devices, over_rep(): lax.ppermute(value, 'rep', list(enumerate(targets(name, step, reps))))  8.84 us
    ppermute x6, starting transfers between devices, over_chips(): return lax.ppermute(value, 'rows', pairs)  8.61 us
    ppermute x6, waiting for transfers between devices, over_chips(): return lax.ppermute(value, 'rows', pairs)  4.27 us
    pallas_call x1, Pallas kernels, local(): pl.pallas_call(lambda *refs: plane_kernel(reps, chips, slot_count, *refs)...  2.65 us
    unnamed x13, local copies, waits for them, and re-layouts  2.13 us
    ppermute x9, starting transfers between devices, to_mate(): return lax.ppermute(value, 'rows', [(i, i ^ 1) for i in range(peers)])  1.72 us
    ppermute x9, waiting for transfers between devices, to_mate(): return lax.ppermute(value, 'rows', [(i, i ^ 1) for i in range(peers)])  1.6 us
  transfers between devices with their start and end apart: 21, of which 11 were waited for; matrix products, arithmetic and copies ran while one was open for 0% of the time, Pallas kernels for 4%

profile of v5, /device:TPU:0, one launch (start us, length us, event | category | flops | bytes accessed | tf_op | source)
XLA Modules:
  0.0 42.4 jit_solution(18319761217913356002)
XLA Ops:
  0.6 0.9 %constant_dynamic-update-slice_fusion.1 = bf16[256,256]{1,0:T(8,128)(2,1)S(1)} fusion(bf16[128,256]{1,0:T(8,128)(2,1)} %refs_2_.1), kind=kLoop, calls=%fused_computation.1 | loop fusion | bytes 131072
  1.6 3.0 %collective-permute-start.3 = (bf16[256,256]{1,0:T(8,128)(2,1)S(1)}, bf16[256,256]{1,0:T(8,128)(2,1)S(1)}, u32[]{:S(2)}, u32[]{:S(2)}) collective-permute-start(bf16[256,256]{1,0:T(8,128)(2,1)S(1)} %constant_dynamic-update-slice_fusion.refs_10_), channel_id=1, source_target_pairs={{0,16},{4,20},{8,24},{12,28},{16,0},{20,4},{24,8},{28,12},{1,17},{... | collective-permute-start | bytes 393224 | tf_op jit(solution)/shard_map/ppermute | solution.py:335
  4.6 3.6 %collective-permute-start.1 = (bf16[128,256]{1,0:T(8,128)(2,1)S(1)}, bf16[128,256]{1,0:T(8,128)(2,1)S(1)}, u32[]{:S(2)}, u32[]{:S(2)}) collective-permute-start(bf16[128,256]{1,0:T(8,128)(2,1)S(1)} %copy-done.1), channel_id=1, source_target_pairs={{0,3},{1,2},{2,1},{3,0},{4,7},{5,6},{6,5},{7,4},{8,11},{9,10},{10,... | collective-permute-start | bytes 196616 | tf_op jit(solution)/shard_map/ppermute | solution.py:327
  8.2 0.8 %collective-permute-start.2 = (bf16[128,256]{1,0:T(8,128)(2,1)S(1)}, bf16[128,256]{1,0:T(8,128)(2,1)S(1)}, u32[]{:S(2)}, u32[]{:S(2)}) collective-permute-start(bf16[128,256]{1,0:T(8,128)(2,1)S(1)} %copy-done.1), channel_id=1, source_target_pairs={{0,2},{1,3},{2,0},{3,1},{4,6},{5,7},{6,4},{7,5},{8,10},{9,11},{10,... | collective-permute-start | bytes 196616 | tf_op jit(solution)/shard_map/ppermute | solution.py:327
  9.0 1.5 %collective-permute-start.5 = (bf16[256,256]{1,0:T(8,128)(2,1)S(1)}, bf16[256,256]{1,0:T(8,128)(2,1)S(1)}, u32[]{:S(2)}, u32[]{:S(2)}) collective-permute-start(bf16[256,256]{1,0:T(8,128)(2,1)S(1)} %constant_dynamic-update-slice_fusion.refs_10_), channel_id=1, source_target_pairs={{0,8},{4,12},{8,0},{12,4},{16,24},{20,28},{24,16},{28,20},{1,9},{5... | collective-permute-start | bytes 393224 | tf_op jit(solution)/shard_map/ppermute | solution.py:335
  10.5 0.5 %collective-permute-start.4 = (bf16[256,256]{1,0:T(8,128)(2,1)S(1)}, bf16[256,256]{1,0:T(8,128)(2,1)S(1)}, u32[]{:S(2)}, u32[]{:S(2)}) collective-permute-start(bf16[256,256]{1,0:T(8,128)(2,1)S(1)} %collective-permute-done.3.refs_13_), channel_id=1, source_target_pairs={{0,8},{4,12},{8,0},{12,4},{16,24},{20,28},{24,16},{28,20},{1,9},{5... | collective-permute-start | bytes 393224 | tf_op jit(solution)/shard_map/ppermute | solution.py:335
  11.0 1.2 %copy-done = bf16[1,1,4,8,128,128]{5,4,3,2,1,0:T(8,128)(2,1)S(1)} copy-done((bf16[1,1,4,8,128,128]{5,4,3,2,1,0:T(8,128)(2,1)S(1)}, bf16[1,1,4,8,128,128]{5,4,3,2,1,0:T(8,128)(2,1)}, u32[]{:S(2)}) %copy-start) | copy-done | bytes 1048600
  12.3 0.9 %inputs.1 = (bf16[4,256,128]{2,1,0:T(8,128)(2,1)S(1)}, f32[256,256]{1,0:T(8,128)S(1)}) custom-call(s32[8,24]{1,0:T(8,128)S(1)} %bitcast.4, s32[8,24]{1,0:T(8,128)S(1)} %bitcast.5, bf16[128,256]{1,0:T(8,128)(2,1)S(1)} %copy-done.1, bf16[4,8,128,128]{3,2,1,0:T(8,128)(2,1)S(1)} %bitcast.3), custom_call_target="tpu_custom_call" | custom-call | tf_op jit(solution)/shard_map/inputs/pallas_call | solution.py:342
  13.8 1.1 %collective-permute-start.10 = (bf16[256,256]{1,0:T(8,128)(2,1)S(1)}, bf16[256,256]{1,0:T(8,128)(2,1)S(1)}, u32[]{:S(2)}, u32[]{:S(2)}) collective-permute-start(bf16[256,256]{1,0:T(8,128)(2,1)S(1)} %partial.1.refs_2_), channel_id=1, source_target_pairs={{0,16},{4,20},{8,24},{12,28},{16,0},{20,4},{24,8},{28,12},{1,17},{... | collective-permute-start | bytes 393224 | tf_op jit(solution)/shard_map/ppermute | solution.py:335
  14.9 1.5 %collective-permute-start.9 = (bf16[256,256]{1,0:T(8,128)(2,1)S(1)}, bf16[256,256]{1,0:T(8,128)(2,1)S(1)}, u32[]{:S(2)}, u32[]{:S(2)}) collective-permute-start(bf16[256,256]{1,0:T(8,128)(2,1)S(1)} %partial.1.refs_2_), channel_id=1, source_target_pairs={{0,8},{4,12},{8,0},{12,4},{16,24},{20,28},{24,16},{28,20},{1,9},{5... | collective-permute-start | bytes 393224 | tf_op jit(solution)/shard_map/ppermute | solution.py:335
  16.4 1.0 %collective-permute-start.8 = (bf16[256,256]{1,0:T(8,128)(2,1)S(1)}, bf16[256,256]{1,0:T(8,128)(2,1)S(1)}, u32[]{:S(2)}, u32[]{:S(2)}) collective-permute-start(bf16[256,256]{1,0:T(8,128)(2,1)S(1)} %partial.1.refs_2_), channel_id=1, source_target_pairs={{0,24},{4,28},{8,16},{12,20},{16,8},{20,12},{24,0},{28,4},{1,25},{... | collective-permute-start | bytes 393224 | tf_op jit(solution)/shard_map/ppermute | solution.py:335
  17.4 0.5 %collective-permute-start.7 = (bf16[256,256]{1,0:T(8,128)(2,1)S(1)}, bf16[256,256]{1,0:T(8,128)(2,1)S(1)}, u32[]{:S(2)}, u32[]{:S(2)}) collective-permute-start(bf16[256,256]{1,0:T(8,128)(2,1)S(1)} %collective-permute-done.5.refs_12_), channel_id=1, source_target_pairs={{0,4},{4,0},{8,12},{12,8},{16,20},{20,16},{24,28},{28,24},{1,5},{5... | collective-permute-start | bytes 393224 | tf_op jit(solution)/shard_map/ppermute | solution.py:338
  17.9 2.4 %collective-permute-done.10.refs_5_ = bf16[256,256]{1,0:T(8,128)(2,1)S(1)} collective-permute-done((bf16[256,256]{1,0:T(8,128)(2,1)S(1)}, bf16[256,256]{1,0:T(8,128)(2,1)S(1)}, u32[]{:S(2)}, u32[]{:S(2)}) %collective-permute-start.10) | collective-permute-done | bytes 131104 | tf_op jit(solution)/shard_map/ppermute | solution.py:335
  20.8 1.5 %collective-permute-done.8.refs_3_ = bf16[256,256]{1,0:T(8,128)(2,1)S(1)} collective-permute-done((bf16[256,256]{1,0:T(8,128)(2,1)S(1)}, bf16[256,256]{1,0:T(8,128)(2,1)S(1)}, u32[]{:S(2)}, u32[]{:S(2)}) %collective-permute-start.8) | collective-permute-done | bytes 131104 | tf_op jit(solution)/shard_map/ppermute | solution.py:335
  22.3 0.5 %collective-permute-start.15 = (bf16[256,256]{1,0:T(8,128)(2,1)S(1)}, bf16[256,256]{1,0:T(8,128)(2,1)S(1)}, u32[]{:S(2)}, u32[]{:S(2)}) collective-permute-start(bf16[256,256]{1,0:T(8,128)(2,1)S(1)} %collective-permute-done.4.refs_11_), channel_id=1, source_target_pairs={{0,4},{4,0},{8,12},{12,8},{16,20},{20,16},{24,28},{28,24},{1,5},{5... | collective-permute-start | bytes 393224 | tf_op jit(solution)/shard_map/ppermute | solution.py:338
  22.9 0.4 %collective-permute-start.12 = (bf16[256,256]{1,0:T(8,128)(2,1)S(1)}, bf16[256,256]{1,0:T(8,128)(2,1)S(1)}, u32[]{:S(2)}, u32[]{:S(2)}) collective-permute-start(bf16[256,256]{1,0:T(8,128)(2,1)S(1)} %collective-permute-done.8.refs_3_), channel_id=1, source_target_pairs={{0,4},{4,0},{8,12},{12,8},{16,20},{20,16},{24,28},{28,24},{1,5},{5... | collective-permute-start | bytes 393224 | tf_op jit(solution)/shard_map/ppermute | solution.py:338
  24.3 2.6 %plane.1 = (bf16[128,256]{1,0:T(8,128)(2,1)}, f32[256,256]{1,0:T(8,128)S(1)}, bf16[256,256]{1,0:T(8,128)(2,1)S(1)}, bf16[256,256]{1,0:T(8,128)(2,1)S(1)}, bf16[256,256]{1,0:T(8,128)(2,1)S(1)}) custom-call(bf16[4,256,128]{2,1,0:T(8,128)(2,1)S(1)} %get-tuple-element.17.refs_0_, bf16[256,256]{1,0:T(8,128)(2,1)S(1)} %copy-done.2, ...), custom_call_target="tpu_custom_call" | custom-call | tf_op jit(solution)/shard_map/plane/pallas_call | solution.py:385
  27.0 3.3 %collective-permute-start.17 = (bf16[256,256]{1,0:T(8,128)(2,1)S(1)}, bf16[256,256]{1,0:T(8,128)(2,1)S(1)}, u32[]{:S(2)}, u32[]{:S(2)}) collective-permute-start(bf16[256,256]{1,0:T(8,128)(2,1)S(1)} %get-tuple-element.28), channel_id=1, source_target_pairs={{0,3},{1,2},{2,0},{3,1},{4,7},{5,6},{6,4},{7,5},{8,11},{9,10},{10,... | collective-permute-start | bytes 393224 | tf_op jit(solution)/shard_map/ppermute | solution.py:327
  30.3 1.1 %collective-permute-start.19 = (bf16[256,256]{1,0:T(8,128)(2,1)S(1)}, bf16[256,256]{1,0:T(8,128)(2,1)S(1)}, u32[]{:S(2)}, u32[]{:S(2)}) collective-permute-start(bf16[256,256]{1,0:T(8,128)(2,1)S(1)} %get-tuple-element.30), channel_id=1, source_target_pairs={{0,1},{1,0},{2,3},{3,2},{4,5},{5,4},{6,7},{7,6},{8,9},{9,8},{10,11... | collective-permute-start | bytes 393224 | tf_op jit(solution)/shard_map/ppermute | solution.py:327
  31.4 8.4 %collective-permute-done.17.refs_1_.refs_0_ = bf16[256,256]{1,0:T(8,128)(2,1)S(1)} collective-permute-done((bf16[256,256]{1,0:T(8,128)(2,1)S(1)}, bf16[256,256]{1,0:T(8,128)(2,1)S(1)}, u32[]{:S(2)}, u32[]{:S(2)}) %collective-permute-start.17) | collective-permute-done | bytes 131104 | tf_op jit(solution)/shard_map/ppermute | solution.py:327
  39.9 0.4 %collective-permute-done.19.refs_3_.refs_2_ = bf16[256,256]{1,0:T(8,128)(2,1)S(1)} collective-permute-done((bf16[256,256]{1,0:T(8,128)(2,1)S(1)}, bf16[256,256]{1,0:T(8,128)(2,1)S(1)}, u32[]{:S(2)}, u32[]{:S(2)}) %collective-permute-start.19) | collective-permute-done | bytes 131104 | tf_op jit(solution)/shard_map/ppermute | solution.py:327
  40.4 0.7 %grad_x.1 = bf16[128,256]{1,0:T(8,128)(2,1)} custom-call(f32[256,256]{1,0:T(8,128)S(1)} %get-tuple-element.27.refs_0_.kept_ref, bf16[256,256]{1,0:T(8,128)(2,1)S(1)} %collective-permute-done.17.refs_1_.refs_0_, bf16[256,256]{1,0:T(8,128)(2,1)S(1)} %collective-permute-done.18.refs_2_.refs_1_, bf16[256,256]{1,0:T(8,128)(2,1)S(1)} %collective-permute-done.19.refs_3_.refs_2_), custom_call_target="tpu_custom_call" | custom-call | tf_op jit(solution)/shard_map/grad_x/pallas_call | solution.py:461
  41.1 0.6 %collective-permute-done.20.refs_1_ = bf16[128,256]{1,0:T(8,128)(2,1)S(1)} collective-permute-done((bf16[128,256]{1,0:T(8,128)(2,1)S(1)}, bf16[128,256]{1,0:T(8,128)(2,1)S(1)}, u32[]{:S(2)}, u32[]{:S(2)}) %collective-permute-start.20) | collective-permute-done | bytes 65568 | tf_op jit(solution)/shard_map/ppermute | solution.py:338
  41.7 0.7 %grad_w.1 = f32[256,256]{1,0:T(8,128)} custom-call(bf16[128,256]{1,0:T(8,128)(2,1)S(1)} %chunk.1.refs_0_, bf16[128,256]{1,0:T(8,128)(2,1)S(1)} %collective-permute-done.20.refs_1_), custom_call_target="tpu_custom_call" | custom-call | tf_op jit(solution)/shard_map/grad_w/pallas_call | solution.py:471
  (38 shorter events, 2.4 us)
Async XLA Ops:
  1.5 9.5 %copy-start.4 = (s32[1,1,8,24]{3,2,1,0:T(8,128)S(1)}, s32[1,1,8,24]{3,2,1,0:T(8,128)}, u32[]{:S(2)}) copy-start(s32[1,1,8,24]{3,2,1,0:T(8,128)} %param.10) | copy-start | bytes 2308
  1.6 9.5 %copy-start.3 = (s32[1,1,8,24]{3,2,1,0:T(8,128)S(1)}, s32[1,1,8,24]{3,2,1,0:T(8,128)}, u32[]{:S(2)}) copy-start(s32[1,1,8,24]{3,2,1,0:T(8,128)} %param.9) | copy-start | bytes 2308
  1.6 8.9 %collective-permute-start.3 = (bf16[256,256]{1,0:T(8,128)(2,1)S(1)}, bf16[256,256]{1,0:T(8,128)(2,1)S(1)}, u32[]{:S(2)}, u32[]{:S(2)}) collective-permute-start(bf16[256,256]{1,0:T(8,128)(2,1)S(1)} %constant_dynamic-update-slice_fusion.refs_10_), channel_id=1, source_target_pairs={{0,16},{4,20},{8,24},{12,28},{16,0},{20,4},{24,8},{28,12},{1,17},{... | collective-permute-start | bytes 393224 | tf_op jit(solution)/shard_map/ppermute | solution.py:335
  4.6 8.6 %collective-permute-start.1 = (bf16[128,256]{1,0:T(8,128)(2,1)S(1)}, bf16[128,256]{1,0:T(8,128)(2,1)S(1)}, u32[]{:S(2)}, u32[]{:S(2)}) collective-permute-start(bf16[128,256]{1,0:T(8,128)(2,1)S(1)} %copy-done.1), channel_id=1, source_target_pairs={{0,3},{1,2},{2,1},{3,0},{4,7},{5,6},{6,5},{7,4},{8,11},{9,10},{10,... | collective-permute-start | bytes 196616 | tf_op jit(solution)/shard_map/ppermute | solution.py:327
  8.2 5.0 %collective-permute-start = (bf16[128,256]{1,0:T(8,128)(2,1)S(1)}, bf16[128,256]{1,0:T(8,128)(2,1)S(1)}, u32[]{:S(2)}, u32[]{:S(2)}) collective-permute-start(bf16[128,256]{1,0:T(8,128)(2,1)S(1)} %copy-done.1), channel_id=1, source_target_pairs={{0,1},{1,0},{2,3},{3,2},{4,5},{5,4},{6,7},{7,6},{8,9},{9,8},{10,11... | collective-permute-start | bytes 196616 | tf_op jit(solution)/shard_map/ppermute | solution.py:327
  8.2 5.4 %collective-permute-start.2 = (bf16[128,256]{1,0:T(8,128)(2,1)S(1)}, bf16[128,256]{1,0:T(8,128)(2,1)S(1)}, u32[]{:S(2)}, u32[]{:S(2)}) collective-permute-start(bf16[128,256]{1,0:T(8,128)(2,1)S(1)} %copy-done.1), channel_id=1, source_target_pairs={{0,2},{1,3},{2,0},{3,1},{4,6},{5,7},{6,4},{7,5},{8,10},{9,11},{10,... | collective-permute-start | bytes 196616 | tf_op jit(solution)/shard_map/ppermute | solution.py:327
  9.0 8.4 %collective-permute-start.5 = (bf16[256,256]{1,0:T(8,128)(2,1)S(1)}, bf16[256,256]{1,0:T(8,128)(2,1)S(1)}, u32[]{:S(2)}, u32[]{:S(2)}) collective-permute-start(bf16[256,256]{1,0:T(8,128)(2,1)S(1)} %constant_dynamic-update-slice_fusion.refs_10_), channel_id=1, source_target_pairs={{0,8},{4,12},{8,0},{12,4},{16,24},{20,28},{24,16},{28,20},{1,9},{5... | collective-permute-start | bytes 393224 | tf_op jit(solution)/shard_map/ppermute | solution.py:335
  10.5 6.9 %collective-permute-start.4 = (bf16[256,256]{1,0:T(8,128)(2,1)S(1)}, bf16[256,256]{1,0:T(8,128)(2,1)S(1)}, u32[]{:S(2)}, u32[]{:S(2)}) collective-permute-start(bf16[256,256]{1,0:T(8,128)(2,1)S(1)} %collective-permute-done.3.refs_13_), channel_id=1, source_target_pairs={{0,8},{4,12},{8,0},{12,4},{16,24},{20,28},{24,16},{28,20},{1,9},{5... | collective-permute-start | bytes 393224 | tf_op jit(solution)/shard_map/ppermute | solution.py:335
  13.6 10.8 %copy-start.2 = (bf16[256,256]{1,0:T(8,128)(2,1)S(1)}, bf16[256,256]{1,0:T(8,128)(2,1)}, u32[]{:S(2)}) copy-start(bf16[256,256]{1,0:T(8,128)(2,1)} %refs_1_.1) | copy-start | bytes 393220
  13.8 6.4 %collective-permute-start.10 = (bf16[256,256]{1,0:T(8,128)(2,1)S(1)}, bf16[256,256]{1,0:T(8,128)(2,1)S(1)}, u32[]{:S(2)}, u32[]{:S(2)}) collective-permute-start(bf16[256,256]{1,0:T(8,128)(2,1)S(1)} %partial.1.refs_2_), channel_id=1, source_target_pairs={{0,16},{4,20},{8,24},{12,28},{16,0},{20,4},{24,8},{28,12},{1,17},{... | collective-permute-start | bytes 393224 | tf_op jit(solution)/shard_map/ppermute | solution.py:335
  14.9 5.8 %collective-permute-start.9 = (bf16[256,256]{1,0:T(8,128)(2,1)S(1)}, bf16[256,256]{1,0:T(8,128)(2,1)S(1)}, u32[]{:S(2)}, u32[]{:S(2)}) collective-permute-start(bf16[256,256]{1,0:T(8,128)(2,1)S(1)} %partial.1.refs_2_), channel_id=1, source_target_pairs={{0,8},{4,12},{8,0},{12,4},{16,24},{20,28},{24,16},{28,20},{1,9},{5... | collective-permute-start | bytes 393224 | tf_op jit(solution)/shard_map/ppermute | solution.py:335
  16.4 5.9 %collective-permute-start.8 = (bf16[256,256]{1,0:T(8,128)(2,1)S(1)}, bf16[256,256]{1,0:T(8,128)(2,1)S(1)}, u32[]{:S(2)}, u32[]{:S(2)}) collective-permute-start(bf16[256,256]{1,0:T(8,128)(2,1)S(1)} %partial.1.refs_2_), channel_id=1, source_target_pairs={{0,24},{4,28},{8,16},{12,20},{16,8},{20,12},{24,0},{28,4},{1,25},{... | collective-permute-start | bytes 393224 | tf_op jit(solution)/shard_map/ppermute | solution.py:335
  17.4 4.9 %collective-permute-start.6 = (bf16[256,256]{1,0:T(8,128)(2,1)S(1)}, bf16[256,256]{1,0:T(8,128)(2,1)S(1)}, u32[]{:S(2)}, u32[]{:S(2)}) collective-permute-start(bf16[256,256]{1,0:T(8,128)(2,1)S(1)} %constant_dynamic-update-slice_fusion.refs_10_), channel_id=1, source_target_pairs={{0,4},{4,0},{8,12},{12,8},{16,20},{20,16},{24,28},{28,24},{1,5},{5... | collective-permute-start | bytes 393224 | tf_op jit(solution)/shard_map/ppermute | solution.py:338
  17.4 5.4 %collective-permute-start.7 = (bf16[256,256]{1,0:T(8,128)(2,1)S(1)}, bf16[256,256]{1,0:T(8,128)(2,1)S(1)}, u32[]{:S(2)}, u32[]{:S(2)}) collective-permute-start(bf16[256,256]{1,0:T(8,128)(2,1)S(1)} %collective-permute-done.5.refs_12_), channel_id=1, source_target_pairs={{0,4},{4,0},{8,12},{12,8},{16,20},{20,16},{24,28},{28,24},{1,5},{5... | collective-permute-start | bytes 393224 | tf_op jit(solution)/shard_map/ppermute | solution.py:338
  20.3 2.6 %collective-permute-start.11 = (bf16[256,256]{1,0:T(8,128)(2,1)S(1)}, bf16[256,256]{1,0:T(8,128)(2,1)S(1)}, u32[]{:S(2)}, u32[]{:S(2)}) collective-permute-start(bf16[256,256]{1,0:T(8,128)(2,1)S(1)} %partial.1.refs_2_), channel_id=1, source_target_pairs={{0,4},{4,0},{8,12},{12,8},{16,20},{20,16},{24,28},{28,24},{1,5},{5... | collective-permute-start | bytes 393224 | tf_op jit(solution)/shard_map/ppermute | solution.py:338
  20.6 2.7 %collective-permute-start.14 = (bf16[256,256]{1,0:T(8,128)(2,1)S(1)}, bf16[256,256]{1,0:T(8,128)(2,1)S(1)}, u32[]{:S(2)}, u32[]{:S(2)}) collective-permute-start(bf16[256,256]{1,0:T(8,128)(2,1)S(1)} %collective-permute-done.10.refs_5_), channel_id=1, source_target_pairs={{0,4},{4,0},{8,12},{12,8},{16,20},{20,16},{24,28},{28,24},{1,5},{5... | collective-permute-start | bytes 393224 | tf_op jit(solution)/shard_map/ppermute | solution.py:338
  22.3 1.3 %collective-permute-start.13 = (bf16[256,256]{1,0:T(8,128)(2,1)S(1)}, bf16[256,256]{1,0:T(8,128)(2,1)S(1)}, u32[]{:S(2)}, u32[]{:S(2)}) collective-permute-start(bf16[256,256]{1,0:T(8,128)(2,1)S(1)} %collective-permute-done.9.refs_4_), channel_id=1, source_target_pairs={{0,4},{4,0},{8,12},{12,8},{16,20},{20,16},{24,28},{28,24},{1,5},{5... | collective-permute-start | bytes 393224 | tf_op jit(solution)/shard_map/ppermute | solution.py:338
  22.3 1.5 %collective-permute-start.15 = (bf16[256,256]{1,0:T(8,128)(2,1)S(1)}, bf16[256,256]{1,0:T(8,128)(2,1)S(1)}, u32[]{:S(2)}, u32[]{:S(2)}) collective-permute-start(bf16[256,256]{1,0:T(8,128)(2,1)S(1)} %collective-permute-done.4.refs_11_), channel_id=1, source_target_pairs={{0,4},{4,0},{8,12},{12,8},{16,20},{20,16},{24,28},{28,24},{1,5},{5... | collective-permute-start | bytes 393224 | tf_op jit(solution)/shard_map/ppermute | solution.py:338
  22.8 1.3 %collective-permute-start.16 = (bf16[256,256]{1,0:T(8,128)(2,1)S(1)}, bf16[256,256]{1,0:T(8,128)(2,1)S(1)}, u32[]{:S(2)}, u32[]{:S(2)}) collective-permute-start(bf16[256,256]{1,0:T(8,128)(2,1)S(1)} %collective-permute-done.3.refs_13_), channel_id=1, source_target_pairs={{0,4},{4,0},{8,12},{12,8},{16,20},{20,16},{24,28},{28,24},{1,5},{5... | collective-permute-start | bytes 393224 | tf_op jit(solution)/shard_map/ppermute | solution.py:338
  22.9 1.5 %collective-permute-start.12 = (bf16[256,256]{1,0:T(8,128)(2,1)S(1)}, bf16[256,256]{1,0:T(8,128)(2,1)S(1)}, u32[]{:S(2)}, u32[]{:S(2)}) collective-permute-start(bf16[256,256]{1,0:T(8,128)(2,1)S(1)} %collective-permute-done.8.refs_3_), channel_id=1, source_target_pairs={{0,4},{4,0},{8,12},{12,8},{16,20},{20,16},{24,28},{28,24},{1,5},{5... | collective-permute-start | bytes 393224 | tf_op jit(solution)/shard_map/ppermute | solution.py:338
  27.0 12.9 %collective-permute-start.17 = (bf16[256,256]{1,0:T(8,128)(2,1)S(1)}, bf16[256,256]{1,0:T(8,128)(2,1)S(1)}, u32[]{:S(2)}, u32[]{:S(2)}) collective-permute-start(bf16[256,256]{1,0:T(8,128)(2,1)S(1)} %get-tuple-element.28), channel_id=1, source_target_pairs={{0,3},{1,2},{2,0},{3,1},{4,7},{5,6},{6,4},{7,5},{8,11},{9,10},{10,... | collective-permute-start | bytes 393224 | tf_op jit(solution)/shard_map/ppermute | solution.py:327
  30.3 9.6 %collective-permute-start.18 = (bf16[256,256]{1,0:T(8,128)(2,1)S(1)}, bf16[256,256]{1,0:T(8,128)(2,1)S(1)}, u32[]{:S(2)}, u32[]{:S(2)}) collective-permute-start(bf16[256,256]{1,0:T(8,128)(2,1)S(1)} %get-tuple-element.29), channel_id=1, source_target_pairs={{0,2},{1,3},{2,1},{3,0},{4,6},{5,7},{6,5},{7,4},{8,10},{9,11},{10,... | collective-permute-start | bytes 393224 | tf_op jit(solution)/shard_map/ppermute | solution.py:327
  30.3 10.0 %collective-permute-start.19 = (bf16[256,256]{1,0:T(8,128)(2,1)S(1)}, bf16[256,256]{1,0:T(8,128)(2,1)S(1)}, u32[]{:S(2)}, u32[]{:S(2)}) collective-permute-start(bf16[256,256]{1,0:T(8,128)(2,1)S(1)} %get-tuple-element.30), channel_id=1, source_target_pairs={{0,1},{1,0},{2,3},{3,2},{4,5},{5,4},{6,7},{7,6},{8,9},{9,8},{10,11... | collective-permute-start | bytes 393224 | tf_op jit(solution)/shard_map/ppermute | solution.py:327
  40.4 1.3 %collective-permute-start.20 = (bf16[128,256]{1,0:T(8,128)(2,1)S(1)}, bf16[128,256]{1,0:T(8,128)(2,1)S(1)}, u32[]{:S(2)}, u32[]{:S(2)}) collective-permute-start(bf16[128,256]{1,0:T(8,128)(2,1)S(1)} %chunk.1.refs_0_), channel_id=1, source_target_pairs={{0,4},{4,0},{8,12},{12,8},{16,20},{20,16},{24,28},{28,24},{1,5},{5... | collective-permute-start | bytes 196616 | tf_op jit(solution)/shard_map/ppermute | solution.py:338
  (3 other events, 5.2 us)

commit v6 on v5

--- a/solution.py
+++ b/solution.py
@@ -77,7 +77,7 @@
 
 
 def inputs_kernel(
-    chips, plane, source_ref, target_ref, features_ref, tiles_ref, picked_ref, base_ref, named_ref
+    chips, plane, source_ref, target_ref, features_ref, tiles_ref, picked_ref, base_ref, wanted_ref, named_ref
 ):
     cols, per_col, block = tiles_ref.shape[:3]
     peers, slot_count = source_ref.shape
@@ -96,6 +96,10 @@
     named_ref[...] = jnp.zeros(named_ref.shape, jnp.int32)
     named_ref[:, :slot_count] = target
     notes = named_ref[...]
+    spread = jnp.broadcast_to(notes[:, None, :], (peers, PAD, LANES)).reshape(slots, LANES)
+    landing = jnp.sum(jnp.where(lane == slot, spread, 0).astype(F32), axis=1, keepdims=True)
+    here = (jnp.broadcast_to(landing, (slots, LANES)) == lane.astype(F32)) & (slot < slot_count)
+    wanted_ref[...] = jnp.where(here, 1.0, 0.0).astype(BF16)
     tiled = notes
     for turn in range(1, LANES // PAD):
         tiled += pltpu.roll(notes, turn * PAD, 1)
@@ -144,16 +148,20 @@
         sends[step][...] = total_ref[pl.ds(first, depth), :].astype(BF16)
 
 
-def plane_kernel(reps, chips, slot_count, picked_ref, weight_ref, *refs):
+def plane_kernel(reps, chips, slot_count, picked_ref, wanted_ref, weight_ref, *refs):
     peers = PAIR * chips
     got, nodes, refs = refs[:peers], refs[peers : 2 * peers], refs[2 * peers :]
-    output_ref, kept_ref, *sends, aggregated_ref, grads_ref, block_ref, rows_ref = refs
+    output_ref, kept_ref, *sends, aggregated_ref, cotangent_ref, block_ref, wide_ref = refs
     rows, width = output_ref.shape
     wide = width // PAD
     rep = lax.axis_index("rep")
     core = lax.rem(lax.axis_index("rows"), PAIR)
     chip = lax.div(lax.axis_index("rows"), PAIR)
     groups = pl.cdiv(peers, wide)
+    wide_ref[...] = jnp.zeros(wide_ref.shape, BF16)
+    for at in range(peers):
+        here = slice(at * PAD, (at + 1) * PAD)
+        wide_ref[here, at * rows : (at + 1) * rows] = wanted_ref[here, :]
     device = [
         origin_of("B", chip, at % chips, chips) * PAIR + (core if at < chips else 1 - core)
         for at in range(peers)
@@ -162,17 +170,15 @@
     lane = lax.broadcasted_iota(jnp.int32, (rows, width), 1)
     valid = lax.rem(lane, PAD) < slot_count
     spot = lax.div(lax.broadcasted_iota(jnp.int32, (1, width), 1), PAD)
-    own_lanes = (lane < slot_count)[:, :LANES]
     weight = weight_ref[...]
+    hots = []
     for at in range(peers):
         first = pl.multiple_of(device[at] * PAD, PAD)
         notes = [jnp.zeros((1, width), F32)] * groups
-        mine = None
         for source in range(peers):
             block = got[source][pl.ds(first, PAD), :]
             block_ref[at, pl.ds(pl.multiple_of(device[source] * PAD, PAD), PAD), :] = block
             note = block[16:].astype(F32)[slot_count - 16 :][:1]
-            mine = note if source == 0 else mine
             for e in range(groups):
                 notes[e] = jnp.where(spot + e * wide == device[source], note, notes[e])
         parts = [
@@ -180,28 +186,32 @@
             for note in notes
         ]
         hot = parts[0] if groups == 1 else jnp.concatenate(parts, axis=1)
-        arrived = dot(hot[:, : peers * PAD], block_ref[at], 1, 0)
-        aggregated = (nodes[at][:rows, :].astype(F32) + arrived).astype(BF16)
+        hots.append(hot[:, : peers * PAD])
+    arrived = [dot(hots[at], block_ref[at], 1, 0) for at in range(peers)]
+    aggregates = [
+        (nodes[at][:rows, :].astype(F32) + arrived[at]).astype(BF16) for at in range(peers)
+    ]
+    for at in range(peers):
+        node = pl.multiple_of(device[at] * rows, rows)
+        aggregated_ref[pl.ds(node, rows), :] = aggregates[at]
+        cotangent_ref[pl.ds(node, rows), :] = nodes[at][rows:, :]
+
+    def layer(aggregated, cotangent):
         preact = dot(aggregated, weight, 1, 0)
         sigmoid = jax.nn.sigmoid(preact)
-        pre_grad = (
-            nodes[at][rows:, :].astype(F32) * sigmoid * (1.0 + preact * (1.0 - sigmoid))
-        ).astype(BF16)
-        node = pl.multiple_of(device[at] * rows, rows)
-        aggregated_ref[pl.ds(node, rows), :] = aggregated
-        grads_ref[pl.ds(node, rows), :] = pre_grad
-        here = own_lanes & (mine.astype(jnp.int32)[:, :LANES] == row[:, :LANES])
-        asked = dot(jnp.where(here, 1.0, 0.0).astype(BF16), pre_grad, 0, 0)
-        rows_ref[pl.ds(first, PAD), :] = asked[:PAD].astype(BF16)
-        if at == 0:
-            output_ref[...] = (preact * sigmoid).astype(BF16)
-            back_in = dot(pre_grad, weight, 1, 1).astype(BF16)
+        pre_grad = cotangent.astype(F32) * sigmoid * (1.0 + preact * (1.0 - sigmoid))
+        return (preact * sigmoid).astype(BF16), pre_grad.astype(BF16)
+
+    output_ref[...], own_grad = layer(aggregates[0], nodes[0][rows:, :])
+    back_in = dot(own_grad, weight, 1, 1).astype(BF16)
+    _, grads = layer(aggregated_ref[...], cotangent_ref[...])
     part = width // PAIR
     columns = aggregated_ref[:, :part]
     for half in range(1, PAIR):
         columns = jnp.where(core == half, aggregated_ref[:, half * part : (half + 1) * part], columns)
-    grad = dot(columns, grads_ref[...], 0, 0)
-    back = dot(rows_ref[...], weight, 1, 1).astype(BF16)
+    grad = dot(columns, grads, 0, 0)
+    asked = dot(wide_ref[...], grads, 1, 0).astype(BF16)
+    back = dot(asked, weight, 1, 1).astype(BF16)
     for step in range(1, reps):
         term = dot(picked_ref[target_of("D", rep, step, reps)], back, 0, 0)
         sends[step - 1][...] = jnp.concatenate([term, grad], axis=0).astype(BF16)
@@ -339,14 +349,15 @@
 
     gathered = [over_rep("A", features, step) for step in range(1, reps)]
 
-    picked, base = pl.pallas_call(
+    picked, base, wanted = pl.pallas_call(
         lambda *refs: inputs_kernel(chips, plane, *refs),
         out_shape=(
             jax.ShapeDtypeStruct((cols, slots, block), BF16),
             jax.ShapeDtypeStruct((slots, width), F32),
+            jax.ShapeDtypeStruct((slots, rows), BF16),
         ),
         in_specs=whole(4),
-        out_specs=tuple(whole(2)),
+        out_specs=tuple(whole(3)),
         scratch_shapes=[
             pltpu.VMEM((peers, LANES), jnp.int32),
         ],
@@ -370,7 +381,7 @@
         both = jnp.concatenate([features, cotangent], axis=0)
         if chips == 4:
             low, high = (over_chips("B", both, step) for step in (2, 3))
-            nodes = [both, over_chips("B", high, 2), low, high]
+            nodes = [both, over_chips("B", low, 3), low, high]
         else:
             nodes = [both] + [over_chips("B", both, step) for step in range(1, chips)]
         direct = [outgoing] + [over_chips("B", outgoing, step) for step in range(1, chips)]
@@ -389,17 +400,17 @@
                 jax.ShapeDtypeStruct((rows + chunk, width), F32),
             )
             + (jax.ShapeDtypeStruct((rows + chunk, width), BF16),) * (reps - 1),
-            in_specs=whole(2 + 2 * peers),
+            in_specs=whole(3 + 2 * peers),
             out_specs=tuple(whole(1 + reps)),
             scratch_shapes=[
                 pltpu.VMEM((peers * rows, width), BF16),
                 pltpu.VMEM((peers * rows, width), BF16),
                 pltpu.VMEM((peers, slots, width), BF16),
-                pltpu.VMEM((slots, width), BF16),
+                pltpu.VMEM((slots, peers * rows), BF16),
             ],
             compiler_params=params(slots),
             name="plane",
-        )(picked, weight, *rows_in, *nodes)
+        )(picked, wanted, weight, *rows_in, *nodes)
     else:
         outgoing = partial((PAIR * PAD, width), chips)
         direct = [outgoing[0]] + [over_chips("B", outgoing[step], step) for step in range(1, chips)]

time: 42.6 us -> 41.8 us (0.981)
  Pallas kernels: 5.28 us -> 4.82 us
    pallas_call x1, Pallas kernels: 2.65 us -> 2.19 us  [local(): pl.pallas_call(lambda *refs: plane_kernel(reps, chips, slot_count, *refs)...]
where the time goes in v6:
time: 41.8 us; the launch traced here: 41.6 us
  starting transfers between devices  19 us (45%)
  waiting for transfers between devices  14.9 us (36%)
  Pallas kernels  4.82 us (12%)
  local copies, waits for them, and re-layouts  2.13 us (5%)
  between operations  0.74 us (2%)
    ppermute x6, waiting for transfers between devices, over_rep(): lax.ppermute(value, 'rep', list(enumerate(targets(name, step, reps))))  8.87 us
    ppermute x6, starting transfers between devices, over_rep(): lax.ppermute(value, 'rep', list(enumerate(targets(name, step, reps))))  8.85 us
    ppermute x6, starting transfers between devices, over_chips(): return lax.ppermute(value, 'rows', pairs)  8.58 us
    ppermute x6, waiting for transfers between devices, over_chips(): return lax.ppermute(value, 'rows', pairs)  4.42 us
    pallas_call x1, Pallas kernels, local(): pl.pallas_call(lambda *refs: plane_kernel(reps, chips, slot_count, *refs)...  2.19 us
    unnamed x13, local copies, waits for them, and re-layouts  2.13 us
    ppermute x9, waiting for transfers between devices, to_mate(): return lax.ppermute(value, 'rows', [(i, i ^ 1) for i in range(peers)])  1.6 us
    ppermute x9, starting transfers between devices, to_mate(): return lax.ppermute(value, 'rows', [(i, i ^ 1) for i in range(peers)])  1.6 us
  transfers between devices with their start and end apart: 21, of which 11 were waited for; matrix products, arithmetic and copies ran while one was open for 0% of the time, Pallas kernels for 4%

profile of v6, /device:TPU:0, one launch (start us, length us, event | category | flops | bytes accessed | tf_op | source)
XLA Modules:
  0.0 41.6 jit_solution(6275663276499673310)
XLA Ops:
  0.6 0.9 %constant_dynamic-update-slice_fusion.1 = bf16[256,256]{1,0:T(8,128)(2,1)S(1)} fusion(bf16[128,256]{1,0:T(8,128)(2,1)} %refs_2_.2), kind=kLoop, calls=%fused_computation.1 | loop fusion | bytes 131072
  1.6 3.0 %collective-permute-start.3 = (bf16[256,256]{1,0:T(8,128)(2,1)S(1)}, bf16[256,256]{1,0:T(8,128)(2,1)S(1)}, u32[]{:S(2)}, u32[]{:S(2)}) collective-permute-start(bf16[256,256]{1,0:T(8,128)(2,1)S(1)} %constant_dynamic-update-slice_fusion.refs_11_), channel_id=1, source_target_pairs={{0,8},{4,12},{8,0},{12,4},{16,24},{20,28},{24,16},{28,20},{1,9},{5... | collective-permute-start | bytes 393224 | tf_op jit(solution)/shard_map/ppermute | solution.py:345
  4.6 3.6 %collective-permute-start.1 = (bf16[128,256]{1,0:T(8,128)(2,1)S(1)}, bf16[128,256]{1,0:T(8,128)(2,1)S(1)}, u32[]{:S(2)}, u32[]{:S(2)}) collective-permute-start(bf16[128,256]{1,0:T(8,128)(2,1)S(1)} %copy-done.1), channel_id=1, source_target_pairs={{0,3},{1,2},{2,1},{3,0},{4,7},{5,6},{6,5},{7,4},{8,11},{9,10},{10,... | collective-permute-start | bytes 196616 | tf_op jit(solution)/shard_map/ppermute | solution.py:337
  8.2 0.8 %collective-permute-start.2 = (bf16[128,256]{1,0:T(8,128)(2,1)S(1)}, bf16[128,256]{1,0:T(8,128)(2,1)S(1)}, u32[]{:S(2)}, u32[]{:S(2)}) collective-permute-start(bf16[128,256]{1,0:T(8,128)(2,1)S(1)} %copy-done.1), channel_id=1, source_target_pairs={{0,2},{1,3},{2,0},{3,1},{4,6},{5,7},{6,4},{7,5},{8,10},{9,11},{10,... | collective-permute-start | bytes 196616 | tf_op jit(solution)/shard_map/ppermute | solution.py:337
  9.0 1.5 %collective-permute-start.5 = (bf16[256,256]{1,0:T(8,128)(2,1)S(1)}, bf16[256,256]{1,0:T(8,128)(2,1)S(1)}, u32[]{:S(2)}, u32[]{:S(2)}) collective-permute-start(bf16[256,256]{1,0:T(8,128)(2,1)S(1)} %constant_dynamic-update-slice_fusion.refs_11_), channel_id=1, source_target_pairs={{0,16},{4,20},{8,24},{12,28},{16,0},{20,4},{24,8},{28,12},{1,17},{... | collective-permute-start | bytes 393224 | tf_op jit(solution)/shard_map/ppermute | solution.py:345
  10.5 0.5 %collective-permute-start.4 = (bf16[256,256]{1,0:T(8,128)(2,1)S(1)}, bf16[256,256]{1,0:T(8,128)(2,1)S(1)}, u32[]{:S(2)}, u32[]{:S(2)}) collective-permute-start(bf16[256,256]{1,0:T(8,128)(2,1)S(1)} %collective-permute-done.3.refs_13_), channel_id=1, source_target_pairs={{0,16},{4,20},{8,24},{12,28},{16,0},{20,4},{24,8},{28,12},{1,17},{... | collective-permute-start | bytes 393224 | tf_op jit(solution)/shard_map/ppermute | solution.py:345
  11.0 1.2 %copy-done = bf16[1,1,4,8,128,128]{5,4,3,2,1,0:T(8,128)(2,1)S(1)} copy-done((bf16[1,1,4,8,128,128]{5,4,3,2,1,0:T(8,128)(2,1)S(1)}, bf16[1,1,4,8,128,128]{5,4,3,2,1,0:T(8,128)(2,1)}, u32[]{:S(2)}) %copy-start) | copy-done | bytes 1048600
  12.2 0.9 %inputs.1 = (bf16[4,256,128]{2,1,0:T(8,128)(2,1)S(1)}, f32[256,256]{1,0:T(8,128)S(1)}, bf16[256,128]{1,0:T(8,128)(2,1)S(1)}) custom-call(s32[8,24]{1,0:T(8,128)S(1)} %bitcast.4, s32[8,24]{1,0:T(8,128)S(1)} %bitcast.5, bf16[128,256]{1,0:T(8,128)(2,1)S(1)} %copy-done.1, bf16[4,8,128,128]{3,2,1,0:T(8,128)(2,1)S(1)} %bitcast.3), custom_call_target="tpu_custom_call" | custom-call | tf_op jit(solution)/shard_map/inputs/pallas_call | solution.py:352
  13.8 1.6 %collective-permute-start.10 = (bf16[256,256]{1,0:T(8,128)(2,1)S(1)}, bf16[256,256]{1,0:T(8,128)(2,1)S(1)}, u32[]{:S(2)}, u32[]{:S(2)}) collective-permute-start(bf16[256,256]{1,0:T(8,128)(2,1)S(1)} %partial.1.refs_3_), channel_id=1, source_target_pairs={{0,16},{4,20},{8,24},{12,28},{16,0},{20,4},{24,8},{28,12},{1,17},{... | collective-permute-start | bytes 393224 | tf_op jit(solution)/shard_map/ppermute | solution.py:345
  15.4 1.0 %collective-permute-start.9 = (bf16[256,256]{1,0:T(8,128)(2,1)S(1)}, bf16[256,256]{1,0:T(8,128)(2,1)S(1)}, u32[]{:S(2)}, u32[]{:S(2)}) collective-permute-start(bf16[256,256]{1,0:T(8,128)(2,1)S(1)} %partial.1.refs_3_), channel_id=1, source_target_pairs={{0,8},{4,12},{8,0},{12,4},{16,24},{20,28},{24,16},{28,20},{1,9},{5... | collective-permute-start | bytes 393224 | tf_op jit(solution)/shard_map/ppermute | solution.py:345
  16.4 1.0 %collective-permute-start.8 = (bf16[256,256]{1,0:T(8,128)(2,1)S(1)}, bf16[256,256]{1,0:T(8,128)(2,1)S(1)}, u32[]{:S(2)}, u32[]{:S(2)}) collective-permute-start(bf16[256,256]{1,0:T(8,128)(2,1)S(1)} %partial.1.refs_3_), channel_id=1, source_target_pairs={{0,24},{4,28},{8,16},{12,20},{16,8},{20,12},{24,0},{28,4},{1,25},{... | collective-permute-start | bytes 393224 | tf_op jit(solution)/shard_map/ppermute | solution.py:345
  17.4 0.5 %collective-permute-start.7 = (bf16[256,256]{1,0:T(8,128)(2,1)S(1)}, bf16[256,256]{1,0:T(8,128)(2,1)S(1)}, u32[]{:S(2)}, u32[]{:S(2)}) collective-permute-start(bf16[256,256]{1,0:T(8,128)(2,1)S(1)} %collective-permute-done.3.refs_13_), channel_id=1, source_target_pairs={{0,4},{4,0},{8,12},{12,8},{16,20},{20,16},{24,28},{28,24},{1,5},{5... | collective-permute-start | bytes 393224 | tf_op jit(solution)/shard_map/ppermute | solution.py:348
  17.9 2.4 %collective-permute-done.10.refs_6_ = bf16[256,256]{1,0:T(8,128)(2,1)S(1)} collective-permute-done((bf16[256,256]{1,0:T(8,128)(2,1)S(1)}, bf16[256,256]{1,0:T(8,128)(2,1)S(1)}, u32[]{:S(2)}, u32[]{:S(2)}) %collective-permute-start.10) | collective-permute-done | bytes 131104 | tf_op jit(solution)/shard_map/ppermute | solution.py:345
  20.2 0.7 %collective-permute-done.9.refs_5_ = bf16[256,256]{1,0:T(8,128)(2,1)S(1)} collective-permute-done((bf16[256,256]{1,0:T(8,128)(2,1)S(1)}, bf16[256,256]{1,0:T(8,128)(2,1)S(1)}, u32[]{:S(2)}, u32[]{:S(2)}) %collective-permute-start.9) | collective-permute-done | bytes 131104 | tf_op jit(solution)/shard_map/ppermute | solution.py:345
  20.9 1.4 %collective-permute-done.8.refs_4_ = bf16[256,256]{1,0:T(8,128)(2,1)S(1)} collective-permute-done((bf16[256,256]{1,0:T(8,128)(2,1)S(1)}, bf16[256,256]{1,0:T(8,128)(2,1)S(1)}, u32[]{:S(2)}, u32[]{:S(2)}) %collective-permute-start.8) | collective-permute-done | bytes 131104 | tf_op jit(solution)/shard_map/ppermute | solution.py:345
  22.3 0.5 %collective-permute-start.15 = (bf16[256,256]{1,0:T(8,128)(2,1)S(1)}, bf16[256,256]{1,0:T(8,128)(2,1)S(1)}, u32[]{:S(2)}, u32[]{:S(2)}) collective-permute-start(bf16[256,256]{1,0:T(8,128)(2,1)S(1)} %collective-permute-done.4.refs_12_), channel_id=1, source_target_pairs={{0,4},{4,0},{8,12},{12,8},{16,20},{20,16},{24,28},{28,24},{1,5},{5... | collective-permute-start | bytes 393224 | tf_op jit(solution)/shard_map/ppermute | solution.py:348
  22.9 0.4 %collective-permute-start.12 = (bf16[256,256]{1,0:T(8,128)(2,1)S(1)}, bf16[256,256]{1,0:T(8,128)(2,1)S(1)}, u32[]{:S(2)}, u32[]{:S(2)}) collective-permute-start(bf16[256,256]{1,0:T(8,128)(2,1)S(1)} %collective-permute-done.8.refs_4_), channel_id=1, source_target_pairs={{0,4},{4,0},{8,12},{12,8},{16,20},{20,16},{24,28},{28,24},{1,5},{5... | collective-permute-start | bytes 393224 | tf_op jit(solution)/shard_map/ppermute | solution.py:348
  24.3 2.2 %plane.1 = (bf16[128,256]{1,0:T(8,128)(2,1)}, f32[256,256]{1,0:T(8,128)S(1)}, bf16[256,256]{1,0:T(8,128)(2,1)S(1)}, bf16[256,256]{1,0:T(8,128)(2,1)S(1)}, bf16[256,256]{1,0:T(8,128)(2,1)S(1)}) custom-call(bf16[4,256,128]{2,1,0:T(8,128)(2,1)S(1)} %get-tuple-element.18.refs_0_, bf16[256,128]{1,0:T(8,128)(2,1)S(1)} %get-tuple-element.19.refs_1_, ...), custom_call_target="tpu_custom_call" | custom-call | tf_op jit(solution)/shard_map/plane/pallas_call | solution.py:396
  26.5 3.0 %collective-permute-start.17 = (bf16[256,256]{1,0:T(8,128)(2,1)S(1)}, bf16[256,256]{1,0:T(8,128)(2,1)S(1)}, u32[]{:S(2)}, u32[]{:S(2)}) collective-permute-start(bf16[256,256]{1,0:T(8,128)(2,1)S(1)} %get-tuple-element.30), channel_id=1, source_target_pairs={{0,3},{1,2},{2,0},{3,1},{4,7},{5,6},{6,4},{7,5},{8,11},{9,10},{10,... | collective-permute-start | bytes 393224 | tf_op jit(solution)/shard_map/ppermute | solution.py:337
  29.5 1.5 %collective-permute-start.19 = (bf16[256,256]{1,0:T(8,128)(2,1)S(1)}, bf16[256,256]{1,0:T(8,128)(2,1)S(1)}, u32[]{:S(2)}, u32[]{:S(2)}) collective-permute-start(bf16[256,256]{1,0:T(8,128)(2,1)S(1)} %get-tuple-element.32), channel_id=1, source_target_pairs={{0,1},{1,0},{2,3},{3,2},{4,5},{5,4},{6,7},{7,6},{8,9},{9,8},{10,11... | collective-permute-start | bytes 393224 | tf_op jit(solution)/shard_map/ppermute | solution.py:337
  31.0 8.4 %collective-permute-done.17.refs_1_.refs_0_ = bf16[256,256]{1,0:T(8,128)(2,1)S(1)} collective-permute-done((bf16[256,256]{1,0:T(8,128)(2,1)S(1)}, bf16[256,256]{1,0:T(8,128)(2,1)S(1)}, u32[]{:S(2)}, u32[]{:S(2)}) %collective-permute-start.17) | collective-permute-done | bytes 131104 | tf_op jit(solution)/shard_map/ppermute | solution.py:337
  39.7 0.7 %grad_x.1 = bf16[128,256]{1,0:T(8,128)(2,1)} custom-call(f32[256,256]{1,0:T(8,128)S(1)} %get-tuple-element.29.refs_0_.kept_ref, bf16[256,256]{1,0:T(8,128)(2,1)S(1)} %collective-permute-done.17.refs_1_.refs_0_, bf16[256,256]{1,0:T(8,128)(2,1)S(1)} %collective-permute-done.18.refs_2_.refs_1_, bf16[256,256]{1,0:T(8,128)(2,1)S(1)} %collective-permute-done.19.refs_3_.refs_2_), custom_call_target="tpu_custom_call" | custom-call | tf_op jit(solution)/shard_map/grad_x/pallas_call | solution.py:472
  40.3 0.6 %collective-permute-done.20.refs_1_ = bf16[128,256]{1,0:T(8,128)(2,1)S(1)} collective-permute-done((bf16[128,256]{1,0:T(8,128)(2,1)S(1)}, bf16[128,256]{1,0:T(8,128)(2,1)S(1)}, u32[]{:S(2)}, u32[]{:S(2)}) %collective-permute-start.20) | collective-permute-done | bytes 65568 | tf_op jit(solution)/shard_map/ppermute | solution.py:348
  40.9 0.7 %grad_w.1 = f32[256,256]{1,0:T(8,128)} custom-call(bf16[128,256]{1,0:T(8,128)(2,1)S(1)} %chunk.1.refs_0_, bf16[128,256]{1,0:T(8,128)(2,1)S(1)} %collective-permute-done.20.refs_1_), custom_call_target="tpu_custom_call" | custom-call | tf_op jit(solution)/shard_map/grad_w/pallas_call | solution.py:482
  (38 shorter events, 2.0 us)
Async XLA Ops:
  1.5 9.5 %copy-start.4 = (s32[1,1,8,24]{3,2,1,0:T(8,128)S(1)}, s32[1,1,8,24]{3,2,1,0:T(8,128)}, u32[]{:S(2)}) copy-start(s32[1,1,8,24]{3,2,1,0:T(8,128)} %param.10) | copy-start | bytes 2308
  1.6 9.4 %copy-start.3 = (s32[1,1,8,24]{3,2,1,0:T(8,128)S(1)}, s32[1,1,8,24]{3,2,1,0:T(8,128)}, u32[]{:S(2)}) copy-start(s32[1,1,8,24]{3,2,1,0:T(8,128)} %param.9) | copy-start | bytes 2308
  1.6 8.9 %collective-permute-start.3 = (bf16[256,256]{1,0:T(8,128)(2,1)S(1)}, bf16[256,256]{1,0:T(8,128)(2,1)S(1)}, u32[]{:S(2)}, u32[]{:S(2)}) collective-permute-start(bf16[256,256]{1,0:T(8,128)(2,1)S(1)} %constant_dynamic-update-slice_fusion.refs_11_), channel_id=1, source_target_pairs={{0,8},{4,12},{8,0},{12,4},{16,24},{20,28},{24,16},{28,20},{1,9},{5... | collective-permute-start | bytes 393224 | tf_op jit(solution)/shard_map/ppermute | solution.py:345
  4.6 8.6 %collective-permute-start.1 = (bf16[128,256]{1,0:T(8,128)(2,1)S(1)}, bf16[128,256]{1,0:T(8,128)(2,1)S(1)}, u32[]{:S(2)}, u32[]{:S(2)}) collective-permute-start(bf16[128,256]{1,0:T(8,128)(2,1)S(1)} %copy-done.1), channel_id=1, source_target_pairs={{0,3},{1,2},{2,1},{3,0},{4,7},{5,6},{6,5},{7,4},{8,11},{9,10},{10,... | collective-permute-start | bytes 196616 | tf_op jit(solution)/shard_map/ppermute | solution.py:337
  8.2 5.0 %collective-permute-start = (bf16[128,256]{1,0:T(8,128)(2,1)S(1)}, bf16[128,256]{1,0:T(8,128)(2,1)S(1)}, u32[]{:S(2)}, u32[]{:S(2)}) collective-permute-start(bf16[128,256]{1,0:T(8,128)(2,1)S(1)} %copy-done.1), channel_id=1, source_target_pairs={{0,1},{1,0},{2,3},{3,2},{4,5},{5,4},{6,7},{7,6},{8,9},{9,8},{10,11... | collective-permute-start | bytes 196616 | tf_op jit(solution)/shard_map/ppermute | solution.py:337
  8.2 5.4 %collective-permute-start.2 = (bf16[128,256]{1,0:T(8,128)(2,1)S(1)}, bf16[128,256]{1,0:T(8,128)(2,1)S(1)}, u32[]{:S(2)}, u32[]{:S(2)}) collective-permute-start(bf16[128,256]{1,0:T(8,128)(2,1)S(1)} %copy-done.1), channel_id=1, source_target_pairs={{0,2},{1,3},{2,0},{3,1},{4,6},{5,7},{6,4},{7,5},{8,10},{9,11},{10,... | collective-permute-start | bytes 196616 | tf_op jit(solution)/shard_map/ppermute | solution.py:337
  9.0 8.4 %collective-permute-start.5 = (bf16[256,256]{1,0:T(8,128)(2,1)S(1)}, bf16[256,256]{1,0:T(8,128)(2,1)S(1)}, u32[]{:S(2)}, u32[]{:S(2)}) collective-permute-start(bf16[256,256]{1,0:T(8,128)(2,1)S(1)} %constant_dynamic-update-slice_fusion.refs_11_), channel_id=1, source_target_pairs={{0,16},{4,20},{8,24},{12,28},{16,0},{20,4},{24,8},{28,12},{1,17},{... | collective-permute-start | bytes 393224 | tf_op jit(solution)/shard_map/ppermute | solution.py:345
  10.5 6.9 %collective-permute-start.4 = (bf16[256,256]{1,0:T(8,128)(2,1)S(1)}, bf16[256,256]{1,0:T(8,128)(2,1)S(1)}, u32[]{:S(2)}, u32[]{:S(2)}) collective-permute-start(bf16[256,256]{1,0:T(8,128)(2,1)S(1)} %collective-permute-done.3.refs_13_), channel_id=1, source_target_pairs={{0,16},{4,20},{8,24},{12,28},{16,0},{20,4},{24,8},{28,12},{1,17},{... | collective-permute-start | bytes 393224 | tf_op jit(solution)/shard_map/ppermute | solution.py:345
  13.5 10.8 %copy-start.2 = (bf16[256,256]{1,0:T(8,128)(2,1)S(1)}, bf16[256,256]{1,0:T(8,128)(2,1)}, u32[]{:S(2)}) copy-start(bf16[256,256]{1,0:T(8,128)(2,1)} %refs_2_.3) | copy-start | bytes 393220
  13.8 6.4 %collective-permute-start.10 = (bf16[256,256]{1,0:T(8,128)(2,1)S(1)}, bf16[256,256]{1,0:T(8,128)(2,1)S(1)}, u32[]{:S(2)}, u32[]{:S(2)}) collective-permute-start(bf16[256,256]{1,0:T(8,128)(2,1)S(1)} %partial.1.refs_3_), channel_id=1, source_target_pairs={{0,16},{4,20},{8,24},{12,28},{16,0},{20,4},{24,8},{28,12},{1,17},{... | collective-permute-start | bytes 393224 | tf_op jit(solution)/shard_map/ppermute | solution.py:345
  15.4 5.5 %collective-permute-start.9 = (bf16[256,256]{1,0:T(8,128)(2,1)S(1)}, bf16[256,256]{1,0:T(8,128)(2,1)S(1)}, u32[]{:S(2)}, u32[]{:S(2)}) collective-permute-start(bf16[256,256]{1,0:T(8,128)(2,1)S(1)} %partial.1.refs_3_), channel_id=1, source_target_pairs={{0,8},{4,12},{8,0},{12,4},{16,24},{20,28},{24,16},{28,20},{1,9},{5... | collective-permute-start | bytes 393224 | tf_op jit(solution)/shard_map/ppermute | solution.py:345
  16.4 5.9 %collective-permute-start.8 = (bf16[256,256]{1,0:T(8,128)(2,1)S(1)}, bf16[256,256]{1,0:T(8,128)(2,1)S(1)}, u32[]{:S(2)}, u32[]{:S(2)}) collective-permute-start(bf16[256,256]{1,0:T(8,128)(2,1)S(1)} %partial.1.refs_3_), channel_id=1, source_target_pairs={{0,24},{4,28},{8,16},{12,20},{16,8},{20,12},{24,0},{28,4},{1,25},{... | collective-permute-start | bytes 393224 | tf_op jit(solution)/shard_map/ppermute | solution.py:345
  17.3 4.9 %collective-permute-start.6 = (bf16[256,256]{1,0:T(8,128)(2,1)S(1)}, bf16[256,256]{1,0:T(8,128)(2,1)S(1)}, u32[]{:S(2)}, u32[]{:S(2)}) collective-permute-start(bf16[256,256]{1,0:T(8,128)(2,1)S(1)} %constant_dynamic-update-slice_fusion.refs_11_), channel_id=1, source_target_pairs={{0,4},{4,0},{8,12},{12,8},{16,20},{20,16},{24,28},{28,24},{1,5},{5... | collective-permute-start | bytes 393224 | tf_op jit(solution)/shard_map/ppermute | solution.py:348
  17.4 5.4 %collective-permute-start.7 = (bf16[256,256]{1,0:T(8,128)(2,1)S(1)}, bf16[256,256]{1,0:T(8,128)(2,1)S(1)}, u32[]{:S(2)}, u32[]{:S(2)}) collective-permute-start(bf16[256,256]{1,0:T(8,128)(2,1)S(1)} %collective-permute-done.3.refs_13_), channel_id=1, source_target_pairs={{0,4},{4,0},{8,12},{12,8},{16,20},{20,16},{24,28},{28,24},{1,5},{5... | collective-permute-start | bytes 393224 | tf_op jit(solution)/shard_map/ppermute | solution.py:348
  20.2 2.6 %collective-permute-start.11 = (bf16[256,256]{1,0:T(8,128)(2,1)S(1)}, bf16[256,256]{1,0:T(8,128)(2,1)S(1)}, u32[]{:S(2)}, u32[]{:S(2)}) collective-permute-start(bf16[256,256]{1,0:T(8,128)(2,1)S(1)} %partial.1.refs_3_), channel_id=1, source_target_pairs={{0,4},{4,0},{8,12},{12,8},{16,20},{20,16},{24,28},{28,24},{1,5},{5... | collective-permute-start | bytes 393224 | tf_op jit(solution)/shard_map/ppermute | solution.py:348
  20.9 2.4 %collective-permute-start.14 = (bf16[256,256]{1,0:T(8,128)(2,1)S(1)}, bf16[256,256]{1,0:T(8,128)(2,1)S(1)}, u32[]{:S(2)}, u32[]{:S(2)}) collective-permute-start(bf16[256,256]{1,0:T(8,128)(2,1)S(1)} %collective-permute-done.10.refs_6_), channel_id=1, source_target_pairs={{0,4},{4,0},{8,12},{12,8},{16,20},{20,16},{24,28},{28,24},{1,5},{5... | collective-permute-start | bytes 393224 | tf_op jit(solution)/shard_map/ppermute | solution.py:348
  22.3 1.3 %collective-permute-start.13 = (bf16[256,256]{1,0:T(8,128)(2,1)S(1)}, bf16[256,256]{1,0:T(8,128)(2,1)S(1)}, u32[]{:S(2)}, u32[]{:S(2)}) collective-permute-start(bf16[256,256]{1,0:T(8,128)(2,1)S(1)} %collective-permute-done.9.refs_5_), channel_id=1, source_target_pairs={{0,4},{4,0},{8,12},{12,8},{16,20},{20,16},{24,28},{28,24},{1,5},{5... | collective-permute-start | bytes 393224 | tf_op jit(solution)/shard_map/ppermute | solution.py:348
  22.3 1.5 %collective-permute-start.15 = (bf16[256,256]{1,0:T(8,128)(2,1)S(1)}, bf16[256,256]{1,0:T(8,128)(2,1)S(1)}, u32[]{:S(2)}, u32[]{:S(2)}) collective-permute-start(bf16[256,256]{1,0:T(8,128)(2,1)S(1)} %collective-permute-done.4.refs_12_), channel_id=1, source_target_pairs={{0,4},{4,0},{8,12},{12,8},{16,20},{20,16},{24,28},{28,24},{1,5},{5... | collective-permute-start | bytes 393224 | tf_op jit(solution)/shard_map/ppermute | solution.py:348
  22.8 1.3 %collective-permute-start.16 = (bf16[256,256]{1,0:T(8,128)(2,1)S(1)}, bf16[256,256]{1,0:T(8,128)(2,1)S(1)}, u32[]{:S(2)}, u32[]{:S(2)}) collective-permute-start(bf16[256,256]{1,0:T(8,128)(2,1)S(1)} %collective-permute-done.5.refs_14_), channel_id=1, source_target_pairs={{0,4},{4,0},{8,12},{12,8},{16,20},{20,16},{24,28},{28,24},{1,5},{5... | collective-permute-start | bytes 393224 | tf_op jit(solution)/shard_map/ppermute | solution.py:348
  22.9 1.5 %collective-permute-start.12 = (bf16[256,256]{1,0:T(8,128)(2,1)S(1)}, bf16[256,256]{1,0:T(8,128)(2,1)S(1)}, u32[]{:S(2)}, u32[]{:S(2)}) collective-permute-start(bf16[256,256]{1,0:T(8,128)(2,1)S(1)} %collective-permute-done.8.refs_4_), channel_id=1, source_target_pairs={{0,4},{4,0},{8,12},{12,8},{16,20},{20,16},{24,28},{28,24},{1,5},{5... | collective-permute-start | bytes 393224 | tf_op jit(solution)/shard_map/ppermute | solution.py:348
  26.5 12.9 %collective-permute-start.17 = (bf16[256,256]{1,0:T(8,128)(2,1)S(1)}, bf16[256,256]{1,0:T(8,128)(2,1)S(1)}, u32[]{:S(2)}, u32[]{:S(2)}) collective-permute-start(bf16[256,256]{1,0:T(8,128)(2,1)S(1)} %get-tuple-element.30), channel_id=1, source_target_pairs={{0,3},{1,2},{2,0},{3,1},{4,7},{5,6},{6,4},{7,5},{8,11},{9,10},{10,... | collective-permute-start | bytes 393224 | tf_op jit(solution)/shard_map/ppermute | solution.py:337
  29.5 9.9 %collective-permute-start.18 = (bf16[256,256]{1,0:T(8,128)(2,1)S(1)}, bf16[256,256]{1,0:T(8,128)(2,1)S(1)}, u32[]{:S(2)}, u32[]{:S(2)}) collective-permute-start(bf16[256,256]{1,0:T(8,128)(2,1)S(1)} %get-tuple-element.31), channel_id=1, source_target_pairs={{0,2},{1,3},{2,1},{3,0},{4,6},{5,7},{6,5},{7,4},{8,10},{9,11},{10,... | collective-permute-start | bytes 393224 | tf_op jit(solution)/shard_map/ppermute | solution.py:337
  29.5 10.0 %collective-permute-start.19 = (bf16[256,256]{1,0:T(8,128)(2,1)S(1)}, bf16[256,256]{1,0:T(8,128)(2,1)S(1)}, u32[]{:S(2)}, u32[]{:S(2)}) collective-permute-start(bf16[256,256]{1,0:T(8,128)(2,1)S(1)} %get-tuple-element.32), channel_id=1, source_target_pairs={{0,1},{1,0},{2,3},{3,2},{4,5},{5,4},{6,7},{7,6},{8,9},{9,8},{10,11... | collective-permute-start | bytes 393224 | tf_op jit(solution)/shard_map/ppermute | solution.py:337
  39.6 1.3 %collective-permute-start.20 = (bf16[128,256]{1,0:T(8,128)(2,1)S(1)}, bf16[128,256]{1,0:T(8,128)(2,1)S(1)}, u32[]{:S(2)}, u32[]{:S(2)}) collective-permute-start(bf16[128,256]{1,0:T(8,128)(2,1)S(1)} %chunk.1.refs_0_), channel_id=1, source_target_pairs={{0,4},{4,0},{8,12},{12,8},{16,20},{20,16},{24,28},{28,24},{1,5},{5... | collective-permute-start | bytes 196616 | tf_op jit(solution)/shard_map/ppermute | solution.py:348
  (3 other events, 5.2 us)

commit v7 on v6

--- a/solution.py
+++ b/solution.py
@@ -202,7 +202,8 @@
         pre_grad = cotangent.astype(F32) * sigmoid * (1.0 + preact * (1.0 - sigmoid))
         return (preact * sigmoid).astype(BF16), pre_grad.astype(BF16)
 
-    output_ref[...], own_grad = layer(aggregates[0], nodes[0][rows:, :])
+    output_ref[...] = aggregates[0]
+    _, own_grad = layer(aggregates[0], nodes[0][rows:, :])
     back_in = dot(own_grad, weight, 1, 1).astype(BF16)
     _, grads = layer(aggregated_ref[...], cotangent_ref[...])
     part = width // PAIR
@@ -217,6 +218,11 @@
         sends[step - 1][...] = jnp.concatenate([term, grad], axis=0).astype(BF16)
     own = dot(picked_ref[rep], back, 0, 0) + back_in.astype(F32)
     kept_ref[...] = jnp.concatenate([own, grad], axis=0)
+
+
+def output_kernel(aggregated_ref, weight_ref, output_ref):
+    preact = dot(aggregated_ref[...], weight_ref[...], 1, 0)
+    output_ref[...] = (preact * jax.nn.sigmoid(preact)).astype(BF16)
 
 
 def layer_kernel(chips, slot_count, *refs):
@@ -393,7 +399,7 @@
             )
         nodes += hops
         rows_in = direct + [to_mate(value) for value in direct]
-        output, kept, *sends = pl.pallas_call(
+        aggregated, kept, *sends = pl.pallas_call(
             lambda *refs: plane_kernel(reps, chips, slot_count, *refs),
             out_shape=(
                 jax.ShapeDtypeStruct((rows, width), BF16),
@@ -411,6 +417,15 @@
             compiler_params=params(slots),
             name="plane",
         )(picked, wanted, weight, *rows_in, *nodes)
+        output = pl.pallas_call(
+            output_kernel,
+            out_shape=jax.ShapeDtypeStruct((rows, width), BF16),
+            in_specs=whole(2),
+            out_specs=whole(1)[0],
+            compiler_params=params(slots),
+            name="output",
+        )(aggregated, weight)
+        kept, output = lax.optimization_barrier((kept, output))
     else:
         outgoing = partial((PAIR * PAD, width), chips)
         direct = [outgoing[0]] + [over_chips("B", outgoing[step], step) for step in range(1, chips)]

time: 41.8 us -> 41.4 us (level)
  waiting for transfers between devices: 14.9 us -> 14.1 us
    pallas_call x0 -> x1, Pallas kernels: none -> 0.8 us  [local(): pl.pallas_call(output_kernel, out_shape=jax.ShapeDtypeStruct((rows, width...]
    ppermute x6, waiting for transfers between devices: 8.87 us -> 8.08 us  [over_rep(): lax.ppermute(value, 'rep', list(enumerate(targets(name, step, reps))))]
    pallas_call x1, Pallas kernels: 2.19 us -> 1.65 us  [local(): pl.pallas_call(lambda *refs: plane_kernel(reps, chips, slot_count, *refs)...]
  transfers between devices with their start and end apart: 21 -> 21, of which waited for: 11 -> 11; matrix products, arithmetic and copies ran while one was open for 0% -> 0% of each run, Pallas kernels for 4% -> 6%
where the time goes in v7:
time: 41.4 us; the launch traced here: 41.2 us
  starting transfers between devices  19.1 us (46%)
  waiting for transfers between devices  14.1 us (34%)
  Pallas kernels  5.09 us (12%)
  local copies, waits for them, and re-layouts  2.13 us (5%)
  between operations  0.74 us (2%)
    ppermute x6, starting transfers between devices, over_rep(): lax.ppermute(value, 'rep', list(enumerate(targets(name, step, reps))))  8.89 us
    ppermute x6, starting transfers between devices, over_chips(): return lax.ppermute(value, 'rows', pairs)  8.58 us
    ppermute x6, waiting for transfers between devices, over_rep(): lax.ppermute(value, 'rep', list(enumerate(targets(name, step, reps))))  8.08 us
    ppermute x6, waiting for transfers between devices, over_chips(): return lax.ppermute(value, 'rows', pairs)  4.42 us
    unnamed x13, local copies, waits for them, and re-layouts  2.13 us
    pallas_call x1, Pallas kernels, local(): pl.pallas_call(lambda *refs: plane_kernel(reps, chips, slot_count, *refs)...  1.65 us
    ppermute x9, waiting for transfers between devices, to_mate(): return lax.ppermute(value, 'rows', [(i, i ^ 1) for i in range(peers)])  1.6 us
    ppermute x9, starting transfers between devices, to_mate(): return lax.ppermute(value, 'rows', [(i, i ^ 1) for i in range(peers)])  1.6 us
  transfers between devices with their start and end apart: 21, of which 11 were waited for; matrix products, arithmetic and copies ran while one was open for 0% of the time, Pallas kernels for 6%

profile of v7, /device:TPU:0, one launch (start us, length us, event | category | flops | bytes accessed | tf_op | source)
XLA Modules:
  0.0 41.2 jit_solution(9359627749486520207)
XLA Ops:
  0.6 0.9 %constant_dynamic-update-slice_fusion.1 = bf16[256,256]{1,0:T(8,128)(2,1)S(1)} fusion(bf16[128,256]{1,0:T(8,128)(2,1)} %refs_2_.2), kind=kLoop, calls=%fused_computation.1 | loop fusion | bytes 131072
  1.6 3.0 %collective-permute-start.3 = (bf16[256,256]{1,0:T(8,128)(2,1)S(1)}, bf16[256,256]{1,0:T(8,128)(2,1)S(1)}, u32[]{:S(2)}, u32[]{:S(2)}) collective-permute-start(bf16[256,256]{1,0:T(8,128)(2,1)S(1)} %constant_dynamic-update-slice_fusion.refs_11_), channel_id=1, source_target_pairs={{0,8},{4,12},{8,0},{12,4},{16,24},{20,28},{24,16},{28,20},{1,9},{5... | collective-permute-start | bytes 393224 | tf_op jit(solution)/shard_map/ppermute | solution.py:351
  4.6 3.6 %collective-permute-start.1 = (bf16[128,256]{1,0:T(8,128)(2,1)S(1)}, bf16[128,256]{1,0:T(8,128)(2,1)S(1)}, u32[]{:S(2)}, u32[]{:S(2)}) collective-permute-start(bf16[128,256]{1,0:T(8,128)(2,1)S(1)} %copy-done.2), channel_id=1, source_target_pairs={{0,3},{1,2},{2,1},{3,0},{4,7},{5,6},{6,5},{7,4},{8,11},{9,10},{10,... | collective-permute-start | bytes 196616 | tf_op jit(solution)/shard_map/ppermute | solution.py:343
  8.2 0.8 %collective-permute-start.2 = (bf16[128,256]{1,0:T(8,128)(2,1)S(1)}, bf16[128,256]{1,0:T(8,128)(2,1)S(1)}, u32[]{:S(2)}, u32[]{:S(2)}) collective-permute-start(bf16[128,256]{1,0:T(8,128)(2,1)S(1)} %copy-done.2), channel_id=1, source_target_pairs={{0,2},{1,3},{2,0},{3,1},{4,6},{5,7},{6,4},{7,5},{8,10},{9,11},{10,... | collective-permute-start | bytes 196616 | tf_op jit(solution)/shard_map/ppermute | solution.py:343
  9.0 1.5 %collective-permute-start.5 = (bf16[256,256]{1,0:T(8,128)(2,1)S(1)}, bf16[256,256]{1,0:T(8,128)(2,1)S(1)}, u32[]{:S(2)}, u32[]{:S(2)}) collective-permute-start(bf16[256,256]{1,0:T(8,128)(2,1)S(1)} %constant_dynamic-update-slice_fusion.refs_11_), channel_id=1, source_target_pairs={{0,16},{4,20},{8,24},{12,28},{16,0},{20,4},{24,8},{28,12},{1,17},{... | collective-permute-start | bytes 393224 | tf_op jit(solution)/shard_map/ppermute | solution.py:351
  10.5 0.5 %collective-permute-start.4 = (bf16[256,256]{1,0:T(8,128)(2,1)S(1)}, bf16[256,256]{1,0:T(8,128)(2,1)S(1)}, u32[]{:S(2)}, u32[]{:S(2)}) collective-permute-start(bf16[256,256]{1,0:T(8,128)(2,1)S(1)} %collective-permute-done.3.refs_13_), channel_id=1, source_target_pairs={{0,16},{4,20},{8,24},{12,28},{16,0},{20,4},{24,8},{28,12},{1,17},{... | collective-permute-start | bytes 393224 | tf_op jit(solution)/shard_map/ppermute | solution.py:351
  11.0 1.2 %copy-done = bf16[1,1,4,8,128,128]{5,4,3,2,1,0:T(8,128)(2,1)S(1)} copy-done((bf16[1,1,4,8,128,128]{5,4,3,2,1,0:T(8,128)(2,1)S(1)}, bf16[1,1,4,8,128,128]{5,4,3,2,1,0:T(8,128)(2,1)}, u32[]{:S(2)}) %copy-start) | copy-done | bytes 1048600
  12.2 0.9 %inputs.1 = (bf16[4,256,128]{2,1,0:T(8,128)(2,1)S(1)}, f32[256,256]{1,0:T(8,128)S(1)}, bf16[256,128]{1,0:T(8,128)(2,1)S(1)}) custom-call(s32[8,24]{1,0:T(8,128)S(1)} %bitcast.4, s32[8,24]{1,0:T(8,128)S(1)} %bitcast.5, bf16[128,256]{1,0:T(8,128)(2,1)S(1)} %copy-done.2, bf16[4,8,128,128]{3,2,1,0:T(8,128)(2,1)S(1)} %bitcast.3), custom_call_target="tpu_custom_call" | custom-call | tf_op jit(solution)/shard_map/inputs/pallas_call | solution.py:358
  13.8 1.6 %collective-permute-start.10 = (bf16[256,256]{1,0:T(8,128)(2,1)S(1)}, bf16[256,256]{1,0:T(8,128)(2,1)S(1)}, u32[]{:S(2)}, u32[]{:S(2)}) collective-permute-start(bf16[256,256]{1,0:T(8,128)(2,1)S(1)} %partial.1.refs_3_), channel_id=1, source_target_pairs={{0,16},{4,20},{8,24},{12,28},{16,0},{20,4},{24,8},{28,12},{1,17},{... | collective-permute-start | bytes 393224 | tf_op jit(solution)/shard_map/ppermute | solution.py:351
  15.4 1.0 %collective-permute-start.9 = (bf16[256,256]{1,0:T(8,128)(2,1)S(1)}, bf16[256,256]{1,0:T(8,128)(2,1)S(1)}, u32[]{:S(2)}, u32[]{:S(2)}) collective-permute-start(bf16[256,256]{1,0:T(8,128)(2,1)S(1)} %partial.1.refs_3_), channel_id=1, source_target_pairs={{0,8},{4,12},{8,0},{12,4},{16,24},{20,28},{24,16},{28,20},{1,9},{5... | collective-permute-start | bytes 393224 | tf_op jit(solution)/shard_map/ppermute | solution.py:351
  16.4 1.0 %collective-permute-start.8 = (bf16[256,256]{1,0:T(8,128)(2,1)S(1)}, bf16[256,256]{1,0:T(8,128)(2,1)S(1)}, u32[]{:S(2)}, u32[]{:S(2)}) collective-permute-start(bf16[256,256]{1,0:T(8,128)(2,1)S(1)} %partial.1.refs_3_), channel_id=1, source_target_pairs={{0,24},{4,28},{8,16},{12,20},{16,8},{20,12},{24,0},{28,4},{1,25},{... | collective-permute-start | bytes 393224 | tf_op jit(solution)/shard_map/ppermute | solution.py:351
  17.4 0.5 %collective-permute-start.7 = (bf16[256,256]{1,0:T(8,128)(2,1)S(1)}, bf16[256,256]{1,0:T(8,128)(2,1)S(1)}, u32[]{:S(2)}, u32[]{:S(2)}) collective-permute-start(bf16[256,256]{1,0:T(8,128)(2,1)S(1)} %collective-permute-done.3.refs_13_), channel_id=1, source_target_pairs={{0,4},{4,0},{8,12},{12,8},{16,20},{20,16},{24,28},{28,24},{1,5},{5... | collective-permute-start | bytes 393224 | tf_op jit(solution)/shard_map/ppermute | solution.py:354
  17.9 2.4 %collective-permute-done.10.refs_6_ = bf16[256,256]{1,0:T(8,128)(2,1)S(1)} collective-permute-done((bf16[256,256]{1,0:T(8,128)(2,1)S(1)}, bf16[256,256]{1,0:T(8,128)(2,1)S(1)}, u32[]{:S(2)}, u32[]{:S(2)}) %collective-permute-start.10) | collective-permute-done | bytes 131104 | tf_op jit(solution)/shard_map/ppermute | solution.py:351
  20.2 0.7 %collective-permute-done.9.refs_5_ = bf16[256,256]{1,0:T(8,128)(2,1)S(1)} collective-permute-done((bf16[256,256]{1,0:T(8,128)(2,1)S(1)}, bf16[256,256]{1,0:T(8,128)(2,1)S(1)}, u32[]{:S(2)}, u32[]{:S(2)}) %collective-permute-start.9) | collective-permute-done | bytes 131104 | tf_op jit(solution)/shard_map/ppermute | solution.py:351
  20.9 1.4 %collective-permute-done.8.refs_4_ = bf16[256,256]{1,0:T(8,128)(2,1)S(1)} collective-permute-done((bf16[256,256]{1,0:T(8,128)(2,1)S(1)}, bf16[256,256]{1,0:T(8,128)(2,1)S(1)}, u32[]{:S(2)}, u32[]{:S(2)}) %collective-permute-start.8) | collective-permute-done | bytes 131104 | tf_op jit(solution)/shard_map/ppermute | solution.py:351
  22.3 0.5 %collective-permute-start.15 = (bf16[256,256]{1,0:T(8,128)(2,1)S(1)}, bf16[256,256]{1,0:T(8,128)(2,1)S(1)}, u32[]{:S(2)}, u32[]{:S(2)}) collective-permute-start(bf16[256,256]{1,0:T(8,128)(2,1)S(1)} %collective-permute-done.4.refs_12_), channel_id=1, source_target_pairs={{0,4},{4,0},{8,12},{12,8},{16,20},{20,16},{24,28},{28,24},{1,5},{5... | collective-permute-start | bytes 393224 | tf_op jit(solution)/shard_map/ppermute | solution.py:354
  24.3 1.6 %plane.1 = (bf16[128,256]{1,0:T(8,128)(2,1)S(1)}, f32[256,256]{1,0:T(8,128)S(1)}, bf16[256,256]{1,0:T(8,128)(2,1)S(1)}, bf16[256,256]{1,0:T(8,128)(2,1)S(1)}, bf16[256,256]{1,0:T(8,128)(2,1)S(1)}) custom-call(bf16[4,256,128]{2,1,0:T(8,128)(2,1)S(1)} %get-tuple-element.20.refs_0_, bf16[256,128]{1,0:T(8,128)(2,1)S(1)} %get-tuple-element.21.refs_1_, ...), custom_call_target="tpu_custom_call" | custom-call | tf_op jit(solution)/shard_map/plane/pallas_call | solution.py:402
  26.0 3.0 %collective-permute-start.17 = (bf16[256,256]{1,0:T(8,128)(2,1)S(1)}, bf16[256,256]{1,0:T(8,128)(2,1)S(1)}, u32[]{:S(2)}, u32[]{:S(2)}) collective-permute-start(bf16[256,256]{1,0:T(8,128)(2,1)S(1)} %get-tuple-element.34), channel_id=1, source_target_pairs={{0,3},{1,2},{2,0},{3,1},{4,7},{5,6},{6,4},{7,5},{8,11},{9,10},{10,... | collective-permute-start | bytes 393224 | tf_op jit(solution)/shard_map/ppermute | solution.py:343
  29.0 1.5 %collective-permute-start.19 = (bf16[256,256]{1,0:T(8,128)(2,1)S(1)}, bf16[256,256]{1,0:T(8,128)(2,1)S(1)}, u32[]{:S(2)}, u32[]{:S(2)}) collective-permute-start(bf16[256,256]{1,0:T(8,128)(2,1)S(1)} %get-tuple-element.36), channel_id=1, source_target_pairs={{0,1},{1,0},{2,3},{3,2},{4,5},{5,4},{6,7},{7,6},{8,9},{9,8},{10,11... | collective-permute-start | bytes 393224 | tf_op jit(solution)/shard_map/ppermute | solution.py:343
  30.5 0.8 %output.1 = bf16[128,256]{1,0:T(8,128)(2,1)} custom-call(bf16[128,256]{1,0:T(8,128)(2,1)S(1)} %get-tuple-element.31.aggregated_ref, bf16[256,256]{1,0:T(8,128)(2,1)S(1)} %copy-done.1), custom_call_target="tpu_custom_call" | custom-call | tf_op jit(solution)/shard_map/output/pallas_call | solution.py:420
  31.3 7.6 %collective-permute-done.17.refs_1_.refs_0_ = bf16[256,256]{1,0:T(8,128)(2,1)S(1)} collective-permute-done((bf16[256,256]{1,0:T(8,128)(2,1)S(1)}, bf16[256,256]{1,0:T(8,128)(2,1)S(1)}, u32[]{:S(2)}, u32[]{:S(2)}) %collective-permute-start.17) | collective-permute-done | bytes 131104 | tf_op jit(solution)/shard_map/ppermute | solution.py:343
  39.2 0.7 %grad_x.1 = bf16[128,256]{1,0:T(8,128)(2,1)} custom-call(f32[256,256]{1,0:T(8,128)S(1)} %get-tuple-element.33.refs_0_.kept_ref, bf16[256,256]{1,0:T(8,128)(2,1)S(1)} %collective-permute-done.17.refs_1_.refs_0_, bf16[256,256]{1,0:T(8,128)(2,1)S(1)} %collective-permute-done.18.refs_2_.refs_1_, bf16[256,256]{1,0:T(8,128)(2,1)S(1)} %collective-permute-done.19.refs_3_.refs_2_), custom_call_target="tpu_custom_call" | custom-call | tf_op jit(solution)/shard_map/grad_x/pallas_call | solution.py:487
  39.8 0.6 %collective-permute-done.20.refs_1_ = bf16[128,256]{1,0:T(8,128)(2,1)S(1)} collective-permute-done((bf16[128,256]{1,0:T(8,128)(2,1)S(1)}, bf16[128,256]{1,0:T(8,128)(2,1)S(1)}, u32[]{:S(2)}, u32[]{:S(2)}) %collective-permute-start.20) | collective-permute-done | bytes 65568 | tf_op jit(solution)/shard_map/ppermute | solution.py:354
  40.4 0.7 %grad_w.1 = f32[256,256]{1,0:T(8,128)} custom-call(bf16[128,256]{1,0:T(8,128)(2,1)S(1)} %chunk.1.refs_0_, bf16[128,256]{1,0:T(8,128)(2,1)S(1)} %collective-permute-done.20.refs_1_), custom_call_target="tpu_custom_call" | custom-call | tf_op jit(solution)/shard_map/grad_w/pallas_call | solution.py:497
  (39 shorter events, 2.4 us)
Async XLA Ops:
  1.5 9.5 %copy-start.4 = (s32[1,1,8,24]{3,2,1,0:T(8,128)S(1)}, s32[1,1,8,24]{3,2,1,0:T(8,128)}, u32[]{:S(2)}) copy-start(s32[1,1,8,24]{3,2,1,0:T(8,128)} %param.10) | copy-start | bytes 2308
  1.6 9.4 %copy-start.3 = (s32[1,1,8,24]{3,2,1,0:T(8,128)S(1)}, s32[1,1,8,24]{3,2,1,0:T(8,128)}, u32[]{:S(2)}) copy-start(s32[1,1,8,24]{3,2,1,0:T(8,128)} %param.9) | copy-start | bytes 2308
  1.6 8.9 %collective-permute-start.3 = (bf16[256,256]{1,0:T(8,128)(2,1)S(1)}, bf16[256,256]{1,0:T(8,128)(2,1)S(1)}, u32[]{:S(2)}, u32[]{:S(2)}) collective-permute-start(bf16[256,256]{1,0:T(8,128)(2,1)S(1)} %constant_dynamic-update-slice_fusion.refs_11_), channel_id=1, source_target_pairs={{0,8},{4,12},{8,0},{12,4},{16,24},{20,28},{24,16},{28,20},{1,9},{5... | collective-permute-start | bytes 393224 | tf_op jit(solution)/shard_map/ppermute | solution.py:351
  4.6 8.6 %collective-permute-start.1 = (bf16[128,256]{1,0:T(8,128)(2,1)S(1)}, bf16[128,256]{1,0:T(8,128)(2,1)S(1)}, u32[]{:S(2)}, u32[]{:S(2)}) collective-permute-start(bf16[128,256]{1,0:T(8,128)(2,1)S(1)} %copy-done.2), channel_id=1, source_target_pairs={{0,3},{1,2},{2,1},{3,0},{4,7},{5,6},{6,5},{7,4},{8,11},{9,10},{10,... | collective-permute-start | bytes 196616 | tf_op jit(solution)/shard_map/ppermute | solution.py:343
  8.2 5.0 %collective-permute-start = (bf16[128,256]{1,0:T(8,128)(2,1)S(1)}, bf16[128,256]{1,0:T(8,128)(2,1)S(1)}, u32[]{:S(2)}, u32[]{:S(2)}) collective-permute-start(bf16[128,256]{1,0:T(8,128)(2,1)S(1)} %copy-done.2), channel_id=1, source_target_pairs={{0,1},{1,0},{2,3},{3,2},{4,5},{5,4},{6,7},{7,6},{8,9},{9,8},{10,11... | collective-permute-start | bytes 196616 | tf_op jit(solution)/shard_map/ppermute | solution.py:343
  8.2 5.4 %collective-permute-start.2 = (bf16[128,256]{1,0:T(8,128)(2,1)S(1)}, bf16[128,256]{1,0:T(8,128)(2,1)S(1)}, u32[]{:S(2)}, u32[]{:S(2)}) collective-permute-start(bf16[128,256]{1,0:T(8,128)(2,1)S(1)} %copy-done.2), channel_id=1, source_target_pairs={{0,2},{1,3},{2,0},{3,1},{4,6},{5,7},{6,4},{7,5},{8,10},{9,11},{10,... | collective-permute-start | bytes 196616 | tf_op jit(solution)/shard_map/ppermute | solution.py:343
  9.0 8.4 %collective-permute-start.5 = (bf16[256,256]{1,0:T(8,128)(2,1)S(1)}, bf16[256,256]{1,0:T(8,128)(2,1)S(1)}, u32[]{:S(2)}, u32[]{:S(2)}) collective-permute-start(bf16[256,256]{1,0:T(8,128)(2,1)S(1)} %constant_dynamic-update-slice_fusion.refs_11_), channel_id=1, source_target_pairs={{0,16},{4,20},{8,24},{12,28},{16,0},{20,4},{24,8},{28,12},{1,17},{... | collective-permute-start | bytes 393224 | tf_op jit(solution)/shard_map/ppermute | solution.py:351
  10.5 6.9 %collective-permute-start.4 = (bf16[256,256]{1,0:T(8,128)(2,1)S(1)}, bf16[256,256]{1,0:T(8,128)(2,1)S(1)}, u32[]{:S(2)}, u32[]{:S(2)}) collective-permute-start(bf16[256,256]{1,0:T(8,128)(2,1)S(1)} %collective-permute-done.3.refs_13_), channel_id=1, source_target_pairs={{0,16},{4,20},{8,24},{12,28},{16,0},{20,4},{24,8},{28,12},{1,17},{... | collective-permute-start | bytes 393224 | tf_op jit(solution)/shard_map/ppermute | solution.py:351
  13.5 10.8 %copy-start.1 = (bf16[256,256]{1,0:T(8,128)(2,1)S(1)}, bf16[256,256]{1,0:T(8,128)(2,1)}, u32[]{:S(2)}) copy-start(bf16[256,256]{1,0:T(8,128)(2,1)} %weight_ref.1) | copy-start | bytes 393220
  13.8 6.4 %collective-permute-start.10 = (bf16[256,256]{1,0:T(8,128)(2,1)S(1)}, bf16[256,256]{1,0:T(8,128)(2,1)S(1)}, u32[]{:S(2)}, u32[]{:S(2)}) collective-permute-start(bf16[256,256]{1,0:T(8,128)(2,1)S(1)} %partial.1.refs_3_), channel_id=1, source_target_pairs={{0,16},{4,20},{8,24},{12,28},{16,0},{20,4},{24,8},{28,12},{1,17},{... | collective-permute-start | bytes 393224 | tf_op jit(solution)/shard_map/ppermute | solution.py:351
  15.4 5.5 %collective-permute-start.9 = (bf16[256,256]{1,0:T(8,128)(2,1)S(1)}, bf16[256,256]{1,0:T(8,128)(2,1)S(1)}, u32[]{:S(2)}, u32[]{:S(2)}) collective-permute-start(bf16[256,256]{1,0:T(8,128)(2,1)S(1)} %partial.1.refs_3_), channel_id=1, source_target_pairs={{0,8},{4,12},{8,0},{12,4},{16,24},{20,28},{24,16},{28,20},{1,9},{5... | collective-permute-start | bytes 393224 | tf_op jit(solution)/shard_map/ppermute | solution.py:351
  16.4 5.9 %collective-permute-start.8 = (bf16[256,256]{1,0:T(8,128)(2,1)S(1)}, bf16[256,256]{1,0:T(8,128)(2,1)S(1)}, u32[]{:S(2)}, u32[]{:S(2)}) collective-permute-start(bf16[256,256]{1,0:T(8,128)(2,1)S(1)} %partial.1.refs_3_), channel_id=1, source_target_pairs={{0,24},{4,28},{8,16},{12,20},{16,8},{20,12},{24,0},{28,4},{1,25},{... | collective-permute-start | bytes 393224 | tf_op jit(solution)/shard_map/ppermute | solution.py:351
  17.3 4.9 %collective-permute-start.6 = (bf16[256,256]{1,0:T(8,128)(2,1)S(1)}, bf16[256,256]{1,0:T(8,128)(2,1)S(1)}, u32[]{:S(2)}, u32[]{:S(2)}) collective-permute-start(bf16[256,256]{1,0:T(8,128)(2,1)S(1)} %constant_dynamic-update-slice_fusion.refs_11_), channel_id=1, source_target_pairs={{0,4},{4,0},{8,12},{12,8},{16,20},{20,16},{24,28},{28,24},{1,5},{5... | collective-permute-start | bytes 393224 | tf_op jit(solution)/shard_map/ppermute | solution.py:354
  17.4 5.4 %collective-permute-start.7 = (bf16[256,256]{1,0:T(8,128)(2,1)S(1)}, bf16[256,256]{1,0:T(8,128)(2,1)S(1)}, u32[]{:S(2)}, u32[]{:S(2)}) collective-permute-start(bf16[256,256]{1,0:T(8,128)(2,1)S(1)} %collective-permute-done.3.refs_13_), channel_id=1, source_target_pairs={{0,4},{4,0},{8,12},{12,8},{16,20},{20,16},{24,28},{28,24},{1,5},{5... | collective-permute-start | bytes 393224 | tf_op jit(solution)/shard_map/ppermute | solution.py:354
  20.2 2.6 %collective-permute-start.11 = (bf16[256,256]{1,0:T(8,128)(2,1)S(1)}, bf16[256,256]{1,0:T(8,128)(2,1)S(1)}, u32[]{:S(2)}, u32[]{:S(2)}) collective-permute-start(bf16[256,256]{1,0:T(8,128)(2,1)S(1)} %partial.1.refs_3_), channel_id=1, source_target_pairs={{0,4},{4,0},{8,12},{12,8},{16,20},{20,16},{24,28},{28,24},{1,5},{5... | collective-permute-start | bytes 393224 | tf_op jit(solution)/shard_map/ppermute | solution.py:354
  20.9 2.4 %collective-permute-start.14 = (bf16[256,256]{1,0:T(8,128)(2,1)S(1)}, bf16[256,256]{1,0:T(8,128)(2,1)S(1)}, u32[]{:S(2)}, u32[]{:S(2)}) collective-permute-start(bf16[256,256]{1,0:T(8,128)(2,1)S(1)} %collective-permute-done.10.refs_6_), channel_id=1, source_target_pairs={{0,4},{4,0},{8,12},{12,8},{16,20},{20,16},{24,28},{28,24},{1,5},{5... | collective-permute-start | bytes 393224 | tf_op jit(solution)/shard_map/ppermute | solution.py:354
  22.3 1.3 %collective-permute-start.13 = (bf16[256,256]{1,0:T(8,128)(2,1)S(1)}, bf16[256,256]{1,0:T(8,128)(2,1)S(1)}, u32[]{:S(2)}, u32[]{:S(2)}) collective-permute-start(bf16[256,256]{1,0:T(8,128)(2,1)S(1)} %collective-permute-done.9.refs_5_), channel_id=1, source_target_pairs={{0,4},{4,0},{8,12},{12,8},{16,20},{20,16},{24,28},{28,24},{1,5},{5... | collective-permute-start | bytes 393224 | tf_op jit(solution)/shard_map/ppermute | solution.py:354
  22.3 1.5 %collective-permute-start.15 = (bf16[256,256]{1,0:T(8,128)(2,1)S(1)}, bf16[256,256]{1,0:T(8,128)(2,1)S(1)}, u32[]{:S(2)}, u32[]{:S(2)}) collective-permute-start(bf16[256,256]{1,0:T(8,128)(2,1)S(1)} %collective-permute-done.4.refs_12_), channel_id=1, source_target_pairs={{0,4},{4,0},{8,12},{12,8},{16,20},{20,16},{24,28},{28,24},{1,5},{5... | collective-permute-start | bytes 393224 | tf_op jit(solution)/shard_map/ppermute | solution.py:354
  22.8 1.3 %collective-permute-start.16 = (bf16[256,256]{1,0:T(8,128)(2,1)S(1)}, bf16[256,256]{1,0:T(8,128)(2,1)S(1)}, u32[]{:S(2)}, u32[]{:S(2)}) collective-permute-start(bf16[256,256]{1,0:T(8,128)(2,1)S(1)} %collective-permute-done.5.refs_14_), channel_id=1, source_target_pairs={{0,4},{4,0},{8,12},{12,8},{16,20},{20,16},{24,28},{28,24},{1,5},{5... | collective-permute-start | bytes 393224 | tf_op jit(solution)/shard_map/ppermute | solution.py:354
  22.9 1.5 %collective-permute-start.12 = (bf16[256,256]{1,0:T(8,128)(2,1)S(1)}, bf16[256,256]{1,0:T(8,128)(2,1)S(1)}, u32[]{:S(2)}, u32[]{:S(2)}) collective-permute-start(bf16[256,256]{1,0:T(8,128)(2,1)S(1)} %collective-permute-done.8.refs_4_), channel_id=1, source_target_pairs={{0,4},{4,0},{8,12},{12,8},{16,20},{20,16},{24,28},{28,24},{1,5},{5... | collective-permute-start | bytes 393224 | tf_op jit(solution)/shard_map/ppermute | solution.py:354
  26.0 12.9 %collective-permute-start.17 = (bf16[256,256]{1,0:T(8,128)(2,1)S(1)}, bf16[256,256]{1,0:T(8,128)(2,1)S(1)}, u32[]{:S(2)}, u32[]{:S(2)}) collective-permute-start(bf16[256,256]{1,0:T(8,128)(2,1)S(1)} %get-tuple-element.34), channel_id=1, source_target_pairs={{0,3},{1,2},{2,0},{3,1},{4,7},{5,6},{6,4},{7,5},{8,11},{9,10},{10,... | collective-permute-start | bytes 393224 | tf_op jit(solution)/shard_map/ppermute | solution.py:343
  29.0 9.9 %collective-permute-start.18 = (bf16[256,256]{1,0:T(8,128)(2,1)S(1)}, bf16[256,256]{1,0:T(8,128)(2,1)S(1)}, u32[]{:S(2)}, u32[]{:S(2)}) collective-permute-start(bf16[256,256]{1,0:T(8,128)(2,1)S(1)} %get-tuple-element.35), channel_id=1, source_target_pairs={{0,2},{1,3},{2,1},{3,0},{4,6},{5,7},{6,5},{7,4},{8,10},{9,11},{10,... | collective-permute-start | bytes 393224 | tf_op jit(solution)/shard_map/ppermute | solution.py:343
  29.0 10.0 %collective-permute-start.19 = (bf16[256,256]{1,0:T(8,128)(2,1)S(1)}, bf16[256,256]{1,0:T(8,128)(2,1)S(1)}, u32[]{:S(2)}, u32[]{:S(2)}) collective-permute-start(bf16[256,256]{1,0:T(8,128)(2,1)S(1)} %get-tuple-element.36), channel_id=1, source_target_pairs={{0,1},{1,0},{2,3},{3,2},{4,5},{5,4},{6,7},{7,6},{8,9},{9,8},{10,11... | collective-permute-start | bytes 393224 | tf_op jit(solution)/shard_map/ppermute | solution.py:343
  39.1 1.3 %collective-permute-start.20 = (bf16[128,256]{1,0:T(8,128)(2,1)S(1)}, bf16[128,256]{1,0:T(8,128)(2,1)S(1)}, u32[]{:S(2)}, u32[]{:S(2)}) collective-permute-start(bf16[128,256]{1,0:T(8,128)(2,1)S(1)} %chunk.1.refs_0_), channel_id=1, source_target_pairs={{0,4},{4,0},{8,12},{12,8},{16,20},{20,16},{24,28},{28,24},{1,5},{5... | collective-permute-start | bytes 196616 | tf_op jit(solution)/shard_map/ppermute | solution.py:354
  (3 other events, 5.2 us)

commit v8 on v6

--- a/solution.py
+++ b/solution.py
@@ -202,8 +202,7 @@
         pre_grad = cotangent.astype(F32) * sigmoid * (1.0 + preact * (1.0 - sigmoid))
         return (preact * sigmoid).astype(BF16), pre_grad.astype(BF16)
 
-    output_ref[...], own_grad = layer(aggregates[0], nodes[0][rows:, :])
-    back_in = dot(own_grad, weight, 1, 1).astype(BF16)
+    output_ref[...] = aggregates[0]
     _, grads = layer(aggregated_ref[...], cotangent_ref[...])
     part = width // PAIR
     columns = aggregated_ref[:, :part]
@@ -215,8 +214,17 @@
     for step in range(1, reps):
         term = dot(picked_ref[target_of("D", rep, step, reps)], back, 0, 0)
         sends[step - 1][...] = jnp.concatenate([term, grad], axis=0).astype(BF16)
-    own = dot(picked_ref[rep], back, 0, 0) + back_in.astype(F32)
+    own = dot(picked_ref[rep], back, 0, 0)
     kept_ref[...] = jnp.concatenate([own, grad], axis=0)
+
+
+def output_kernel(aggregated_ref, cotangent_ref, weight_ref, output_ref, back_ref):
+    weight = weight_ref[...]
+    preact = dot(aggregated_ref[...], weight, 1, 0)
+    sigmoid = jax.nn.sigmoid(preact)
+    output_ref[...] = (preact * sigmoid).astype(BF16)
+    pre_grad = cotangent_ref[...].astype(F32) * sigmoid * (1.0 + preact * (1.0 - sigmoid))
+    back_ref[...] = dot(pre_grad.astype(BF16), weight, 1, 1).astype(BF16)
 
 
 def layer_kernel(chips, slot_count, *refs):
@@ -393,7 +401,7 @@
             )
         nodes += hops
         rows_in = direct + [to_mate(value) for value in direct]
-        output, kept, *sends = pl.pallas_call(
+        aggregated, kept, *sends = pl.pallas_call(
             lambda *refs: plane_kernel(reps, chips, slot_count, *refs),
             out_shape=(
                 jax.ShapeDtypeStruct((rows, width), BF16),
@@ -411,7 +419,18 @@
             compiler_params=params(slots),
             name="plane",
         )(picked, wanted, weight, *rows_in, *nodes)
+        output, back_in = pl.pallas_call(
+            output_kernel,
+            out_shape=(jax.ShapeDtypeStruct((rows, width), BF16),) * 2,
+            in_specs=whole(3),
+            out_specs=tuple(whole(2)),
+            compiler_params=params(slots),
+            name="output",
+        )(aggregated, cotangent, weight)
+        kept, output, back_in = lax.optimization_barrier((kept, output, back_in))
+        backs = [back_in]
     else:
+        backs = []
         outgoing = partial((PAIR * PAD, width), chips)
         direct = [outgoing[0]] + [over_chips("B", outgoing[step], step) for step in range(1, chips)]
         shared = [to_mate(value) for value in direct]
@@ -472,11 +491,11 @@
     grad_x = pl.pallas_call(
         grad_x_kernel,
         out_shape=jax.ShapeDtypeStruct((rows, width), BF16),
-        in_specs=whole(reps),
+        in_specs=whole(reps + len(backs)),
         out_specs=whole(1)[0],
         compiler_params=params(slots),
         name="grad_x",
-    )(kept, *arrived)
+    )(kept, *backs, *arrived)
 
     node_count = rows * lax.axis_size("rows") * reps
     grad_w = pl.pallas_call(

time: 41.8 us -> 41.3 us (0.988)
  waiting for transfers between devices: 14.9 us -> 14.1 us
    pallas_call x0 -> x1, Pallas kernels: none -> 0.82 us  [local(): pl.pallas_call(output_kernel, out_shape=(jax.ShapeDtypeStruct((rows, widt...]
    ppermute x6, waiting for transfers between devices: 8.87 us -> 8.07 us  [over_rep(): lax.ppermute(value, 'rep', list(enumerate(targets(name, step, reps))))]
    pallas_call x1, Pallas kernels: 2.19 us -> 1.63 us  [local(): pl.pallas_call(lambda *refs: plane_kernel(reps, chips, slot_count, *refs)...]
  transfers between devices with their start and end apart: 21 -> 21, of which waited for: 11 -> 11; matrix products, arithmetic and copies ran while one was open for 0% -> 0% of each run, Pallas kernels for 4% -> 6%
where the time goes in v8:
time: 41.3 us; the launch traced here: 41.1 us
  starting transfers between devices  19.1 us (46%)
  waiting for transfers between devices  14.1 us (34%)
  Pallas kernels  5.1 us (12%)
  local copies, waits for them, and re-layouts  2.13 us (5%)
  between operations  0.74 us (2%)
    ppermute x6, starting transfers between devices, over_rep(): lax.ppermute(value, 'rep', list(enumerate(targets(name, step, reps))))  8.89 us
    ppermute x6, starting transfers between devices, over_chips(): return lax.ppermute(value, 'rows', pairs)  8.58 us
    ppermute x6, waiting for transfers between devices, over_rep(): lax.ppermute(value, 'rep', list(enumerate(targets(name, step, reps))))  8.07 us
    ppermute x6, waiting for transfers between devices, over_chips(): return lax.ppermute(value, 'rows', pairs)  4.42 us
    unnamed x13, local copies, waits for them, and re-layouts  2.13 us
    pallas_call x1, Pallas kernels, local(): pl.pallas_call(lambda *refs: plane_kernel(reps, chips, slot_count, *refs)...  1.63 us
    ppermute x9, starting transfers between devices, to_mate(): return lax.ppermute(value, 'rows', [(i, i ^ 1) for i in range(peers)])  1.6 us
    ppermute x9, waiting for transfers between devices, to_mate(): return lax.ppermute(value, 'rows', [(i, i ^ 1) for i in range(peers)])  1.6 us
  transfers between devices with their start and end apart: 21, of which 11 were waited for; matrix products, arithmetic and copies ran while one was open for 0% of the time, Pallas kernels for 6%

profile of v8, /device:TPU:0, one launch (start us, length us, event | category | flops | bytes accessed | tf_op | source)
XLA Modules:
  0.0 41.1 jit_solution(3958271040463084886)
XLA Ops:
  0.6 0.9 %constant_dynamic-update-slice_fusion.1 = bf16[256,256]{1,0:T(8,128)(2,1)S(1)} fusion(bf16[128,256]{1,0:T(8,128)(2,1)} %refs_2_.2), kind=kLoop, calls=%fused_computation.1 | loop fusion | bytes 131072
  1.6 3.0 %collective-permute-start.3 = (bf16[256,256]{1,0:T(8,128)(2,1)S(1)}, bf16[256,256]{1,0:T(8,128)(2,1)S(1)}, u32[]{:S(2)}, u32[]{:S(2)}) collective-permute-start(bf16[256,256]{1,0:T(8,128)(2,1)S(1)} %constant_dynamic-update-slice_fusion.refs_11_), channel_id=1, source_target_pairs={{0,8},{4,12},{8,0},{12,4},{16,24},{20,28},{24,16},{28,20},{1,9},{5... | collective-permute-start | bytes 393224 | tf_op jit(solution)/shard_map/ppermute | solution.py:353
  4.6 3.6 %collective-permute-start.1 = (bf16[128,256]{1,0:T(8,128)(2,1)S(1)}, bf16[128,256]{1,0:T(8,128)(2,1)S(1)}, u32[]{:S(2)}, u32[]{:S(2)}) collective-permute-start(bf16[128,256]{1,0:T(8,128)(2,1)S(1)} %copy-done.2), channel_id=1, source_target_pairs={{0,3},{1,2},{2,1},{3,0},{4,7},{5,6},{6,5},{7,4},{8,11},{9,10},{10,... | collective-permute-start | bytes 196616 | tf_op jit(solution)/shard_map/ppermute | solution.py:345
  8.2 0.8 %collective-permute-start.2 = (bf16[128,256]{1,0:T(8,128)(2,1)S(1)}, bf16[128,256]{1,0:T(8,128)(2,1)S(1)}, u32[]{:S(2)}, u32[]{:S(2)}) collective-permute-start(bf16[128,256]{1,0:T(8,128)(2,1)S(1)} %copy-done.2), channel_id=1, source_target_pairs={{0,2},{1,3},{2,0},{3,1},{4,6},{5,7},{6,4},{7,5},{8,10},{9,11},{10,... | collective-permute-start | bytes 196616 | tf_op jit(solution)/shard_map/ppermute | solution.py:345
  9.0 1.5 %collective-permute-start.5 = (bf16[256,256]{1,0:T(8,128)(2,1)S(1)}, bf16[256,256]{1,0:T(8,128)(2,1)S(1)}, u32[]{:S(2)}, u32[]{:S(2)}) collective-permute-start(bf16[256,256]{1,0:T(8,128)(2,1)S(1)} %constant_dynamic-update-slice_fusion.refs_11_), channel_id=1, source_target_pairs={{0,16},{4,20},{8,24},{12,28},{16,0},{20,4},{24,8},{28,12},{1,17},{... | collective-permute-start | bytes 393224 | tf_op jit(solution)/shard_map/ppermute | solution.py:353
  10.5 0.5 %collective-permute-start.4 = (bf16[256,256]{1,0:T(8,128)(2,1)S(1)}, bf16[256,256]{1,0:T(8,128)(2,1)S(1)}, u32[]{:S(2)}, u32[]{:S(2)}) collective-permute-start(bf16[256,256]{1,0:T(8,128)(2,1)S(1)} %collective-permute-done.3.refs_13_), channel_id=1, source_target_pairs={{0,16},{4,20},{8,24},{12,28},{16,0},{20,4},{24,8},{28,12},{1,17},{... | collective-permute-start | bytes 393224 | tf_op jit(solution)/shard_map/ppermute | solution.py:353
  11.0 1.2 %copy-done = bf16[1,1,4,8,128,128]{5,4,3,2,1,0:T(8,128)(2,1)S(1)} copy-done((bf16[1,1,4,8,128,128]{5,4,3,2,1,0:T(8,128)(2,1)S(1)}, bf16[1,1,4,8,128,128]{5,4,3,2,1,0:T(8,128)(2,1)}, u32[]{:S(2)}) %copy-start) | copy-done | bytes 1048600
  12.2 0.9 %inputs.1 = (bf16[4,256,128]{2,1,0:T(8,128)(2,1)S(1)}, f32[256,256]{1,0:T(8,128)S(1)}, bf16[256,128]{1,0:T(8,128)(2,1)S(1)}) custom-call(s32[8,24]{1,0:T(8,128)S(1)} %bitcast.4, s32[8,24]{1,0:T(8,128)S(1)} %bitcast.5, bf16[128,256]{1,0:T(8,128)(2,1)S(1)} %copy-done.2, bf16[4,8,128,128]{3,2,1,0:T(8,128)(2,1)S(1)} %bitcast.3), custom_call_target="tpu_custom_call" | custom-call | tf_op jit(solution)/shard_map/inputs/pallas_call | solution.py:360
  13.8 1.6 %collective-permute-start.10 = (bf16[256,256]{1,0:T(8,128)(2,1)S(1)}, bf16[256,256]{1,0:T(8,128)(2,1)S(1)}, u32[]{:S(2)}, u32[]{:S(2)}) collective-permute-start(bf16[256,256]{1,0:T(8,128)(2,1)S(1)} %partial.1.refs_3_), channel_id=1, source_target_pairs={{0,16},{4,20},{8,24},{12,28},{16,0},{20,4},{24,8},{28,12},{1,17},{... | collective-permute-start | bytes 393224 | tf_op jit(solution)/shard_map/ppermute | solution.py:353
  15.4 1.0 %collective-permute-start.9 = (bf16[256,256]{1,0:T(8,128)(2,1)S(1)}, bf16[256,256]{1,0:T(8,128)(2,1)S(1)}, u32[]{:S(2)}, u32[]{:S(2)}) collective-permute-start(bf16[256,256]{1,0:T(8,128)(2,1)S(1)} %partial.1.refs_3_), channel_id=1, source_target_pairs={{0,8},{4,12},{8,0},{12,4},{16,24},{20,28},{24,16},{28,20},{1,9},{5... | collective-permute-start | bytes 393224 | tf_op jit(solution)/shard_map/ppermute | solution.py:353
  16.4 1.0 %collective-permute-start.8 = (bf16[256,256]{1,0:T(8,128)(2,1)S(1)}, bf16[256,256]{1,0:T(8,128)(2,1)S(1)}, u32[]{:S(2)}, u32[]{:S(2)}) collective-permute-start(bf16[256,256]{1,0:T(8,128)(2,1)S(1)} %partial.1.refs_3_), channel_id=1, source_target_pairs={{0,24},{4,28},{8,16},{12,20},{16,8},{20,12},{24,0},{28,4},{1,25},{... | collective-permute-start | bytes 393224 | tf_op jit(solution)/shard_map/ppermute | solution.py:353
  17.4 0.5 %collective-permute-start.7 = (bf16[256,256]{1,0:T(8,128)(2,1)S(1)}, bf16[256,256]{1,0:T(8,128)(2,1)S(1)}, u32[]{:S(2)}, u32[]{:S(2)}) collective-permute-start(bf16[256,256]{1,0:T(8,128)(2,1)S(1)} %collective-permute-done.3.refs_13_), channel_id=1, source_target_pairs={{0,4},{4,0},{8,12},{12,8},{16,20},{20,16},{24,28},{28,24},{1,5},{5... | collective-permute-start | bytes 393224 | tf_op jit(solution)/shard_map/ppermute | solution.py:356
  17.9 2.4 %collective-permute-done.10.refs_6_ = bf16[256,256]{1,0:T(8,128)(2,1)S(1)} collective-permute-done((bf16[256,256]{1,0:T(8,128)(2,1)S(1)}, bf16[256,256]{1,0:T(8,128)(2,1)S(1)}, u32[]{:S(2)}, u32[]{:S(2)}) %collective-permute-start.10) | collective-permute-done | bytes 131104 | tf_op jit(solution)/shard_map/ppermute | solution.py:353
  20.2 0.7 %collective-permute-done.9.refs_5_ = bf16[256,256]{1,0:T(8,128)(2,1)S(1)} collective-permute-done((bf16[256,256]{1,0:T(8,128)(2,1)S(1)}, bf16[256,256]{1,0:T(8,128)(2,1)S(1)}, u32[]{:S(2)}, u32[]{:S(2)}) %collective-permute-start.9) | collective-permute-done | bytes 131104 | tf_op jit(solution)/shard_map/ppermute | solution.py:353
  20.9 1.4 %collective-permute-done.8.refs_4_ = bf16[256,256]{1,0:T(8,128)(2,1)S(1)} collective-permute-done((bf16[256,256]{1,0:T(8,128)(2,1)S(1)}, bf16[256,256]{1,0:T(8,128)(2,1)S(1)}, u32[]{:S(2)}, u32[]{:S(2)}) %collective-permute-start.8) | collective-permute-done | bytes 131104 | tf_op jit(solution)/shard_map/ppermute | solution.py:353
  22.3 0.5 %collective-permute-start.15 = (bf16[256,256]{1,0:T(8,128)(2,1)S(1)}, bf16[256,256]{1,0:T(8,128)(2,1)S(1)}, u32[]{:S(2)}, u32[]{:S(2)}) collective-permute-start(bf16[256,256]{1,0:T(8,128)(2,1)S(1)} %collective-permute-done.4.refs_12_), channel_id=1, source_target_pairs={{0,4},{4,0},{8,12},{12,8},{16,20},{20,16},{24,28},{28,24},{1,5},{5... | collective-permute-start | bytes 393224 | tf_op jit(solution)/shard_map/ppermute | solution.py:356
  24.3 1.6 %plane.1 = (bf16[128,256]{1,0:T(8,128)(2,1)S(1)}, f32[256,256]{1,0:T(8,128)S(1)}, bf16[256,256]{1,0:T(8,128)(2,1)S(1)}, bf16[256,256]{1,0:T(8,128)(2,1)S(1)}, bf16[256,256]{1,0:T(8,128)(2,1)S(1)}) custom-call(bf16[4,256,128]{2,1,0:T(8,128)(2,1)S(1)} %get-tuple-element.23.refs_0_, bf16[256,128]{1,0:T(8,128)(2,1)S(1)} %get-tuple-element.24.refs_1_, ...), custom_call_target="tpu_custom_call" | custom-call | tf_op jit(solution)/shard_map/plane/pallas_call | solution.py:404
  26.0 3.0 %collective-permute-start.17 = (bf16[256,256]{1,0:T(8,128)(2,1)S(1)}, bf16[256,256]{1,0:T(8,128)(2,1)S(1)}, u32[]{:S(2)}, u32[]{:S(2)}) collective-permute-start(bf16[256,256]{1,0:T(8,128)(2,1)S(1)} %get-tuple-element.39), channel_id=1, source_target_pairs={{0,3},{1,2},{2,0},{3,1},{4,7},{5,6},{6,4},{7,5},{8,11},{9,10},{10,... | collective-permute-start | bytes 393224 | tf_op jit(solution)/shard_map/ppermute | solution.py:345
  29.0 1.5 %collective-permute-start.19 = (bf16[256,256]{1,0:T(8,128)(2,1)S(1)}, bf16[256,256]{1,0:T(8,128)(2,1)S(1)}, u32[]{:S(2)}, u32[]{:S(2)}) collective-permute-start(bf16[256,256]{1,0:T(8,128)(2,1)S(1)} %get-tuple-element.41), channel_id=1, source_target_pairs={{0,1},{1,0},{2,3},{3,2},{4,5},{5,4},{6,7},{7,6},{8,9},{9,8},{10,11... | collective-permute-start | bytes 393224 | tf_op jit(solution)/shard_map/ppermute | solution.py:345
  30.5 0.8 %output.1 = (bf16[128,256]{1,0:T(8,128)(2,1)}, bf16[128,256]{1,0:T(8,128)(2,1)S(1)}) custom-call(bf16[128,256]{1,0:T(8,128)(2,1)S(1)} %get-tuple-element.34.aggregated_ref, bf16[128,256]{1,0:T(8,128)(2,1)S(1)} %copy-done.3, bf16[256,256]{1,0:T(8,128)(2,1)S(1)} %copy-done.1), custom_call_target="tpu_custom_call" | custom-call | tf_op jit(solution)/shard_map/output/pallas_call | solution.py:422
  31.3 7.6 %collective-permute-done.17.refs_1_ = bf16[256,256]{1,0:T(8,128)(2,1)S(1)} collective-permute-done((bf16[256,256]{1,0:T(8,128)(2,1)S(1)}, bf16[256,256]{1,0:T(8,128)(2,1)S(1)}, u32[]{:S(2)}, u32[]{:S(2)}) %collective-permute-start.17) | collective-permute-done | bytes 131104 | tf_op jit(solution)/shard_map/ppermute | solution.py:345
  39.2 0.7 %grad_x.1 = bf16[128,256]{1,0:T(8,128)(2,1)} custom-call(f32[256,256]{1,0:T(8,128)S(1)} %get-tuple-element.38.refs_0_.kept_ref, bf16[128,256]{1,0:T(8,128)(2,1)S(1)} %get-tuple-element.42.refs_0_, bf16[256,256]{1,0:T(8,128)(2,1)S(1)} %collective-permute-done.17.refs_1_, bf16[256,256]{1,0:T(8,128)(2,1)S(1)} %collective-permute-done.18.refs_2_, ...), custom_call_target="tpu_custom_call" | custom-call | tf_op jit(solution)/shard_map/grad_x/pallas_call | solution.py:491
  39.8 0.6 %collective-permute-done.20.refs_1_ = bf16[128,256]{1,0:T(8,128)(2,1)S(1)} collective-permute-done((bf16[128,256]{1,0:T(8,128)(2,1)S(1)}, bf16[128,256]{1,0:T(8,128)(2,1)S(1)}, u32[]{:S(2)}, u32[]{:S(2)}) %collective-permute-start.20) | collective-permute-done | bytes 65568 | tf_op jit(solution)/shard_map/ppermute | solution.py:356
  40.4 0.7 %grad_w.1 = f32[256,256]{1,0:T(8,128)} custom-call(bf16[128,256]{1,0:T(8,128)(2,1)S(1)} %chunk.1.refs_0_, bf16[128,256]{1,0:T(8,128)(2,1)S(1)} %collective-permute-done.20.refs_1_), custom_call_target="tpu_custom_call" | custom-call | tf_op jit(solution)/shard_map/grad_w/pallas_call | solution.py:501
  (39 shorter events, 2.5 us)
Async XLA Ops:
  1.5 9.5 %copy-start.5 = (s32[1,1,8,24]{3,2,1,0:T(8,128)S(1)}, s32[1,1,8,24]{3,2,1,0:T(8,128)}, u32[]{:S(2)}) copy-start(s32[1,1,8,24]{3,2,1,0:T(8,128)} %param.10) | copy-start | bytes 2308
  1.6 9.4 %copy-start.4 = (s32[1,1,8,24]{3,2,1,0:T(8,128)S(1)}, s32[1,1,8,24]{3,2,1,0:T(8,128)}, u32[]{:S(2)}) copy-start(s32[1,1,8,24]{3,2,1,0:T(8,128)} %param.9) | copy-start | bytes 2308
  1.6 8.9 %collective-permute-start.3 = (bf16[256,256]{1,0:T(8,128)(2,1)S(1)}, bf16[256,256]{1,0:T(8,128)(2,1)S(1)}, u32[]{:S(2)}, u32[]{:S(2)}) collective-permute-start(bf16[256,256]{1,0:T(8,128)(2,1)S(1)} %constant_dynamic-update-slice_fusion.refs_11_), channel_id=1, source_target_pairs={{0,8},{4,12},{8,0},{12,4},{16,24},{20,28},{24,16},{28,20},{1,9},{5... | collective-permute-start | bytes 393224 | tf_op jit(solution)/shard_map/ppermute | solution.py:353
  4.6 8.6 %collective-permute-start.1 = (bf16[128,256]{1,0:T(8,128)(2,1)S(1)}, bf16[128,256]{1,0:T(8,128)(2,1)S(1)}, u32[]{:S(2)}, u32[]{:S(2)}) collective-permute-start(bf16[128,256]{1,0:T(8,128)(2,1)S(1)} %copy-done.2), channel_id=1, source_target_pairs={{0,3},{1,2},{2,1},{3,0},{4,7},{5,6},{6,5},{7,4},{8,11},{9,10},{10,... | collective-permute-start | bytes 196616 | tf_op jit(solution)/shard_map/ppermute | solution.py:345
  8.2 5.0 %collective-permute-start = (bf16[128,256]{1,0:T(8,128)(2,1)S(1)}, bf16[128,256]{1,0:T(8,128)(2,1)S(1)}, u32[]{:S(2)}, u32[]{:S(2)}) collective-permute-start(bf16[128,256]{1,0:T(8,128)(2,1)S(1)} %copy-done.2), channel_id=1, source_target_pairs={{0,1},{1,0},{2,3},{3,2},{4,5},{5,4},{6,7},{7,6},{8,9},{9,8},{10,11... | collective-permute-start | bytes 196616 | tf_op jit(solution)/shard_map/ppermute | solution.py:345
  8.2 5.4 %collective-permute-start.2 = (bf16[128,256]{1,0:T(8,128)(2,1)S(1)}, bf16[128,256]{1,0:T(8,128)(2,1)S(1)}, u32[]{:S(2)}, u32[]{:S(2)}) collective-permute-start(bf16[128,256]{1,0:T(8,128)(2,1)S(1)} %copy-done.2), channel_id=1, source_target_pairs={{0,2},{1,3},{2,0},{3,1},{4,6},{5,7},{6,4},{7,5},{8,10},{9,11},{10,... | collective-permute-start | bytes 196616 | tf_op jit(solution)/shard_map/ppermute | solution.py:345
  9.0 8.4 %collective-permute-start.5 = (bf16[256,256]{1,0:T(8,128)(2,1)S(1)}, bf16[256,256]{1,0:T(8,128)(2,1)S(1)}, u32[]{:S(2)}, u32[]{:S(2)}) collective-permute-start(bf16[256,256]{1,0:T(8,128)(2,1)S(1)} %constant_dynamic-update-slice_fusion.refs_11_), channel_id=1, source_target_pairs={{0,16},{4,20},{8,24},{12,28},{16,0},{20,4},{24,8},{28,12},{1,17},{... | collective-permute-start | bytes 393224 | tf_op jit(solution)/shard_map/ppermute | solution.py:353
  10.5 6.9 %collective-permute-start.4 = (bf16[256,256]{1,0:T(8,128)(2,1)S(1)}, bf16[256,256]{1,0:T(8,128)(2,1)S(1)}, u32[]{:S(2)}, u32[]{:S(2)}) collective-permute-start(bf16[256,256]{1,0:T(8,128)(2,1)S(1)} %collective-permute-done.3.refs_13_), channel_id=1, source_target_pairs={{0,16},{4,20},{8,24},{12,28},{16,0},{20,4},{24,8},{28,12},{1,17},{... | collective-permute-start | bytes 393224 | tf_op jit(solution)/shard_map/ppermute | solution.py:353
  13.5 10.8 %copy-start.1 = (bf16[256,256]{1,0:T(8,128)(2,1)S(1)}, bf16[256,256]{1,0:T(8,128)(2,1)}, u32[]{:S(2)}) copy-start(bf16[256,256]{1,0:T(8,128)(2,1)} %weight_ref.1) | copy-start | bytes 393220
  13.8 6.4 %collective-permute-start.10 = (bf16[256,256]{1,0:T(8,128)(2,1)S(1)}, bf16[256,256]{1,0:T(8,128)(2,1)S(1)}, u32[]{:S(2)}, u32[]{:S(2)}) collective-permute-start(bf16[256,256]{1,0:T(8,128)(2,1)S(1)} %partial.1.refs_3_), channel_id=1, source_target_pairs={{0,16},{4,20},{8,24},{12,28},{16,0},{20,4},{24,8},{28,12},{1,17},{... | collective-permute-start | bytes 393224 | tf_op jit(solution)/shard_map/ppermute | solution.py:353
  15.4 5.5 %collective-permute-start.9 = (bf16[256,256]{1,0:T(8,128)(2,1)S(1)}, bf16[256,256]{1,0:T(8,128)(2,1)S(1)}, u32[]{:S(2)}, u32[]{:S(2)}) collective-permute-start(bf16[256,256]{1,0:T(8,128)(2,1)S(1)} %partial.1.refs_3_), channel_id=1, source_target_pairs={{0,8},{4,12},{8,0},{12,4},{16,24},{20,28},{24,16},{28,20},{1,9},{5... | collective-permute-start | bytes 393224 | tf_op jit(solution)/shard_map/ppermute | solution.py:353
  16.4 5.9 %collective-permute-start.8 = (bf16[256,256]{1,0:T(8,128)(2,1)S(1)}, bf16[256,256]{1,0:T(8,128)(2,1)S(1)}, u32[]{:S(2)}, u32[]{:S(2)}) collective-permute-start(bf16[256,256]{1,0:T(8,128)(2,1)S(1)} %partial.1.refs_3_), channel_id=1, source_target_pairs={{0,24},{4,28},{8,16},{12,20},{16,8},{20,12},{24,0},{28,4},{1,25},{... | collective-permute-start | bytes 393224 | tf_op jit(solution)/shard_map/ppermute | solution.py:353
  17.3 4.9 %collective-permute-start.6 = (bf16[256,256]{1,0:T(8,128)(2,1)S(1)}, bf16[256,256]{1,0:T(8,128)(2,1)S(1)}, u32[]{:S(2)}, u32[]{:S(2)}) collective-permute-start(bf16[256,256]{1,0:T(8,128)(2,1)S(1)} %constant_dynamic-update-slice_fusion.refs_11_), channel_id=1, source_target_pairs={{0,4},{4,0},{8,12},{12,8},{16,20},{20,16},{24,28},{28,24},{1,5},{5... | collective-permute-start | bytes 393224 | tf_op jit(solution)/shard_map/ppermute | solution.py:356
  17.4 5.4 %collective-permute-start.7 = (bf16[256,256]{1,0:T(8,128)(2,1)S(1)}, bf16[256,256]{1,0:T(8,128)(2,1)S(1)}, u32[]{:S(2)}, u32[]{:S(2)}) collective-permute-start(bf16[256,256]{1,0:T(8,128)(2,1)S(1)} %collective-permute-done.3.refs_13_), channel_id=1, source_target_pairs={{0,4},{4,0},{8,12},{12,8},{16,20},{20,16},{24,28},{28,24},{1,5},{5... | collective-permute-start | bytes 393224 | tf_op jit(solution)/shard_map/ppermute | solution.py:356
  20.2 2.6 %collective-permute-start.11 = (bf16[256,256]{1,0:T(8,128)(2,1)S(1)}, bf16[256,256]{1,0:T(8,128)(2,1)S(1)}, u32[]{:S(2)}, u32[]{:S(2)}) collective-permute-start(bf16[256,256]{1,0:T(8,128)(2,1)S(1)} %partial.1.refs_3_), channel_id=1, source_target_pairs={{0,4},{4,0},{8,12},{12,8},{16,20},{20,16},{24,28},{28,24},{1,5},{5... | collective-permute-start | bytes 393224 | tf_op jit(solution)/shard_map/ppermute | solution.py:356
  20.9 2.4 %collective-permute-start.14 = (bf16[256,256]{1,0:T(8,128)(2,1)S(1)}, bf16[256,256]{1,0:T(8,128)(2,1)S(1)}, u32[]{:S(2)}, u32[]{:S(2)}) collective-permute-start(bf16[256,256]{1,0:T(8,128)(2,1)S(1)} %collective-permute-done.10.refs_6_), channel_id=1, source_target_pairs={{0,4},{4,0},{8,12},{12,8},{16,20},{20,16},{24,28},{28,24},{1,5},{5... | collective-permute-start | bytes 393224 | tf_op jit(solution)/shard_map/ppermute | solution.py:356
  22.3 1.3 %collective-permute-start.13 = (bf16[256,256]{1,0:T(8,128)(2,1)S(1)}, bf16[256,256]{1,0:T(8,128)(2,1)S(1)}, u32[]{:S(2)}, u32[]{:S(2)}) collective-permute-start(bf16[256,256]{1,0:T(8,128)(2,1)S(1)} %collective-permute-done.9.refs_5_), channel_id=1, source_target_pairs={{0,4},{4,0},{8,12},{12,8},{16,20},{20,16},{24,28},{28,24},{1,5},{5... | collective-permute-start | bytes 393224 | tf_op jit(solution)/shard_map/ppermute | solution.py:356
  22.3 1.5 %collective-permute-start.15 = (bf16[256,256]{1,0:T(8,128)(2,1)S(1)}, bf16[256,256]{1,0:T(8,128)(2,1)S(1)}, u32[]{:S(2)}, u32[]{:S(2)}) collective-permute-start(bf16[256,256]{1,0:T(8,128)(2,1)S(1)} %collective-permute-done.4.refs_12_), channel_id=1, source_target_pairs={{0,4},{4,0},{8,12},{12,8},{16,20},{20,16},{24,28},{28,24},{1,5},{5... | collective-permute-start | bytes 393224 | tf_op jit(solution)/shard_map/ppermute | solution.py:356
  22.8 1.3 %collective-permute-start.16 = (bf16[256,256]{1,0:T(8,128)(2,1)S(1)}, bf16[256,256]{1,0:T(8,128)(2,1)S(1)}, u32[]{:S(2)}, u32[]{:S(2)}) collective-permute-start(bf16[256,256]{1,0:T(8,128)(2,1)S(1)} %collective-permute-done.5.refs_14_), channel_id=1, source_target_pairs={{0,4},{4,0},{8,12},{12,8},{16,20},{20,16},{24,28},{28,24},{1,5},{5... | collective-permute-start | bytes 393224 | tf_op jit(solution)/shard_map/ppermute | solution.py:356
  22.9 1.5 %collective-permute-start.12 = (bf16[256,256]{1,0:T(8,128)(2,1)S(1)}, bf16[256,256]{1,0:T(8,128)(2,1)S(1)}, u32[]{:S(2)}, u32[]{:S(2)}) collective-permute-start(bf16[256,256]{1,0:T(8,128)(2,1)S(1)} %collective-permute-done.8.refs_4_), channel_id=1, source_target_pairs={{0,4},{4,0},{8,12},{12,8},{16,20},{20,16},{24,28},{28,24},{1,5},{5... | collective-permute-start | bytes 393224 | tf_op jit(solution)/shard_map/ppermute | solution.py:356
  26.0 12.9 %collective-permute-start.17 = (bf16[256,256]{1,0:T(8,128)(2,1)S(1)}, bf16[256,256]{1,0:T(8,128)(2,1)S(1)}, u32[]{:S(2)}, u32[]{:S(2)}) collective-permute-start(bf16[256,256]{1,0:T(8,128)(2,1)S(1)} %get-tuple-element.39), channel_id=1, source_target_pairs={{0,3},{1,2},{2,0},{3,1},{4,7},{5,6},{6,4},{7,5},{8,11},{9,10},{10,... | collective-permute-start | bytes 393224 | tf_op jit(solution)/shard_map/ppermute | solution.py:345
  29.0 9.9 %collective-permute-start.18 = (bf16[256,256]{1,0:T(8,128)(2,1)S(1)}, bf16[256,256]{1,0:T(8,128)(2,1)S(1)}, u32[]{:S(2)}, u32[]{:S(2)}) collective-permute-start(bf16[256,256]{1,0:T(8,128)(2,1)S(1)} %get-tuple-element.40), channel_id=1, source_target_pairs={{0,2},{1,3},{2,1},{3,0},{4,6},{5,7},{6,5},{7,4},{8,10},{9,11},{10,... | collective-permute-start | bytes 393224 | tf_op jit(solution)/shard_map/ppermute | solution.py:345
  29.0 10.0 %collective-permute-start.19 = (bf16[256,256]{1,0:T(8,128)(2,1)S(1)}, bf16[256,256]{1,0:T(8,128)(2,1)S(1)}, u32[]{:S(2)}, u32[]{:S(2)}) collective-permute-start(bf16[256,256]{1,0:T(8,128)(2,1)S(1)} %get-tuple-element.41), channel_id=1, source_target_pairs={{0,1},{1,0},{2,3},{3,2},{4,5},{5,4},{6,7},{7,6},{8,9},{9,8},{10,11... | collective-permute-start | bytes 393224 | tf_op jit(solution)/shard_map/ppermute | solution.py:345
  39.1 1.3 %collective-permute-start.20 = (bf16[128,256]{1,0:T(8,128)(2,1)S(1)}, bf16[128,256]{1,0:T(8,128)(2,1)S(1)}, u32[]{:S(2)}, u32[]{:S(2)}) collective-permute-start(bf16[128,256]{1,0:T(8,128)(2,1)S(1)} %chunk.1.refs_0_), channel_id=1, source_target_pairs={{0,4},{4,0},{8,12},{12,8},{16,20},{20,16},{24,28},{28,24},{1,5},{5... | collective-permute-start | bytes 196616 | tf_op jit(solution)/shard_map/ppermute | solution.py:356
  (3 other events, 5.2 us)
